TPU v7x, 32 devices: a whole 2x2x4 slice. The times are simulated.
32 devices in a mesh: dp: 4 (over z), expert: 2 (over y), tensor: 4 (over x, core).
Axes of the slice: x: 2, y: 2, z: 4, core: 2. Of those that a mesh axis runs over, the one named last changes fastest.
Arguments:
- tokens: bfloat16 [128, 2048], P(('dp', 'expert', 'tensor')), may hold values from -6 to 6
- routes: int32 [128, 6], P(('dp', 'expert')), may hold values from 0 to 15, as said below
- positions: int32 [128, 6], P(('dp', 'expert')), may hold values from 0 to 7, as said below
- combine_weights: float32 [128, 6], P(('dp', 'expert')), may hold values from 0.1 to 1
- cotangent: bfloat16 [128, 2048], P(('dp', 'expert', 'tensor')), may hold values from -6 to 6
- gate_weight: bfloat16 [16, 2048, 1408], P('expert', None, 'tensor'), may hold values from -0.125 to 0.125
- up_weight: bfloat16 [16, 2048, 1408], P('expert', None, 'tensor'), may hold values from -0.125 to 0.125
- down_weight: bfloat16 [16, 2048, 1408], P('expert', None, 'tensor'), may hold values from -0.15625 to 0.15625
Outputs:
- layer_out: bfloat16 [128, 2048], P(('dp', 'expert', 'tensor'))
- grad_tokens: bfloat16 [128, 2048], P(('dp', 'expert', 'tensor'))
- grad_down: bfloat16 [16, 2048, 1408], P('expert', 'dp', 'tensor')
Inputs may be any that keep to these rules, and one draw needn't show every extreme that they name: `routes`: each row names 6 different experts. Within each aligned block of 16 rows, no expert is named by more than 8 rows, and one expert, the same in every block, is named by exactly 8 rows. `positions`: within each aligned block of 16 rows, no two choices share both expert and position.
All inputs are finite; a program needn't handle non-finite values.
Results may differ from a plain program's by a relative error of at most 0.017.
Values may be sent and summed in bfloat16 or wider, within the bound.
No kernel may reach another device: no remote copies, remote signals or barrier semaphores. Data moves between devices by JAX's collectives and lax.ppermute only.
A program may use at most 128 MiB of HBM per device.

v0:
```python
import jax
import jax.numpy as jnp
from jax import lax
from jax.sharding import PartitionSpec as P


def by_replica(left, right, replicas):
    left_view = left.reshape(left.shape[0], replicas, -1, left.shape[2])
    right_view = right.reshape(right.shape[0], replicas, -1, right.shape[2])
    terms = jnp.einsum("eprd,eprf->epdf", left_view, right_view, preferred_element_type=jnp.float32)
    rounded = lax.optimization_barrier(terms.astype(jnp.bfloat16))
    return jnp.sum(rounded.astype(jnp.float32), axis=1)


def shards(
    tokens, routes, positions, combine_weights, cotangent, gate_weight, up_weight, down_weight
):
    experts_here = gate_weight.shape[0]
    experts_all = experts_here * lax.axis_size("expert")
    replicas = lax.axis_size("dp")
    group_size = routes.shape[0]
    capacity = group_size // 2
    slot_count = experts_all * capacity
    slot_ids = routes * capacity + positions
    slot_range = jnp.arange(slot_count, dtype=jnp.int32)
    matches = slot_ids[:, :, None] == slot_range
    chooser = matches.astype(jnp.bfloat16)
    scatter_table = jnp.any(slot_range[:, None, None] == slot_ids[None, :, :], axis=2).astype(
        jnp.bfloat16
    )
    slot_gain = jnp.sum(jnp.where(matches, combine_weights[:, :, None], 0.0), axis=(0, 1))

    def fill_slots(rows_block, gain):
        picked = jnp.dot(scatter_table, rows_block, preferred_element_type=jnp.float32)
        if gain is not None:
            picked = picked * gain[:, None]
        return picked.astype(jnp.bfloat16).reshape(experts_all, capacity, rows_block.shape[1])

    def dispatch(rows, gain):
        gathered = lax.all_gather(rows, "tensor", axis=0, tiled=True)
        return lax.all_to_all(
            fill_slots(gathered, gain), "expert", split_axis=0, concat_axis=1, tiled=True
        )

    def gather_back(partial_slots, weights):
        returned = lax.all_to_all(partial_slots, "expert", split_axis=1, concat_axis=0, tiled=True)
        flattened = returned.reshape(slot_count, returned.shape[2])
        picked = jnp.einsum("tks,sd->tkd", chooser, flattened, preferred_element_type=jnp.float32)
        if weights is not None:
            picked = picked * weights[:, :, None]
        summed = jnp.sum(picked, axis=1)
        return lax.psum_scatter(
            summed.astype(jnp.bfloat16), "tensor", scatter_dimension=0, tiled=True
        ).astype(jnp.float32)

    expert_rows = dispatch(tokens, None)
    gate_pre = jnp.einsum(
        "erd,edf->erf", expert_rows, gate_weight, preferred_element_type=jnp.float32
    )
    up_pre = jnp.einsum("erd,edf->erf", expert_rows, up_weight, preferred_element_type=jnp.float32)
    squash = jax.nn.sigmoid(gate_pre)
    swish = gate_pre * squash
    activation = (swish * up_pre).astype(jnp.bfloat16)
    expert_part = jnp.einsum(
        "erf,edf->erd", activation, down_weight, preferred_element_type=jnp.float32
    ).astype(jnp.bfloat16)
    layer_out = gather_back(expert_part, combine_weights).astype(jnp.bfloat16)
    slot_grads = dispatch(cotangent, slot_gain)
    act_grad = jnp.einsum(
        "erd,edf->erf", slot_grads, down_weight, preferred_element_type=jnp.float32
    )
    gate_back = (act_grad * up_pre * squash * (1.0 + gate_pre * (1.0 - squash))).astype(
        jnp.bfloat16
    )
    up_back = (act_grad * swish).astype(jnp.bfloat16)
    input_gate = jnp.einsum(
        "erf,edf->erd", gate_back, gate_weight, preferred_element_type=jnp.float32
    )
    input_up = jnp.einsum("erf,edf->erd", up_back, up_weight, preferred_element_type=jnp.float32)
    input_part = (input_gate + input_up).astype(jnp.bfloat16)
    grad_tokens = gather_back(input_part, None).astype(jnp.bfloat16)
    cotangent_cols = lax.all_to_all(slot_grads, "dp", split_axis=2, concat_axis=1, tiled=True)
    act_rows = lax.all_gather(activation, "dp", axis=1, tiled=True)
    total = by_replica(cotangent_cols, act_rows, replicas)
    grad_down = (total * (1.0 / replicas)).astype(jnp.bfloat16)
    return (layer_out, grad_tokens, grad_down)


def solution(mesh):
    return jax.shard_map(
        shards,
        mesh=mesh,
        in_specs=(
            P(("dp", "expert", "tensor"), None),
            P(("dp", "expert"), None),
            P(("dp", "expert"), None),
            P(("dp", "expert"), None),
            P(("dp", "expert", "tensor"), None),
            P("expert", None, "tensor"),
            P("expert", None, "tensor"),
            P("expert", None, "tensor"),
        ),
        out_specs=(
            P(("dp", "expert", "tensor"), None),
            P(("dp", "expert", "tensor"), None),
            P("expert", "dp", "tensor"),
        ),
        check_vma=False,
    )
```

profile of v0, /device:TPU:0, one launch (start us, length us, event | category | flops | bytes accessed | tf_op | source)
XLA Modules:
  0.0 169.0 jit_solution(10669823107584005764)
XLA Ops:
  8.8 6.4 %all-gather.1 = bf16[4,4,2048]{2,1,0:T(4,128)(2,1)S(1)} all-gather(bf16[1,4,2048]{2,1,0:T(4,128)(2,1)} %bitcast.71), channel_id=1, replica_groups=mesh['dp'=4,'expert'=2,'tensor'=4] {'tensor'}, dimensions={0}, use_global_device_ids=true | all-gather | bytes 81920 | tf_op jit(solution)/shard_map/all_gather | solution.py:40
  16.3 3.5 %all-to-all-start.2 = ((bf16[16,8,2048]{2,1,0:T(8,128)(2,1)}), bf16[16,8,2048]{2,1,0:T(8,128)(2,1)S(1)}, u32[]{:S(2)}, u32[]{:S(2)}) async-start(bf16[16,8,2048]{2,1,0:T(8,128)(2,1)} %fusion.2), calls=%async_computation.2 | async-start | bytes 1048576 | tf_op jit(solution)/shard_map/all_to_all | solution.py:41
  19.8 5.7 %all-gather = bf16[4,4,2048]{2,1,0:T(4,128)(2,1)S(1)} all-gather(bf16[1,4,2048]{2,1,0:T(4,128)(2,1)} %bitcast.72), channel_id=1, replica_groups=mesh['dp'=4,'expert'=2,'tensor'=4] {'tensor'}, dimensions={0}, use_global_device_ids=true | all-gather | bytes 81920 | tf_op jit(solution)/shard_map/all_gather | solution.py:40
  26.7 2.1 %all-to-all-done.2 = bf16[16,8,2048]{2,1,0:T(8,128)(2,1)S(1)} async-done(((bf16[16,8,2048]{2,1,0:T(8,128)(2,1)}), bf16[16,8,2048]{2,1,0:T(8,128)(2,1)S(1)}, u32[]{:S(2)}, u32[]{:S(2)}) %all-to-all-start.2) | async-done | bytes 524320 | tf_op jit(solution)/shard_map/all_to_all | solution.py:41
  28.8 3.5 %all-to-all-start = ((bf16[16,8,2048]{2,1,0:T(8,128)(2,1)}), bf16[16,8,2048]{2,1,0:T(8,128)(2,1)S(1)}, u32[]{:S(2)}, u32[]{:S(2)}) async-start(bf16[16,8,2048]{2,1,0:T(8,128)(2,1)} %fusion.3), calls=%async_computation | async-start | bytes 1048576 | tf_op jit(solution)/shard_map/all_to_all | solution.py:41
  32.3 7.4 %fusion.21 = f32[8,16,352]{2,1,0:T(8,128)S(1)} fusion(bf16[8,2048,352]{1,2,0:T(8,128)(2,1)} %param.15, bf16[2,8,8,2048]{3,2,1,0:T(8,128)(2,1)S(1)} %bitcast.63), kind=kOutput, calls=%fused_computation.40 | convolution fusion | flops 184549376 | bytes 12238848 | tf_op jit(solution)/shard_map/erd,edf->erf/dot_general | solution.py:69
  40.6 7.5 %fusion.8 = f32[8,16,352]{2,1,0:T(8,128)S(1)} fusion(bf16[8,2048,352]{1,2,0:T(8,128)(2,1)} %param.13, bf16[2,8,8,2048]{3,2,1,0:T(8,128)(2,1)S(1)} %bitcast.61), kind=kOutput, calls=%fused_computation.17 | convolution fusion | flops 184549376 | bytes 12238848 | tf_op jit(solution)/shard_map/erd,edf->erf/dot_general | solution.py:57
  48.1 7.5 %multiply_convert_fusion.3 = (bf16[8,16,352]{2,1,0:T(8,128)(2,1)S(1)}, f32[8,16,352]{2,1,0:T(8,128)S(1)}) fusion(f32[8,16,352]{2,1,0:T(8,128)S(1)} %fusion.8, bf16[8,2048,352]{1,2,0:T(8,128)(2,1)} %param.14, bf16[2,8,8,2048]{3,2,1,0:T(8,128)(2,1)S(1)} %bitcast.62), kind=kOutput, calls=%fused_computation.24 | convolution fusion | flops 184819712 | bytes 12509184 | tf_op jit(solution)/shard_map/erd,edf->erf/dot_general | solution.py:60
  55.6 1.7 %convolution_convert_fusion.1 = bf16[8,16,2048]{2,1,0:T(8,128)(2,1)S(1)} fusion(bf16[8,16,352]{2,1,0:T(8,128)(2,1)S(1)} %get-tuple-element.5, bf16[8,2048,352]{1,2,0:T(8,128)(2,1)S(1)} %bitcast.58), kind=kOutput, calls=%fused_computation.6 | convolution fusion | flops 184811520 | bytes 12148736 | tf_op jit(solution)/shard_map/erf,edf->erd/dot_general | solution.py:64
  58.4 3.7 %all-to-all-start.1 = ((bf16[8,16,2048]{2,0,1:T(8,128)(2,1)}), bf16[8,16,2048]{2,0,1:T(8,128)(2,1)S(1)}, u32[]{:S(2)}, u32[]{:S(2)}) async-start(bf16[8,16,2048]{2,0,1:T(8,128)(2,1)} %copy.36), calls=%async_computation.1 | async-start | bytes 1048576 | tf_op jit(solution)/shard_map/all_to_all | solution.py:46
  62.1 6.0 %fusion.13 = f32[8,16,2048]{2,1,0:T(8,128)S(1)} fusion(bf16[8,2048,352]{1,2,0:T(8,128)(2,1)} %param.13, f32[8,16,352]{2,1,0:T(8,128)S(1)} %fusion.8, f32[8,16,352]{2,1,0:T(8,128)S(1)} %fusion.21, f32[8,16,352]{2,1,0:T(8,128)S(1)} %get-tuple-element.6), kind=kOutput, calls=%fused_computation.27 | convolution fusion | flops 184999936 | bytes 13123584 | tf_op jit(solution)/shard_map/erf,edf->erd/dot_general | solution.py:76
  68.1 6.0 %fusion = bf16[8,16,2048]{2,1,0:T(8,128)(2,1)S(1)} fusion(f32[8,16,2048]{2,1,0:T(8,128)S(1)} %fusion.13, bf16[8,2048,352]{1,2,0:T(8,128)(2,1)} %param.14, f32[8,16,352]{2,1,0:T(8,128)S(1)} %fusion.21, f32[8,16,352]{2,1,0:T(8,128)S(1)} %fusion.8), kind=kOutput, calls=%fused_computation.5 | convolution fusion | flops 185344000 | bytes 13467648 | tf_op jit(solution)/shard_map/erf,edf->erd/dot_general | solution.py:79
  75.3 3.5 %all-to-all-start.3 = ((bf16[8,16,2048]{2,0,1:T(8,128)(2,1)}), bf16[8,16,2048]{2,0,1:T(8,128)(2,1)S(1)}, u32[]{:S(2)}, u32[]{:S(2)}) async-start(bf16[8,16,2048]{2,0,1:T(8,128)(2,1)} %copy.39), calls=%async_computation.3 | async-start | bytes 1048576 | tf_op jit(solution)/shard_map/all_to_all | solution.py:46
  78.8 4.2 %copy.41 = bf16[8,16,2048]{1,0,2:T(8,128)(2,1)} copy(bf16[8,16,2048]{2,1,0:T(8,128)(2,1)S(1)} %bitcast.65) | data formatting | bytes 1048576 | tf_op jit(solution)/shard_map/all_to_all | solution.py:41
  83.0 6.5 %reshape.42 = bf16[4,2,32768]{2,1,0:T(2,128)(2,1)} reshape(bf16[2048,8,16]{2,1,0:T(8,128)(2,1)} %bitcast.59) | data formatting | bytes 1048576
  89.5 4.8 %all-to-all-start.4 = ((bf16[4,2,32768]{2,1,0:T(2,128)(2,1)}), bf16[4,2,32768]{2,1,0:T(2,128)(2,1)S(1)}, u32[]{:S(2)}, u32[]{:S(2)}) async-start(bf16[4,2,32768]{2,1,0:T(2,128)(2,1)} %reshape.42), calls=%async_computation.4 | async-start | bytes 1048576 | tf_op jit(solution)/shard_map/all_to_all | solution.py:82
  98.1 18.7 %all_gather.11 = bf16[8,64,352]{2,1,0:T(8,128)(2,1)S(1)} all-gather(bf16[8,16,352]{2,1,0:T(8,128)(2,1)S(1)} %get-tuple-element.5), channel_id=1, replica_groups=mesh['dp'=4,'expert'=2,'tensor'=4] {'dp'}, dimensions={1}, use_global_device_ids=true | all-gather | bytes 450560 | tf_op jit(solution)/shard_map/all_gather | solution.py:83
  116.8 14.9 %all-reduce.5.cloned.1.call-done = (bf16[16,2048]{1,0:T(8,128)(2,1)}, bf16[16,2048]{1,0:T(8,128)(2,1)}) async-done(((bf16[16,2048]{1,0:T(8,128)(2,1)}, bf16[16,2048]{1,0:T(8,128)(2,1)}), (bf16[16,2048]{1,0:T(8,128)(2,1)}, bf16[16,2048]{1,0:T(8,128)(2,1)})) %all-reduce.5.cloned.1.call-update) | async-done | bytes 131088
  131.7 1.4 constant_dynamic-slice_fusion
  133.1 4.1 %reshape.43 = bf16[2048,8,16]{2,1,0:T(8,128)(2,1)} reshape(bf16[4,2,32768]{2,1,0:T(2,128)(2,1)S(1)} %all-to-all-done.4) | data formatting | bytes 1048576
  137.2 4.4 %copy.43 = bf16[8,16,4,512]{3,1,2,0:T(8,128)(2,1)S(1)} copy(bf16[8,16,4,512]{1,0,3,2:T(8,128)(2,1)} %bitcast.60) | data formatting | bytes 1048576 | tf_op jit(solution)/shard_map/all_to_all | solution.py:82
  141.6 6.1 %convolution_convert_fusion = bf16[8,4,512,352]{2,3,1,0:T(8,128)(2,1)} fusion(bf16[8,4,16,352]{3,2,1,0:T(8,128)(2,1)S(1)} %bitcast.69, bf16[8,16,4,512]{3,1,2,0:T(8,128)(2,1)S(1)} %copy.43), kind=kOutput, calls=%fused_computation.1 | convolution fusion | flops 190316544 | bytes 12419072 | tf_op jit(solution)/shard_map/eprd,eprf->epdf/dot_general | solution.py:10
  147.7 9.5 %convert_reduce_fusion = f32[8,512,352]{1,2,0:T(8,128)} fusion(bf16[8,4,512,352]{2,3,1,0:T(8,128)(2,1)} %convolution_convert_fusion), kind=kLoop, calls=%fused_computation | loop fusion | flops 10092544 | bytes 17301504 | tf_op jit(solution)/shard_map/reduce_sum | solution.py:12
  157.2 5.0 %multiply_convert_fusion = bf16[8,512,352]{1,2,0:T(8,128)(2,1)} fusion(f32[8,512,352]{1,2,0:T(8,128)} %convert_reduce_fusion), kind=kLoop, calls=%fused_computation.2 | loop fusion | flops 2883584 | bytes 8650752 | tf_op jit(solution)/shard_map/convert_element_type | solution.py:85
  (32 shorter events, 10.2 us)
Async XLA Ops:
  16.3 12.5 %all-to-all-start.2 = ((bf16[16,8,2048]{2,1,0:T(8,128)(2,1)}), bf16[16,8,2048]{2,1,0:T(8,128)(2,1)S(1)}, u32[]{:S(2)}, u32[]{:S(2)}) async-start(bf16[16,8,2048]{2,1,0:T(8,128)(2,1)} %fusion.2), calls=%async_computation.2 | async-start | bytes 1048576 | tf_op jit(solution)/shard_map/all_to_all | solution.py:41
  28.8 11.7 %all-to-all-start = ((bf16[16,8,2048]{2,1,0:T(8,128)(2,1)}), bf16[16,8,2048]{2,1,0:T(8,128)(2,1)S(1)}, u32[]{:S(2)}, u32[]{:S(2)}) async-start(bf16[16,8,2048]{2,1,0:T(8,128)(2,1)} %fusion.3), calls=%async_computation | async-start | bytes 1048576 | tf_op jit(solution)/shard_map/all_to_all | solution.py:41
  40.5 15.1 %slice-start = ((s8[11534336]{0:T(1024)(128)(4,1)}), s8[4194304]{0:T(1024)(128)(4,1)S(1)}, s32[]{:S(2)}) async-start(s8[11534336]{0:T(1024)(128)(4,1)} %bitcast.57), calls=%async_computation.6 | async-start | bytes 8388608
  40.6 15.1 %slice-start.1 = ((s8[11534336]{0:T(1024)(128)(4,1)}), s8[4194304]{0:T(1024)(128)(4,1)S(1)}, s32[]{:S(2)}) async-start(s8[11534336]{0:T(1024)(128)(4,1)} %bitcast.57), calls=%async_computation.7 | async-start | bytes 8388608
  48.1 7.6 %slice-start.2 = ((s8[11534336]{0:T(1024)(128)(4,1)}), s8[3145728]{0:T(1024)(128)(4,1)S(1)}, s32[]{:S(2)}) async-start(s8[11534336]{0:T(1024)(128)(4,1)} %bitcast.57), calls=%async_computation.8 | async-start | bytes 6291456
  58.4 16.8 %all-to-all-start.1 = ((bf16[8,16,2048]{2,0,1:T(8,128)(2,1)}), bf16[8,16,2048]{2,0,1:T(8,128)(2,1)S(1)}, u32[]{:S(2)}, u32[]{:S(2)}) async-start(bf16[8,16,2048]{2,0,1:T(8,128)(2,1)} %copy.36), calls=%async_computation.1 | async-start | bytes 1048576 | tf_op jit(solution)/shard_map/all_to_all | solution.py:46
  68.1 26.2 %copy-start.1 = (u32[32]{0:T(128)S(1)}, u32[32]{0:T(128)}, u32[]{:S(2)}) copy-start(u32[32]{0:T(128)} %constant.14) | copy-start | bytes 388
  74.2 23.0 %copy-start = (f32[16,6]{0,1:T(8,128)S(1)}, f32[16,6]{0,1:T(8,128)}, u32[]{:S(2)}) copy-start(f32[16,6]{0,1:T(8,128)} %param.11) | copy-start | bytes 1156
  75.3 14.2 %all-to-all-start.3 = ((bf16[8,16,2048]{2,0,1:T(8,128)(2,1)}), bf16[8,16,2048]{2,0,1:T(8,128)(2,1)S(1)}, u32[]{:S(2)}, u32[]{:S(2)}) async-start(bf16[8,16,2048]{2,0,1:T(8,128)(2,1)} %copy.39), calls=%async_computation.3 | async-start | bytes 1048576 | tf_op jit(solution)/shard_map/all_to_all | solution.py:46
  89.5 43.6 %all-to-all-start.4 = ((bf16[4,2,32768]{2,1,0:T(2,128)(2,1)}), bf16[4,2,32768]{2,1,0:T(2,128)(2,1)S(1)}, u32[]{:S(2)}, u32[]{:S(2)}) async-start(bf16[4,2,32768]{2,1,0:T(2,128)(2,1)} %reshape.42), calls=%async_computation.4 | async-start | bytes 1048576 | tf_op jit(solution)/shard_map/all_to_all | solution.py:82
  94.3 37.4 %all-reduce.5.cloned.1.call-start = ((), (), s32[]{:S(2)}) async-start(), calls=%async_computation.5 | async-start | bytes 262144
Sparse Core Ops, SparseCore 0:
  98.2 33.4 all-reduce.4
where the time goes:
time: 170 us; the launch traced here: 169 us
  matrix products  46.4 us (27%)
  blocking collectives  30.9 us (18%)
  local copies, waits for them, and re-layouts  24.1 us (14%)
  starting transfers between devices  19 us (11%)
  waiting for transfers between devices  17.9 us (11%)
  other arithmetic  16.1 us (9%)
  between operations  14.8 us (9%)
    all_gather x1, blocking collectives, shards(): act_rows = lax.all_gather(activation, 'dp', axis=1, tiled=True)  18.7 us
    unnamed x2, waiting for transfers between devices  14.9 us
    unnamed x16, local copies, waits for them, and re-layouts  12.6 us
    all_gather x2, blocking collectives, dispatch(): gathered = lax.all_gather(rows, 'tensor', axis=0, tiled=True)  12.1 us
    reduce_sum x1, other arithmetic, by_replica(): return jnp.sum(rounded.astype(jnp.float32), axis=1)  9.47 us
    dot_general x1, matrix products, shards(): jnp.einsum('erd,edf->erf', expert_rows, up_weight, preferred_element_type...  7.53 us
    dot_general x1, matrix products, shards(): jnp.einsum('erd,edf->erf', expert_rows, gate_weight, preferred_element_ty...  7.51 us
    dot_general x1, matrix products, shards(): jnp.einsum('erd,edf->erf', slot_grads, down_weight, preferred_element_typ...  7.36 us
  transfers between devices with their start and end apart: 6, of which 3 were waited for; matrix products, arithmetic and copies ran while one was open for 22% of the time, Pallas kernels for 0%

commit v1 on v0

v1 whole, which is shorter than its diff:
```python
import functools

import jax
import jax.numpy as jnp
from jax import lax
from jax.experimental import pallas as pl
from jax.experimental.pallas import tpu as pltpu
from jax.sharding import PartitionSpec as P

F32 = jnp.float32
BF16 = jnp.bfloat16
LANES = 128
NT = (((1,), (1,)), ((), ()))
TN = (((0,), (0,)), ((), ()))


def whole_part(values, divisor):
    return jnp.floor((values + 0.5) * (1.0 / divisor))


def fiota(shape, axis):
    return lax.broadcasted_iota(jnp.int32, shape, axis).astype(F32)


def slot_tables(routing, top, first_expert, capacity, groups, slots):
    rows = routing.shape[0]
    lane = fiota((rows, slots), 1)
    token = fiota((rows, slots), 0)
    expert = whole_part(lane, groups * capacity)
    inner = lane - expert * (groups * capacity)
    group = whole_part(inner, capacity)
    target = (expert + first_expert) * capacity + inner - group * capacity
    target = jnp.where(whole_part(token, rows // groups) == group, target, -1.0)
    names = routing[:, :top] * float(capacity) + routing[:, top : 2 * top]
    weights = routing[:, 2 * top : 3 * top] + routing[:, 3 * top : 4 * top]
    chosen = jnp.zeros((rows, slots), F32)
    gains = jnp.zeros((rows, slots), F32)
    for k in range(top):
        match = names[:, k : k + 1] == target
        chosen = chosen + jnp.where(match, 1.0, 0.0)
        gains = gains + jnp.where(match, weights[:, k : k + 1], 0.0)
    return chosen, gains


def column_blocks(width):
    return [(at, min(LANES, width - at)) for at in range(0, width, LANES)]


def experts_kernel(
    sizes, x_ref, gate_hbm, up_hbm, down_hbm, keep_ref, send_ref, *rest
):
    top, capacity, groups, tensor, replicas = sizes
    packs = rest[:replicas]
    gate_w, up_w, down_w, filled, results, act, sems = rest[replicas:]
    experts, hidden, width = gate_hbm.shape
    rows = x_ref.shape[0]
    slots = filled.shape[0]
    per_expert = slots // experts
    ahead = min(3, experts)

    def fetch(e):
        return [
            pltpu.make_async_copy(source.at[e], target.at[e], sems.at[e, i])
            for i, (source, target) in enumerate(
                ((gate_hbm, gate_w), (up_hbm, up_w), (down_hbm, down_w))
            )
        ]

    for e in range(ahead):
        for copy in fetch(e):
            copy.start()

    first_expert = (lax.axis_index("expert") * experts).astype(F32)
    routing = x_ref[:, 2 * width :].astype(F32)
    chosen, gains = slot_tables(routing, top, first_expert, capacity, groups, slots)
    chooser = chosen.astype(BF16)
    scatter = chosen.T.astype(BF16)
    gain = jnp.sum(gains.T, axis=1, keepdims=True)
    step = min(512, width)
    for at in range(0, width, step):
        filled[:, at : at + step] = jnp.dot(
            scatter, x_ref[:, at : at + step], preferred_element_type=F32
        ).astype(BF16)
    for at in range(width, 2 * width, step):
        filled[:, at : at + step] = (
            gain * jnp.dot(scatter, x_ref[:, at : at + step], preferred_element_type=F32)
        ).astype(BF16)

    def one_expert(e, _):
        for copy in fetch(e):
            copy.wait()

        @pl.when(e + ahead < experts)
        def _():
            for copy in fetch(e + ahead):
                copy.start()

        here = pl.ds(pl.multiple_of(e * per_expert, per_expert), per_expert)
        slot_rows = filled[here, :width]
        slot_grads = filled[here, width:]
        gate_pre = lax.dot_general(slot_rows, gate_w[e], NT, preferred_element_type=F32)
        up_pre = lax.dot_general(slot_rows, up_w[e], NT, preferred_element_type=F32)
        act_grad = lax.dot_general(slot_grads, down_w[e], NT, preferred_element_type=F32)
        squash = 1.0 / (1.0 + jnp.exp(-gate_pre))
        swish = gate_pre * squash
        activation = (swish * up_pre).astype(BF16)
        act[here, :] = activation
        gate_back = (act_grad * up_pre * squash * (1.0 + gate_pre * (1.0 - squash))).astype(BF16)
        up_back = (act_grad * swish).astype(BF16)
        results[here, :width] = jnp.dot(
            activation, down_w[e], preferred_element_type=F32
        ).astype(BF16)
        results[here, width:] = (
            jnp.dot(gate_back, gate_w[e], preferred_element_type=F32)
            + jnp.dot(up_back, up_w[e], preferred_element_type=F32)
        ).astype(BF16)
        return 0

    lax.fori_loop(0, experts, one_expert, 0)

    device = lax.axis_index("expert") * tensor + lax.axis_index("tensor")
    pair = lax.div(device, 2)
    parity = device - pair * 2
    per_device = rows // (groups * tensor)
    half = rows // 2
    row = lax.broadcasted_iota(jnp.int32, (rows, 1), 0)
    second = jnp.where(row >= half, 1, 0)
    within = row - second * half
    block = lax.div(within, jnp.full_like(within, per_device))
    token = (
        (block ^ pair) * (2 * per_device)
        + (second ^ parity) * per_device
        + within
        - block * per_device
    )
    order = jnp.where(lax.broadcasted_iota(jnp.int32, (rows, rows), 1) == token, 1.0, 0.0)
    picker = jnp.dot(order.astype(BF16), chooser, preferred_element_type=F32).astype(BF16)
    for at in range(0, 2 * width, step):
        piece = results[:, at : at + step]
        if at < width:
            piece = (piece.astype(F32) * gain).astype(BF16)
        total = jnp.dot(picker, piece, preferred_element_type=F32)
        keep_ref[:, at : at + step] = total[:half].astype(BF16)
        send_ref[:, at : at + step] = total[half:].astype(BF16)

    replica = lax.axis_index("dp")
    share = width // replicas
    for k in range(replicas):
        peer = replica ^ k
        at = 0
        for lane, size in column_blocks(hidden):
            packs[k][at : at + slots, :size] = act[:, lane : lane + size]
            if size < LANES:
                packs[k][at : at + slots, size:] = jnp.zeros((slots, LANES - size), BF16)
            at += slots
        for lane in range(0, share, LANES):
            column = pl.multiple_of(width + peer * share + lane, LANES)
            packs[k][at : at + rows, :] = x_ref[:, pl.ds(column, LANES)]
            at += rows
        packs[k][at : at + rows, :] = x_ref[:, 2 * width :]


def grad_kernel(sizes, *refs):
    top, capacity, groups, experts, hidden, rows, replicas = sizes
    packs = refs[:replicas]
    out_ref, grads, acts = refs[replicas:]
    slots = experts * groups * capacity
    per_expert = groups * capacity
    share = out_ref.shape[2]

    @pl.when(pl.program_id(0) == 0)
    def _():
        first_expert = (lax.axis_index("expert") * experts).astype(F32)
        for k in range(replicas):
            pack = packs[k]
            at = len(column_blocks(hidden)) * slots
            routing = pack[at + (share // LANES) * rows :, :].astype(F32)
            chosen, gains = slot_tables(routing, top, first_expert, capacity, groups, slots)
            scatter = chosen.T.astype(BF16)
            gain = jnp.sum(gains.T, axis=1, keepdims=True)
            for lane in range(0, share, LANES):
                grads[k, :, lane : lane + LANES] = (
                    gain * jnp.dot(scatter, pack[at : at + rows, :], preferred_element_type=F32)
                ).astype(BF16)
                at += rows
            at = 0
            for lane, size in column_blocks(hidden):
                acts[k, :, lane : lane + LANES] = pack[at : at + slots, :]
                at += slots

    e = pl.program_id(0)
    here = pl.ds(pl.multiple_of(e * per_expert, per_expert), per_expert)
    left = jnp.concatenate([acts[k, here, :] for k in range(replicas)], axis=0)
    right = jnp.concatenate([grads[k, here, :] for k in range(replicas)], axis=0)
    total = lax.dot_general(left, right, TN, preferred_element_type=F32)
    out_ref[0] = (total[:hidden] * (1.0 / replicas)).astype(BF16)


def vmem_specs(count):
    return [pl.BlockSpec(memory_space=pltpu.VMEM)] * count


def shards(
    tokens, routes, positions, combine_weights, cotangent, gate_weight, up_weight, down_weight
):
    experts, width, hidden = gate_weight.shape
    replicas = lax.axis_size("dp")
    groups = lax.axis_size("expert")
    tensor = lax.axis_size("tensor")
    group_size, top = routes.shape
    capacity = group_size // 2
    slots = experts * groups * capacity
    mine = tokens.shape[0]
    devices = groups * tensor
    rows = mine * devices
    both = ("expert", "tensor")

    first = lax.axis_index("tensor") * mine
    high = lax.reduce_precision(combine_weights, 8, 7)
    routing = jnp.concatenate(
        [routes.astype(F32), positions.astype(F32), high, combine_weights - high], axis=1
    ).astype(BF16)
    routing = lax.dynamic_slice_in_dim(routing, first, mine, axis=0)
    routing = jnp.pad(routing, ((0, 0), (0, LANES - 4 * top)))
    sent = jnp.concatenate([tokens, cotangent, routing], axis=1)
    gathered = lax.all_gather(sent, both, axis=0, tiled=True)

    pack_rows = len(column_blocks(hidden)) * slots + (width // replicas // LANES + 1) * rows
    weights = [jnp.swapaxes(w, 1, 2) for w in (gate_weight, up_weight, down_weight)]
    half = jax.ShapeDtypeStruct((rows // 2, 2 * width), BF16)
    pack = jax.ShapeDtypeStruct((pack_rows, LANES), BF16)
    outs = pl.pallas_call(
        functools.partial(experts_kernel, (top, capacity, groups, tensor, replicas)),
        out_shape=[half, half] + [pack] * replicas,
        in_specs=vmem_specs(1) + [pl.BlockSpec(memory_space=pl.ANY)] * 3,
        out_specs=vmem_specs(2 + replicas),
        scratch_shapes=[pltpu.VMEM((experts, hidden, width), BF16)] * 3
        + [
            pltpu.VMEM((slots, 2 * width), BF16),
            pltpu.VMEM((slots, 2 * width), BF16),
            pltpu.VMEM((slots, hidden), BF16),
            pltpu.SemaphoreType.DMA((experts, 3)),
        ],
        compiler_params=pltpu.CompilerParams(vmem_limit_bytes=48 * 2**20),
        cost_estimate=pl.CostEstimate(
            flops=12 * slots * hidden * width,
            bytes_accessed=6 * experts * hidden * width,
            transcendentals=slots * hidden,
        ),
        name="experts",
    )(gathered, *weights)
    keep, send, packs = outs[0], outs[1], outs[2:]

    def swap(values, distance):
        return lax.ppermute(values, both, [(i, i ^ distance) for i in range(devices)])

    near = keep.astype(F32) + swap(send, 1).astype(F32)
    near = near.reshape(devices // 2, mine, 2 * width)
    total = near[0]
    for k in range(1, devices // 2):
        total = total + swap(near[k].astype(BF16), 2 * k).astype(F32)
    total = total.astype(BF16)

    arrived = [packs[0]]
    for k in range(1, replicas):
        arrived.append(lax.ppermute(packs[k], "dp", [(i, i ^ k) for i in range(replicas)]))
    share = width // replicas
    grad = pl.pallas_call(
        functools.partial(
            grad_kernel, (top, capacity, groups, experts, hidden, rows, replicas)
        ),
        grid=(experts,),
        out_shape=jax.ShapeDtypeStruct((experts, hidden, share), BF16),
        in_specs=vmem_specs(replicas),
        out_specs=pl.BlockSpec((1, hidden, share), lambda e: (e, 0, 0)),
        scratch_shapes=[
            pltpu.VMEM((replicas, slots, share), BF16),
            pltpu.VMEM((replicas, slots, len(column_blocks(hidden)) * LANES), BF16),
        ],
        compiler_params=pltpu.CompilerParams(vmem_limit_bytes=24 * 2**20),
        cost_estimate=pl.CostEstimate(
            flops=2 * replicas * slots * share * hidden,
            bytes_accessed=2 * experts * share * hidden,
            transcendentals=0,
        ),
        name="grad_down",
    )(*arrived)
    return (total[:, :width], total[:, width:], jnp.swapaxes(grad, 1, 2))


def solution(mesh):
    return jax.shard_map(
        shards,
        mesh=mesh,
        in_specs=(
            P(("dp", "expert", "tensor"), None),
            P(("dp", "expert"), None),
            P(("dp", "expert"), None),
            P(("dp", "expert"), None),
            P(("dp", "expert", "tensor"), None),
            P("expert", None, "tensor"),
            P("expert", None, "tensor"),
            P("expert", None, "tensor"),
        ),
        out_specs=(
            P(("dp", "expert", "tensor"), None),
            P(("dp", "expert", "tensor"), None),
            P("expert", "dp", "tensor"),
        ),
        check_vma=False,
    )
```

time: 170 us -> 54.2 us (0.32)
  matrix products: 46.4 us -> 0 us
  Pallas kernels: 0 us -> 23.8 us
  local copies, waits for them, and re-layouts: 24.1 us -> 0.83 us
  blocking collectives: 30.9 us -> 10.8 us
  between operations: 14.8 us -> 0.68 us
  other arithmetic: 16.1 us -> 2.32 us
  waiting for transfers between devices: 17.9 us -> 6.03 us
  starting transfers between devices: 19 us -> 9.29 us
    dot_general x11 -> x0, matrix products: 46.4 us -> none  [the longest x1 7.53 us: shards(): jnp.einsum('erd,edf->erf', expert_rows, up_weight, preferred_element_type...]
    pallas_call x0 -> x2, Pallas kernels: none -> 23.8 us  [the longest x1 18 us: shards(): pl.pallas_call(functools.partial(experts_kernel, (top, capacity, groups,...]
    all_gather x3 -> x1, blocking collectives: 30.9 us -> 10.8 us  [shards(): gathered = lax.all_gather(sent, both, axis=0, tiled=True)]
    all_to_all x5 -> x0, starting transfers between devices: 19 us -> none  [the longest x2 7.16 us: gather_back(): lax.all_to_all(partial_slots, 'expert', split_axis=1, concat_axis=0, tile...]
    unnamed x2 -> x0, waiting for transfers between devices: 14.9 us -> none
    unnamed x16 -> x2, local copies, waits for them, and re-layouts: 12.6 us -> 0.16 us
    reduce_sum x2 -> x0, other arithmetic: 10.3 us -> none  [the longest x1 9.47 us: by_replica(): return jnp.sum(rounded.astype(jnp.float32), axis=1)]
    ppermute x0 -> x7, starting transfers between devices: none -> 9.29 us  [the longest x4 4.91 us: swap(): lax.ppermute(values, both, [(i, i ^ distance) for i in range(devices)])]
  transfers between devices with their start and end apart: 6 -> 7, of which waited for: 3 -> 2; matrix products, arithmetic and copies ran while one was open for 22% -> 0% of each run, Pallas kernels for 0% -> 11%
where the time goes in v1:
time: 54.2 us; the launch traced here: 53.8 us
  Pallas kernels  23.8 us (44%)
  blocking collectives  10.8 us (20%)
  starting transfers between devices  9.29 us (17%)
  waiting for transfers between devices  6.03 us (11%)
  other arithmetic  2.32 us (4%)
  local copies, waits for them, and re-layouts  0.83 us (2%)
  between operations  0.68 us (1%)
    pallas_call x1, Pallas kernels, shards(): pl.pallas_call(functools.partial(experts_kernel, (top, capacity, groups,...  18 us
    all_gather x1, blocking collectives, shards(): gathered = lax.all_gather(sent, both, axis=0, tiled=True)  10.8 us
    ppermute x3, waiting for transfers between devices, shards(): lax.ppermute(packs[k], 'dp', [(i, i ^ k) for i in range(replicas)])  6.02 us
    pallas_call x1, Pallas kernels, shards(): pl.pallas_call(functools.partial(grad_kernel, (top, capacity, groups, exp...  5.84 us
    ppermute x4, starting transfers between devices, swap(): lax.ppermute(values, both, [(i, i ^ distance) for i in range(devices)])  4.91 us
    ppermute x3, starting transfers between devices, shards(): lax.ppermute(packs[k], 'dp', [(i, i ^ k) for i in range(replicas)])  4.39 us
    another operation x3, other arithmetic  1.44 us
  transfers between devices with their start and end apart: 7, of which 2 were waited for; matrix products, arithmetic and copies ran while one was open for 0% of the time, Pallas kernels for 11%

profile of v1, /device:TPU:0, one launch (start us, length us, event | category | flops | bytes accessed | tf_op | source)
XLA Modules:
  0.0 53.8 jit_solution(6610666880801896047)
XLA Ops:
  0.6 0.7 %reduce-precision_convert_fusion = (bf16[16,6]{0,1:T(8,128)(2,1)S(1)}, bf16[16,6]{0,1:T(8,128)(2,1)S(1)}) fusion(f32[16,6]{0,1:T(8,128)} %param.11), kind=kLoop, calls=%fused_computation.13 | loop fusion | flops 384 | bytes 768 | tf_op jit(solution)/shard_map/convert.5
  1.3 0.7 %convert_convert_fusion = (bf16[16,6]{0,1:T(8,128)(2,1)S(1)}, bf16[16,6]{0,1:T(8,128)(2,1)S(1)}) fusion(s32[16,6]{0,1:T(8,128)} %param.10, s32[16,6]{0,1:T(8,128)} %param.9), kind=kLoop, calls=%fused_computation.15 | loop fusion | flops 384 | bytes 1152 | tf_op jit(solution)/shard_map/convert.4
  2.0 0.1 dynamic-slice_maximum_fusion
  2.1 0.1 copy.20
  2.2 0.8 %fusion.5 = bf16[1,4,4224]{2,1,0:T(4,128)(2,1)S(1)} fusion(bf16[4,24]{1,0:T(4,128)(2,1)S(1)} %copy.20, bf16[4,2048]{1,0:T(4,128)(2,1)} %param.12, bf16[4,2048]{1,0:T(4,128)(2,1)} %param.8), kind=kLoop, calls=%fused_computation.8 | loop fusion | flops 135168 | bytes 66752
  3.0 10.8 %all-gather = bf16[8,4,4224]{2,1,0:T(4,128)(2,1)S(1)} all-gather(bf16[1,4,4224]{2,1,0:T(4,128)(2,1)S(1)} %fusion.5), channel_id=1, replica_groups=mesh['dp'=4,'expert'=2,'tensor'=4] {'expert','tensor'}, dimensions={0}, use_global_device_ids=true | all-gather | bytes 304128 | tf_op jit(solution)/shard_map/all_gather | solution.py:226
  13.8 0.1 reshape.16.x_ref
  13.8 18.0 %experts.1 = (bf16[16,4096]{1,0:T(8,128)(2,1)S(1)}, bf16[16,4096]{1,0:T(8,128)(2,1)S(1)}, bf16[544,128]{1,0:T(8,128)(2,1)S(1)}, bf16[544,128]{1,0:T(8,128)(2,1)S...) custom-call(bf16[32,4224]{1,0:T(8,128)(2,1)S(1)} %reshape.16.x_ref, bf16[8,352,2048]{2,1,0:T(8,128)(2,1)} %bitcast.6, ...), custom_call_target="tpu_custom_call" | custom-call | flops 1107296256 | bytes 34603008 | tf_op jit(solution)/shard_map/experts/pallas_call | solution.py:232
  31.8 0.4 collective-permute-start
  32.2 1.6 %collective-permute-start.4 = (bf16[544,128]{1,0:T(8,128)(2,1)S(1)}, bf16[544,128]{1,0:T(8,128)(2,1)S(1)}, u32[]{:S(2)}, u32[]{:S(2)}) collective-permute-start(bf16[544,128]{1,0:T(8,128)(2,1)S(1)} %get-tuple-element.12), channel_id=1, source_target_pairs={{0,8},{8,0},{16,24},{24,16},{1,9},{9,1},{17,25},{25,17},{2,10},{10... | collective-permute-start | bytes 417800 | tf_op jit(solution)/shard_map/ppermute | solution.py:266
  33.8 2.6 %collective-permute-start.5 = (bf16[544,128]{1,0:T(8,128)(2,1)S(1)}, bf16[544,128]{1,0:T(8,128)(2,1)S(1)}, u32[]{:S(2)}, u32[]{:S(2)}) collective-permute-start(bf16[544,128]{1,0:T(8,128)(2,1)S(1)} %get-tuple-element.13), channel_id=1, source_target_pairs={{0,16},{8,24},{16,0},{24,8},{1,17},{9,25},{17,1},{25,9},{2,18},{10... | collective-permute-start | bytes 417800 | tf_op jit(solution)/shard_map/ppermute | solution.py:266
  36.4 0.2 collective-permute-start.6
  36.6 0.0 collective-permute-done
  36.7 1.6 %collective-permute-start.1 = (bf16[4,4096]{1,0:T(4,128)(2,1)S(1)}, bf16[4,4096]{1,0:T(4,128)(2,1)S(1)}, u32[]{:S(2)}, u32[]{:S(2)}) collective-permute-start(bf16[4,4096]{1,0:T(4,128)(2,1)S(1)} %get-tuple-element.17), channel_id=1, source_target_pairs={{0,2},{1,3},{2,0},{3,1},{4,6},{5,7},{6,4},{7,5},{8,10},{9,11},{10,... | collective-permute-start | bytes 98312 | tf_op jit(solution)/shard_map/ppermute | solution.py:255
  38.3 1.5 %collective-permute-start.3 = (bf16[4,4096]{1,0:T(4,128)(2,1)S(1)}, bf16[4,4096]{1,0:T(4,128)(2,1)S(1)}, u32[]{:S(2)}, u32[]{:S(2)}) collective-permute-start(bf16[4,4096]{1,0:T(4,128)(2,1)S(1)} %get-tuple-element.18), channel_id=1, source_target_pairs={{0,6},{1,7},{2,4},{3,5},{4,2},{5,3},{6,0},{7,1},{8,14},{9,15},{10,... | collective-permute-start | bytes 98312 | tf_op jit(solution)/shard_map/ppermute | solution.py:255
  39.7 0.4 collective-permute-done.4.refs_1_
  40.2 1.5 %collective-permute-start.2 = (bf16[4,4096]{1,0:T(4,128)(2,1)S(1)}, bf16[4,4096]{1,0:T(4,128)(2,1)S(1)}, u32[]{:S(2)}, u32[]{:S(2)}) collective-permute-start(bf16[4,4096]{1,0:T(4,128)(2,1)S(1)} %get-tuple-element.19), channel_id=1, source_target_pairs={{0,4},{1,5},{2,6},{3,7},{4,0},{5,1},{6,2},{7,3},{8,12},{9,13},{10,... | collective-permute-start | bytes 98312 | tf_op jit(solution)/shard_map/ppermute | solution.py:255
  41.7 5.6 %collective-permute-done.5.refs_2_ = bf16[544,128]{1,0:T(8,128)(2,1)S(1)} collective-permute-done((bf16[544,128]{1,0:T(8,128)(2,1)S(1)}, bf16[544,128]{1,0:T(8,128)(2,1)S(1)}, u32[]{:S(2)}, u32[]{:S(2)}) %collective-permute-start.5) | collective-permute-done | bytes 139296 | tf_op jit(solution)/shard_map/ppermute | solution.py:266
  47.2 0.0 collective-permute-done.6.refs_3_
  47.2 5.8 %grad_down.1 = bf16[8,352,512]{2,1,0:T(8,128)(2,1)} custom-call(bf16[544,128]{1,0:T(8,128)(2,1)S(1)} %get-tuple-element.11.refs_0_, bf16[544,128]{1,0:T(8,128)(2,1)S(1)} %collective-permute-done.4.refs_1_, bf16[544,128]{1,0:T(8,128)(2,1)S(1)} %collective-permute-done.5.refs_2_, bf16[544,128]{1,0:T(8,128)(2,1)S(1)} %collective-permute-done.6.refs_3_), custom_call_target="tpu_custom_call" | custom-call | flops 184549376 | bytes 2883584 | tf_op jit(solution)/shard_map/grad_down/pallas_call | solution.py:268
  53.1 0.0 collective-permute-done.1
  53.1 0.0 collective-permute-done.3
  53.1 0.0 collective-permute-done.2
  53.1 0.6 %fusion.9 = (bf16[4,2048]{1,0:T(4,128)(2,1)}, bf16[4,2048]{1,0:T(4,128)(2,1)}) fusion(bf16[4,4096]{1,0:T(4,128)(2,1)S(1)} %fusion.3), kind=kLoop, calls=%fused_computation.19 | loop fusion | bytes 65536 | tf_op jit(solution)/shard_map/slice | solution.py:288
  (3 shorter events, 0.1 us)
Async XLA Ops:
  31.8 4.8 %collective-permute-start = (bf16[16,4096]{1,0:T(8,128)(2,1)S(1)}, bf16[16,4096]{1,0:T(8,128)(2,1)S(1)}, u32[]{:S(2)}, u32[]{:S(2)}) collective-permute-start(bf16[16,4096]{1,0:T(8,128)(2,1)S(1)} %get-tuple-element.10), channel_id=1, source_target_pairs={{0,1},{1,0},{2,3},{3,2},{4,5},{5,4},{6,7},{7,6},{8,9},{9,8},{10,11... | collective-permute-start | bytes 393224 | tf_op jit(solution)/shard_map/ppermute | solution.py:255
  32.2 7.9 %collective-permute-start.4 = (bf16[544,128]{1,0:T(8,128)(2,1)S(1)}, bf16[544,128]{1,0:T(8,128)(2,1)S(1)}, u32[]{:S(2)}, u32[]{:S(2)}) collective-permute-start(bf16[544,128]{1,0:T(8,128)(2,1)S(1)} %get-tuple-element.12), channel_id=1, source_target_pairs={{0,8},{8,0},{16,24},{24,16},{1,9},{9,1},{17,25},{25,17},{2,10},{10... | collective-permute-start | bytes 417800 | tf_op jit(solution)/shard_map/ppermute | solution.py:266
  33.8 13.4 %collective-permute-start.5 = (bf16[544,128]{1,0:T(8,128)(2,1)S(1)}, bf16[544,128]{1,0:T(8,128)(2,1)S(1)}, u32[]{:S(2)}, u32[]{:S(2)}) collective-permute-start(bf16[544,128]{1,0:T(8,128)(2,1)S(1)} %get-tuple-element.13), channel_id=1, source_target_pairs={{0,16},{8,24},{16,0},{24,8},{1,17},{9,25},{17,1},{25,9},{2,18},{10... | collective-permute-start | bytes 417800 | tf_op jit(solution)/shard_map/ppermute | solution.py:266
  36.4 10.8 %collective-permute-start.6 = (bf16[544,128]{1,0:T(8,128)(2,1)S(1)}, bf16[544,128]{1,0:T(8,128)(2,1)S(1)}, u32[]{:S(2)}, u32[]{:S(2)}) collective-permute-start(bf16[544,128]{1,0:T(8,128)(2,1)S(1)} %get-tuple-element.14), channel_id=1, source_target_pairs={{0,24},{8,16},{16,8},{24,0},{1,25},{9,17},{17,9},{25,1},{2,26},{10... | collective-permute-start | bytes 417800 | tf_op jit(solution)/shard_map/ppermute | solution.py:266
  36.7 16.4 %collective-permute-start.1 = (bf16[4,4096]{1,0:T(4,128)(2,1)S(1)}, bf16[4,4096]{1,0:T(4,128)(2,1)S(1)}, u32[]{:S(2)}, u32[]{:S(2)}) collective-permute-start(bf16[4,4096]{1,0:T(4,128)(2,1)S(1)} %get-tuple-element.17), channel_id=1, source_target_pairs={{0,2},{1,3},{2,0},{3,1},{4,6},{5,7},{6,4},{7,5},{8,10},{9,11},{10,... | collective-permute-start | bytes 98312 | tf_op jit(solution)/shard_map/ppermute | solution.py:255
  38.3 14.8 %collective-permute-start.3 = (bf16[4,4096]{1,0:T(4,128)(2,1)S(1)}, bf16[4,4096]{1,0:T(4,128)(2,1)S(1)}, u32[]{:S(2)}, u32[]{:S(2)}) collective-permute-start(bf16[4,4096]{1,0:T(4,128)(2,1)S(1)} %get-tuple-element.18), channel_id=1, source_target_pairs={{0,6},{1,7},{2,4},{3,5},{4,2},{5,3},{6,0},{7,1},{8,14},{9,15},{10,... | collective-permute-start | bytes 98312 | tf_op jit(solution)/shard_map/ppermute | solution.py:255
  40.2 12.9 %collective-permute-start.2 = (bf16[4,4096]{1,0:T(4,128)(2,1)S(1)}, bf16[4,4096]{1,0:T(4,128)(2,1)S(1)}, u32[]{:S(2)}, u32[]{:S(2)}) collective-permute-start(bf16[4,4096]{1,0:T(4,128)(2,1)S(1)} %get-tuple-element.19), channel_id=1, source_target_pairs={{0,4},{1,5},{2,6},{3,7},{4,0},{5,1},{6,2},{7,3},{8,12},{9,13},{10,... | collective-permute-start | bytes 98312 | tf_op jit(solution)/shard_map/ppermute | solution.py:255

commit v2 on v1

v2 whole, which is shorter than its diff:
```python
import functools

import jax
import jax.numpy as jnp
from jax import lax
from jax.experimental import pallas as pl
from jax.experimental.pallas import tpu as pltpu
from jax.sharding import PartitionSpec as P

F32 = jnp.float32
BF16 = jnp.bfloat16
LANES = 128
NT = (((1,), (1,)), ((), ()))
TN = (((0,), (0,)), ((), ()))


def whole_part(values, divisor):
    return jnp.floor((values + 0.5) * (1.0 / divisor))


def fiota(shape, axis):
    return lax.broadcasted_iota(jnp.int32, shape, axis).astype(F32)


def slot_tables(routing, top, first_expert, capacity, groups, slots):
    rows = routing.shape[0]
    lane = fiota((rows, slots), 1)
    token = fiota((rows, slots), 0)
    expert = whole_part(lane, groups * capacity)
    inner = lane - expert * (groups * capacity)
    group = whole_part(inner, capacity)
    target = (expert + first_expert) * capacity + inner - group * capacity
    target = jnp.where(whole_part(token, rows // groups) == group, target, -1.0)
    names = routing[:, :top] * float(capacity) + routing[:, top : 2 * top]
    weights = routing[:, 2 * top : 3 * top] + routing[:, 3 * top : 4 * top]
    chosen = jnp.zeros((rows, slots), F32)
    gains = jnp.zeros((rows, slots), F32)
    for k in range(top):
        match = names[:, k : k + 1] == target
        chosen = chosen + jnp.where(match, 1.0, 0.0)
        gains = gains + jnp.where(match, weights[:, k : k + 1], 0.0)
    return chosen, gains


def column_blocks(width):
    return [(at, min(LANES, width - at)) for at in range(0, width, LANES)]


def pack_kernel(tokens_ref, cotangent_ref, routes_ref, positions_ref, weights_ref, out_ref):
    mine, width = tokens_ref.shape
    top, group_size = routes_ref.shape
    weights = weights_ref[...]
    high = weights.astype(BF16)
    low = (weights - high.astype(F32)).astype(BF16)
    table = jnp.concatenate(
        [routes_ref[...].astype(F32), positions_ref[...].astype(F32), high.astype(F32), low.astype(F32)],
        axis=0,
    ).astype(BF16)
    first = lax.axis_index("tensor") * mine
    column = lax.broadcasted_iota(jnp.int32, (mine, group_size), 1)
    row = lax.broadcasted_iota(jnp.int32, (mine, group_size), 0)
    pick = jnp.where(column == row + first, 1.0, 0.0).astype(BF16)
    routing = lax.dot_general(pick, table, NT, preferred_element_type=F32)
    out_ref[:, :width] = tokens_ref[...]
    out_ref[:, width : 2 * width] = cotangent_ref[...]
    out_ref[:, 2 * width :] = jnp.concatenate(
        [routing, jnp.zeros((mine, LANES - 4 * top), F32)], axis=1
    ).astype(BF16)


def activations_kernel(
    sizes, x_ref, gate_hbm, up_hbm, down_hbm, gate_w, up_w, down_w, backs, picker_ref, gain_ref, *rest
):
    top, capacity, groups, tensor, replicas = sizes
    packs = rest[:replicas]
    filled, sems = rest[replicas:]
    experts, hidden, width = gate_hbm.shape
    rows = x_ref.shape[0]
    slots = filled.shape[0]
    per_expert = slots // experts
    ahead = min(3, experts)

    def fetch(e):
        return [
            pltpu.make_async_copy(source.at[e], target.at[e], sems.at[e, i])
            for i, (source, target) in enumerate(
                ((gate_hbm, gate_w), (up_hbm, up_w), (down_hbm, down_w))
            )
        ]

    for e in range(ahead):
        for copy in fetch(e):
            copy.start()

    first_expert = (lax.axis_index("expert") * experts).astype(F32)
    routing = x_ref[:, 2 * width :].astype(F32)
    chosen, gains = slot_tables(routing, top, first_expert, capacity, groups, slots)
    scatter = chosen.T.astype(BF16)
    gain = jnp.sum(gains.T, axis=1, keepdims=True)
    gain_ref[...] = gain
    step = min(512, width)
    for at in range(0, width, step):
        filled[:, at : at + step] = jnp.dot(
            scatter, x_ref[:, at : at + step], preferred_element_type=F32
        ).astype(BF16)
    for at in range(width, 2 * width, step):
        filled[:, at : at + step] = (
            gain * jnp.dot(scatter, x_ref[:, at : at + step], preferred_element_type=F32)
        ).astype(BF16)

    device = lax.axis_index("expert") * tensor + lax.axis_index("tensor")
    pair = lax.div(device, 2)
    parity = device - pair * 2
    per_device = rows // (groups * tensor)
    half = rows // 2
    row = lax.broadcasted_iota(jnp.int32, (rows, 1), 0)
    second = jnp.where(row >= half, 1, 0)
    within = row - second * half
    block = lax.div(within, jnp.full_like(within, per_device))
    token = (
        (block ^ pair) * (2 * per_device)
        + (second ^ parity) * per_device
        + within
        - block * per_device
    )
    order = jnp.where(lax.broadcasted_iota(jnp.int32, (rows, rows), 1) == token, 1.0, 0.0)
    picker_ref[...] = jnp.dot(
        order.astype(BF16), chosen.astype(BF16), preferred_element_type=F32
    ).astype(BF16)

    def one_expert(e, _):
        for copy in fetch(e):
            copy.wait()

        @pl.when(e + ahead < experts)
        def _():
            for copy in fetch(e + ahead):
                copy.start()

        here = pl.ds(pl.multiple_of(e * per_expert, per_expert), per_expert)
        slot_rows = filled[here, :width]
        slot_grads = filled[here, width:]
        gate_pre = lax.dot_general(slot_rows, gate_w[e], NT, preferred_element_type=F32)
        up_pre = lax.dot_general(slot_rows, up_w[e], NT, preferred_element_type=F32)
        act_grad = lax.dot_general(slot_grads, down_w[e], NT, preferred_element_type=F32)
        squash = 1.0 / (1.0 + jnp.exp(-gate_pre))
        swish = gate_pre * squash
        backs[0, here, :] = (swish * up_pre).astype(BF16)
        backs[1, here, :] = (
            act_grad * up_pre * squash * (1.0 + gate_pre * (1.0 - squash))
        ).astype(BF16)
        backs[2, here, :] = (act_grad * swish).astype(BF16)
        return 0

    lax.fori_loop(0, experts, one_expert, 0)

    replica = lax.axis_index("dp")
    share = width // replicas
    turned = {
        (block, lane): backs[0, block : block + LANES, lane : lane + size].T
        for block in range(0, slots, LANES)
        for lane, size in column_blocks(hidden)
    }
    for k in range(replicas):
        peer = replica ^ k
        at = 0
        for block in range(0, slots, LANES):
            for lane, size in column_blocks(hidden):
                packs[k][at : at + size, :] = turned[block, lane]
                at += size
        for lane in range(0, share, LANES):
            column = pl.multiple_of(width + peer * share + lane, LANES)
            packs[k][at : at + rows, :] = x_ref[:, pl.ds(column, LANES)]
            at += rows
        packs[k][at : at + rows, :] = x_ref[:, 2 * width :]


def outputs_kernel(
    backs, picker_ref, gain_ref, gate_w, up_w, down_w, keep_ref, send_one, send_two, results
):
    experts, _, width = gate_w.shape
    half = keep_ref.shape[0]
    slots = backs.shape[1]
    per_expert = slots // experts

    def one_expert(e, _):
        here = pl.ds(pl.multiple_of(e * per_expert, per_expert), per_expert)
        forward = jnp.dot(backs[0, here, :], down_w[e], preferred_element_type=F32)
        results[here, :width] = (forward.astype(BF16).astype(F32) * gain_ref[here, :]).astype(BF16)
        results[here, width:] = (
            jnp.dot(backs[1, here, :], gate_w[e], preferred_element_type=F32)
            + jnp.dot(backs[2, here, :], up_w[e], preferred_element_type=F32)
        ).astype(BF16)
        return 0

    lax.fori_loop(0, experts, one_expert, 0)
    step = min(512, width)
    for at in range(0, 2 * width, step):
        total = jnp.dot(picker_ref[...], results[:, at : at + step], preferred_element_type=F32)
        keep_ref[:, at : at + step] = total[:half].astype(BF16)
        send_ref = send_one if at < width else send_two
        to = at % width
        send_ref[:, to : to + step] = total[half:].astype(BF16)


def grad_kernel(sizes, *refs):
    top, capacity, groups, replicas = sizes
    packs = refs[:replicas]
    own_ref, out_hbm, own_out, grads, acts, result, sems = refs[replicas:]
    experts, hidden, share = out_hbm.shape
    per_replica = groups * capacity
    slots = experts * per_replica
    per_expert = replicas * per_replica
    act_rows = slots // LANES * hidden
    rows = (packs[0].shape[0] - act_rows) // (share // LANES + 1)

    first_expert = (lax.axis_index("expert") * experts).astype(F32)
    for k in range(replicas):
        at = act_rows
        routing = packs[k][at + (share // LANES) * rows :, :].astype(F32)
        chosen, gains = slot_tables(routing, top, first_expert, capacity, groups, slots)
        scatter = chosen.T.astype(BF16)
        gain = jnp.sum(gains.T, axis=1, keepdims=True)
        for lane in range(0, share, LANES):
            filled = jnp.dot(scatter, packs[k][at : at + rows, :], preferred_element_type=F32)
            filled = (gain * filled).astype(BF16)
            for e in range(experts):
                to = e * per_expert + k * per_replica
                grads[to : to + per_replica, lane : lane + LANES] = filled[
                    e * per_replica : (e + 1) * per_replica
                ]
            at += rows

    left = jnp.concatenate(
        [
            packs[k][block * hidden : (block + 1) * hidden, :]
            for k in range(replicas)
            for block in range(slots // LANES)
        ],
        axis=1,
    )
    if experts > 1:
        lanes = replicas * slots
        before = fiota((lanes, lanes), 0)
        after = fiota((lanes, lanes), 1)
        source = whole_part(before, slots)
        inner = before - source * slots
        expert = whole_part(inner, per_replica)
        place = expert * per_expert + source * per_replica + inner - expert * per_replica
        order = jnp.where(place == after, 1.0, 0.0).astype(BF16)
        left = jnp.dot(left, order, preferred_element_type=F32).astype(BF16)
    acts[...] = left

    own_out[...] = own_ref[...].astype(F32)

    copies = []
    for e in range(experts):
        low = e * per_expert // LANES * LANES
        high = -(-(e + 1) * per_expert // LANES) * LANES
        right = grads[low:high, :]
        if high - low > per_expert:
            row = lax.broadcasted_iota(jnp.int32, right.shape, 0) + low
            inside = (row >= e * per_expert) & (row < (e + 1) * per_expert)
            right = jnp.where(inside, right.astype(F32), 0.0).astype(BF16)
        total = jnp.dot(acts[:, low:high], right, preferred_element_type=F32)
        result[e] = (total * (1.0 / replicas)).astype(BF16)
        copies.append(pltpu.make_async_copy(result.at[e], out_hbm.at[e], sems.at[e]))
        copies[-1].start()
    for copy in copies:
        copy.wait()


def near_kernel(mine, keep_ref, one_ref, two_ref, own_ref, *parts):
    width = one_ref.shape[1]
    for k, part in enumerate((own_ref, *parts)):
        here = slice(k * mine, (k + 1) * mine)
        for side, ref in enumerate((one_ref, two_ref)):
            columns = slice(side * width, (side + 1) * width)
            part[:, columns] = (
                keep_ref[here, columns].astype(F32) + ref[here, :].astype(F32)
            ).astype(part.dtype)


def vmem_specs(count):
    return [pl.BlockSpec(memory_space=pltpu.VMEM)] * count


def shards(
    tokens, routes, positions, combine_weights, cotangent, gate_weight, up_weight, down_weight
):
    experts, width, hidden = gate_weight.shape
    replicas = lax.axis_size("dp")
    groups = lax.axis_size("expert")
    tensor = lax.axis_size("tensor")
    group_size, top = routes.shape
    capacity = group_size // 2
    slots = experts * groups * capacity
    mine = tokens.shape[0]
    devices = groups * tensor
    rows = mine * devices
    both = ("expert", "tensor")

    sent = pl.pallas_call(
        pack_kernel,
        out_shape=jax.ShapeDtypeStruct((mine, 2 * width + LANES), BF16),
        in_specs=vmem_specs(5),
        out_specs=vmem_specs(1)[0],
        name="pack",
    )(tokens, cotangent, routes.T, positions.T, combine_weights.T)
    gathered = lax.all_gather(sent, both, axis=0, tiled=True)

    pack_rows = slots // LANES * hidden + (width // replicas // LANES + 1) * rows
    weights = [
        pltpu.with_memory_space_constraint(jnp.swapaxes(w, 1, 2), pltpu.HBM)
        for w in (gate_weight, up_weight, down_weight)
    ]
    half = jax.ShapeDtypeStruct((rows // 2, 2 * width), BF16)
    pack = jax.ShapeDtypeStruct((pack_rows, LANES), BF16)
    held = pltpu.VMEM((experts, hidden, width), BF16)
    outs = pl.pallas_call(
        functools.partial(activations_kernel, (top, capacity, groups, tensor, replicas)),
        out_shape=[held] * 3
        + [
            jax.ShapeDtypeStruct((3, slots, hidden), BF16),
            jax.ShapeDtypeStruct((rows, slots), BF16),
            jax.ShapeDtypeStruct((slots, 1), F32),
        ]
        + [pack] * replicas,
        in_specs=vmem_specs(1) + [pl.BlockSpec(memory_space=pltpu.HBM)] * 3,
        out_specs=vmem_specs(6 + replicas),
        scratch_shapes=[
            pltpu.VMEM((slots, 2 * width), BF16),
            pltpu.SemaphoreType.DMA((experts, 3)),
        ],
        compiler_params=pltpu.CompilerParams(vmem_limit_bytes=6 * 2**20),
        cost_estimate=pl.CostEstimate(
            flops=6 * slots * hidden * width,
            bytes_accessed=6 * experts * hidden * width,
            transcendentals=slots * hidden,
        ),
        name="activations",
    )(gathered, *weights)
    held_weights = [pltpu.with_memory_space_constraint(w, pltpu.VMEM) for w in outs[:3]]
    packs = outs[6:]
    side = jax.ShapeDtypeStruct((rows // 2, width), BF16)
    keep, send_one, send_two = pl.pallas_call(
        outputs_kernel,
        out_shape=[half, side, side],
        in_specs=vmem_specs(6),
        out_specs=vmem_specs(3),
        scratch_shapes=[pltpu.VMEM((slots, 2 * width), BF16)],
        compiler_params=pltpu.CompilerParams(vmem_limit_bytes=6 * 2**20),
        cost_estimate=pl.CostEstimate(
            flops=6 * slots * hidden * width,
            bytes_accessed=6 * experts * hidden * width,
            transcendentals=0,
        ),
        name="outputs",
    )(*outs[3:6], *held_weights)

    def swap(values, distance):
        return lax.ppermute(values, both, [(i, i ^ distance) for i in range(devices)])

    own, *others_near = pl.pallas_call(
        functools.partial(near_kernel, mine),
        out_shape=[jax.ShapeDtypeStruct((mine, 2 * width), F32)]
        + [jax.ShapeDtypeStruct((mine, 2 * width), BF16)] * (devices // 2 - 1),
        in_specs=vmem_specs(3),
        out_specs=vmem_specs(devices // 2),
        compiler_params=pltpu.CompilerParams(vmem_limit_bytes=2 * 2**20),
        name="near",
    )(keep, swap(send_one, 1), swap(send_two, 1))
    received = [swap(part, 2 * k) for k, part in enumerate(others_near, 1)]

    arrived = [packs[0]]
    for k in range(1, replicas):
        arrived.append(lax.ppermute(packs[k], "dp", [(i, i ^ k) for i in range(replicas)]))
    share = width // replicas
    grad, total = pl.pallas_call(
        functools.partial(grad_kernel, (top, capacity, groups, replicas)),
        out_shape=[
            jax.ShapeDtypeStruct((experts, hidden, share), BF16),
            jax.ShapeDtypeStruct((mine, 2 * width), F32),
        ],
        in_specs=vmem_specs(replicas + 1),
        out_specs=[pl.BlockSpec(memory_space=pl.ANY)] + vmem_specs(1),
        scratch_shapes=[
            pltpu.VMEM((replicas * slots, share), BF16),
            pltpu.VMEM((hidden, replicas * slots), BF16),
            pltpu.VMEM((experts, hidden, share), BF16),
            pltpu.SemaphoreType.DMA((experts,)),
        ],
        compiler_params=pltpu.CompilerParams(vmem_limit_bytes=10 * 2**20),
        cost_estimate=pl.CostEstimate(
            flops=2 * replicas * slots * share * hidden,
            bytes_accessed=2 * experts * share * hidden,
            transcendentals=0,
        ),
        name="grad_down",
    )(*arrived, own)
    for part in received:
        total = total + part.astype(F32)
    total = total.astype(BF16)
    return (total[:, :width], total[:, width:], jnp.swapaxes(grad, 1, 2))


def solution(mesh):
    return jax.shard_map(
        shards,
        mesh=mesh,
        in_specs=(
            P(("dp", "expert", "tensor"), None),
            P(("dp", "expert"), None),
            P(("dp", "expert"), None),
            P(("dp", "expert"), None),
            P(("dp", "expert", "tensor"), None),
            P("expert", None, "tensor"),
            P("expert", None, "tensor"),
            P("expert", None, "tensor"),
        ),
        out_specs=(
            P(("dp", "expert", "tensor"), None),
            P(("dp", "expert", "tensor"), None),
            P("expert", "dp", "tensor"),
        ),
        check_vma=False,
    )
```

time: 54.2 us -> 45.9 us (0.85)
  waiting for transfers between devices: 6.03 us -> 1.44 us
  other arithmetic: 2.32 us -> 0.04 us
  starting transfers between devices: 9.29 us -> 8.57 us
  Pallas kernels: 23.8 us -> 23.2 us
    ppermute x3, waiting for transfers between devices: 6.02 us -> 0.01 us  [shards(): lax.ppermute(packs[k], 'dp', [(i, i ^ k) for i in range(replicas)])]
    another operation x3 -> x0, other arithmetic: 1.44 us -> none
    ppermute x4 -> x5, waiting for transfers between devices: 0.01 us -> 1.44 us  [swap(): lax.ppermute(values, both, [(i, i ^ distance) for i in range(devices)])]
    ppermute x4 -> x5, starting transfers between devices: 4.91 us -> 4.12 us  [swap(): lax.ppermute(values, both, [(i, i ^ distance) for i in range(devices)])]
    unnamed x1 -> x0, other arithmetic: 0.76 us -> none
    pallas_call x2 -> x5, Pallas kernels: 23.8 us -> 23.2 us  [the longest x1 12.8 us: shards(): pl.pallas_call(functools.partial(activations_kernel, (top, capacity, grou...]
  transfers between devices with their start and end apart: 7 -> 8, of which waited for: 2 -> 3; matrix products, arithmetic and copies ran while one was open for 0% -> 0% of each run, Pallas kernels for 11% -> 19%
where the time goes in v2:
time: 45.9 us; the launch traced here: 45.7 us
  Pallas kernels  23.2 us (51%)
  blocking collectives  11 us (24%)
  starting transfers between devices  8.57 us (19%)
  waiting for transfers between devices  1.44 us (3%)
  between operations  0.7 us (2%)
  local copies, waits for them, and re-layouts  0.69 us (2%)
    pallas_call x1, Pallas kernels, shards(): pl.pallas_call(functools.partial(activations_kernel, (top, capacity, grou...  12.8 us
    all_gather x1, blocking collectives, shards(): gathered = lax.all_gather(sent, both, axis=0, tiled=True)  11 us
    pallas_call x1, Pallas kernels, shards(): pl.pallas_call(outputs_kernel, out_shape=[half, side, side], in_specs=vme...  6.02 us
    ppermute x3, starting transfers between devices, shards(): lax.ppermute(packs[k], 'dp', [(i, i ^ k) for i in range(replicas)])  4.45 us
    ppermute x5, starting transfers between devices, swap(): lax.ppermute(values, both, [(i, i ^ distance) for i in range(devices)])  4.12 us
    pallas_call x1, Pallas kernels, shards(): pl.pallas_call(functools.partial(grad_kernel, (top, capacity, groups, rep...  2.77 us
    pallas_call x1, Pallas kernels, shards(): pl.pallas_call(pack_kernel, out_shape=jax.ShapeDtypeStruct((mine, 2 * wid...  1.5 us
    ppermute x5, waiting for transfers between devices, swap(): lax.ppermute(values, both, [(i, i ^ distance) for i in range(devices)])  1.44 us
  transfers between devices with their start and end apart: 8, of which 3 were waited for; matrix products, arithmetic and copies ran while one was open for 0% of the time, Pallas kernels for 19%

profile of v2, /device:TPU:0, one launch (start us, length us, event | category | flops | bytes accessed | tf_op | source)
XLA Modules:
  0.0 45.7 jit_solution(18216566125498788987)
XLA Ops:
  0.6 1.5 %pack.1 = bf16[4,4224]{1,0:T(4,128)(2,1)} custom-call(bf16[4,2048]{1,0:T(4,128)(2,1)} %tokens_ref.1, bf16[4,2048]{1,0:T(4,128)(2,1)} %cotangent_ref.1, s32[6,16]{1,0:T(8,128)} %bitcast.12, s32[6,16]{1,0:T(8,128)} %bitcast.13, f32[6,16]{1,0:T(8,128)} %bitcast.14), custom_call_target="tpu_custom_call" | custom-call | tf_op jit(solution)/shard_map/pack/pallas_call | solution.py:303
  2.1 11.0 %all-gather = bf16[8,4,4224]{2,1,0:T(4,128)(2,1)S(1)} all-gather(bf16[1,4,4224]{2,1,0:T(4,128)(2,1)} %bitcast.11), channel_id=1, replica_groups=mesh['dp'=4,'expert'=2,'tensor'=4] {'expert','tensor'}, dimensions={0}, use_global_device_ids=true | all-gather | bytes 304128 | tf_op jit(solution)/shard_map/all_gather | solution.py:310
  13.1 0.1 reshape.7.x_ref
  13.2 12.8 %activations.1 = (bf16[8,352,2048]{2,1,0:T(8,128)(2,1)S(1)}, bf16[8,352,2048]{2,1,0:T(8,128)(2,1)S(1)}, bf16[8,352,2048]{2,1,0:T(8,128)(2,1)S(1)}, bf16[3,128,35...) custom-call(bf16[32,4224]{1,0:T(8,128)(2,1)S(1)} %reshape.7.x_ref, ...), custom_call_target="tpu_custom_call" | custom-call | flops 553648128 | bytes 34603008 | tf_op jit(solution)/shard_map/activations/pallas_call | solution.py:320
  26.1 1.6 %collective-permute-start = (bf16[512,128]{1,0:T(8,128)(2,1)S(1)}, bf16[512,128]{1,0:T(8,128)(2,1)S(1)}, u32[]{:S(2)}, u32[]{:S(2)}) collective-permute-start(bf16[512,128]{1,0:T(8,128)(2,1)S(1)} %get-tuple-element.23), channel_id=1, source_target_pairs={{0,8},{8,0},{16,24},{24,16},{1,9},{9,1},{17,25},{25,17},{2,10},{10... | collective-permute-start | bytes 393224 | tf_op jit(solution)/shard_map/ppermute | solution.py:377
  27.7 2.6 %collective-permute-start.1 = (bf16[512,128]{1,0:T(8,128)(2,1)S(1)}, bf16[512,128]{1,0:T(8,128)(2,1)S(1)}, u32[]{:S(2)}, u32[]{:S(2)}) collective-permute-start(bf16[512,128]{1,0:T(8,128)(2,1)S(1)} %get-tuple-element.24), channel_id=1, source_target_pairs={{0,16},{8,24},{16,0},{24,8},{1,17},{9,25},{17,1},{25,9},{2,18},{10... | collective-permute-start | bytes 393224 | tf_op jit(solution)/shard_map/ppermute | solution.py:377
  30.3 0.2 collective-permute-start.2
  30.5 6.0 %outputs.1 = (bf16[16,4096]{1,0:T(8,128)(2,1)S(1)}, bf16[16,2048]{1,0:T(8,128)(2,1)S(1)}, bf16[16,2048]{1,0:T(8,128)(2,1)S(1)}) custom-call(bf16[3,128,352]{2,1,0:T(8,128)(2,1)S(1)} %get-tuple-element.26.backs, bf16[32,128]{1,0:T(8,128)(2,1)S(1)} %get-tuple-element.27.picker_ref, f32[128,1]{1,0:T(8,128)S(1)} %get-tuple-element.28.gain_ref, ...), custom_call_target="tpu_custom_call" | custom-call | flops 553648128 | bytes 34603008 | tf_op jit(solution)/shard_map/outputs/pallas_call | solution.py:346
  36.5 0.1 collective-permute-start.3
  36.6 0.5 %collective-permute-start.4 = (bf16[16,2048]{1,0:T(8,128)(2,1)S(1)}, bf16[16,2048]{1,0:T(8,128)(2,1)S(1)}, u32[]{:S(2)}, u32[]{:S(2)}) collective-permute-start(bf16[16,2048]{1,0:T(8,128)(2,1)S(1)} %get-tuple-element.34), channel_id=1, source_target_pairs={{0,1},{1,0},{2,3},{3,2},{4,5},{5,4},{6,7},{7,6},{8,9},{9,8},{10,11... | collective-permute-start | bytes 196616 | tf_op jit(solution)/shard_map/ppermute | solution.py:362
  37.1 0.7 %collective-permute-done.3.one_ref = bf16[16,2048]{1,0:T(8,128)(2,1)S(1)} collective-permute-done((bf16[16,2048]{1,0:T(8,128)(2,1)S(1)}, bf16[16,2048]{1,0:T(8,128)(2,1)S(1)}, u32[]{:S(2)}, u32[]{:S(2)}) %collective-permute-start.3) | collective-permute-done | bytes 65568 | tf_op jit(solution)/shard_map/ppermute | solution.py:362
  37.9 0.2 collective-permute-done.4.two_ref
  38.0 0.1 near.1
  38.1 1.4 %collective-permute-start.5 = (bf16[4,4096]{1,0:T(4,128)(2,1)S(1)}, bf16[4,4096]{1,0:T(4,128)(2,1)S(1)}, u32[]{:S(2)}, u32[]{:S(2)}) collective-permute-start(bf16[4,4096]{1,0:T(4,128)(2,1)S(1)} %get-tuple-element.37), channel_id=1, source_target_pairs={{0,2},{1,3},{2,0},{3,1},{4,6},{5,7},{6,4},{7,5},{8,10},{9,11},{10,... | collective-permute-start | bytes 98312 | tf_op jit(solution)/shard_map/ppermute | solution.py:362
  39.4 0.7 %collective-permute-start.6 = (bf16[4,4096]{1,0:T(4,128)(2,1)S(1)}, bf16[4,4096]{1,0:T(4,128)(2,1)S(1)}, u32[]{:S(2)}, u32[]{:S(2)}) collective-permute-start(bf16[4,4096]{1,0:T(4,128)(2,1)S(1)} %get-tuple-element.38), channel_id=1, source_target_pairs={{0,4},{1,5},{2,6},{3,7},{4,0},{5,1},{6,2},{7,3},{8,12},{9,13},{10,... | collective-permute-start | bytes 98312 | tf_op jit(solution)/shard_map/ppermute | solution.py:362
  40.2 0.0 collective-permute-done.refs_1_
  40.2 1.5 %collective-permute-start.7 = (bf16[4,4096]{1,0:T(4,128)(2,1)S(1)}, bf16[4,4096]{1,0:T(4,128)(2,1)S(1)}, u32[]{:S(2)}, u32[]{:S(2)}) collective-permute-start(bf16[4,4096]{1,0:T(4,128)(2,1)S(1)} %get-tuple-element.39), channel_id=1, source_target_pairs={{0,6},{1,7},{2,4},{3,5},{4,2},{5,3},{6,0},{7,1},{8,14},{9,15},{10,... | collective-permute-start | bytes 98312 | tf_op jit(solution)/shard_map/ppermute | solution.py:362
  41.6 0.0 collective-permute-done.1.refs_2_
  41.7 0.0 collective-permute-done.2.refs_3_
  41.7 2.8 %grad_down.1 = (bf16[8,352,512]{2,1,0:T(8,128)(2,1)}, f32[4,4096]{1,0:T(4,128)S(1)}) custom-call(bf16[512,128]{1,0:T(8,128)(2,1)S(1)} %get-tuple-element.22.refs_0_, bf16[512,128]{1,0:T(8,128)(2,1)S(1)} %collective-permute-done.refs_1_, bf16[512,128]{1,0:T(8,128)(2,1)S(1)} %collective-permute-done.1.refs_2_, ...), custom_call_target="tpu_custom_call" | custom-call | flops 184549376 | bytes 2883584 | tf_op jit(solution)/shard_map/grad_down/pallas_call | solution.py:379
  44.4 0.0 collective-permute-done.5
  44.4 0.0 collective-permute-done.6
  44.5 0.5 %collective-permute-done.7 = bf16[4,4096]{1,0:T(4,128)(2,1)S(1)} collective-permute-done((bf16[4,4096]{1,0:T(4,128)(2,1)S(1)}, bf16[4,4096]{1,0:T(4,128)(2,1)S(1)}, u32[]{:S(2)}, u32[]{:S(2)}) %collective-permute-start.7) | collective-permute-done | bytes 32800 | tf_op jit(solution)/shard_map/ppermute | solution.py:362
  45.0 0.6 %fusion = (bf16[4,2048]{1,0:T(4,128)(2,1)}, bf16[4,2048]{1,0:T(4,128)(2,1)}) fusion(bf16[4,4096]{1,0:T(4,128)(2,1)S(1)} %add_convert_fusion), kind=kLoop, calls=%fused_computation.1 | loop fusion | bytes 65536 | tf_op jit(solution)/shard_map/slice | solution.py:404
  (1 shorter events, 0.0 us)
Async XLA Ops:
  26.1 14.1 %collective-permute-start = (bf16[512,128]{1,0:T(8,128)(2,1)S(1)}, bf16[512,128]{1,0:T(8,128)(2,1)S(1)}, u32[]{:S(2)}, u32[]{:S(2)}) collective-permute-start(bf16[512,128]{1,0:T(8,128)(2,1)S(1)} %get-tuple-element.23), channel_id=1, source_target_pairs={{0,8},{8,0},{16,24},{24,16},{1,9},{9,1},{17,25},{25,17},{2,10},{10... | collective-permute-start | bytes 393224 | tf_op jit(solution)/shard_map/ppermute | solution.py:377
  27.7 14.0 %collective-permute-start.1 = (bf16[512,128]{1,0:T(8,128)(2,1)S(1)}, bf16[512,128]{1,0:T(8,128)(2,1)S(1)}, u32[]{:S(2)}, u32[]{:S(2)}) collective-permute-start(bf16[512,128]{1,0:T(8,128)(2,1)S(1)} %get-tuple-element.24), channel_id=1, source_target_pairs={{0,16},{8,24},{16,0},{24,8},{1,17},{9,25},{17,1},{25,9},{2,18},{10... | collective-permute-start | bytes 393224 | tf_op jit(solution)/shard_map/ppermute | solution.py:377
  30.3 11.4 %collective-permute-start.2 = (bf16[512,128]{1,0:T(8,128)(2,1)S(1)}, bf16[512,128]{1,0:T(8,128)(2,1)S(1)}, u32[]{:S(2)}, u32[]{:S(2)}) collective-permute-start(bf16[512,128]{1,0:T(8,128)(2,1)S(1)} %get-tuple-element.25), channel_id=1, source_target_pairs={{0,24},{8,16},{16,8},{24,0},{1,25},{9,17},{17,9},{25,1},{2,26},{10... | collective-permute-start | bytes 393224 | tf_op jit(solution)/shard_map/ppermute | solution.py:377
  36.5 1.3 %collective-permute-start.3 = (bf16[16,2048]{1,0:T(8,128)(2,1)S(1)}, bf16[16,2048]{1,0:T(8,128)(2,1)S(1)}, u32[]{:S(2)}, u32[]{:S(2)}) collective-permute-start(bf16[16,2048]{1,0:T(8,128)(2,1)S(1)} %get-tuple-element.33), channel_id=1, source_target_pairs={{0,1},{1,0},{2,3},{3,2},{4,5},{5,4},{6,7},{7,6},{8,9},{9,8},{10,11... | collective-permute-start | bytes 196616 | tf_op jit(solution)/shard_map/ppermute | solution.py:362
  36.6 1.4 %collective-permute-start.4 = (bf16[16,2048]{1,0:T(8,128)(2,1)S(1)}, bf16[16,2048]{1,0:T(8,128)(2,1)S(1)}, u32[]{:S(2)}, u32[]{:S(2)}) collective-permute-start(bf16[16,2048]{1,0:T(8,128)(2,1)S(1)} %get-tuple-element.34), channel_id=1, source_target_pairs={{0,1},{1,0},{2,3},{3,2},{4,5},{5,4},{6,7},{7,6},{8,9},{9,8},{10,11... | collective-permute-start | bytes 196616 | tf_op jit(solution)/shard_map/ppermute | solution.py:362
  38.1 6.3 %collective-permute-start.5 = (bf16[4,4096]{1,0:T(4,128)(2,1)S(1)}, bf16[4,4096]{1,0:T(4,128)(2,1)S(1)}, u32[]{:S(2)}, u32[]{:S(2)}) collective-permute-start(bf16[4,4096]{1,0:T(4,128)(2,1)S(1)} %get-tuple-element.37), channel_id=1, source_target_pairs={{0,2},{1,3},{2,0},{3,1},{4,6},{5,7},{6,4},{7,5},{8,10},{9,11},{10,... | collective-permute-start | bytes 98312 | tf_op jit(solution)/shard_map/ppermute | solution.py:362
  39.4 5.0 %collective-permute-start.6 = (bf16[4,4096]{1,0:T(4,128)(2,1)S(1)}, bf16[4,4096]{1,0:T(4,128)(2,1)S(1)}, u32[]{:S(2)}, u32[]{:S(2)}) collective-permute-start(bf16[4,4096]{1,0:T(4,128)(2,1)S(1)} %get-tuple-element.38), channel_id=1, source_target_pairs={{0,4},{1,5},{2,6},{3,7},{4,0},{5,1},{6,2},{7,3},{8,12},{9,13},{10,... | collective-permute-start | bytes 98312 | tf_op jit(solution)/shard_map/ppermute | solution.py:362
  40.2 4.8 %collective-permute-start.7 = (bf16[4,4096]{1,0:T(4,128)(2,1)S(1)}, bf16[4,4096]{1,0:T(4,128)(2,1)S(1)}, u32[]{:S(2)}, u32[]{:S(2)}) collective-permute-start(bf16[4,4096]{1,0:T(4,128)(2,1)S(1)} %get-tuple-element.39), channel_id=1, source_target_pairs={{0,6},{1,7},{2,4},{3,5},{4,2},{5,3},{6,0},{7,1},{8,14},{9,15},{10,... | collective-permute-start | bytes 98312 | tf_op jit(solution)/shard_map/ppermute | solution.py:362

commit v3 on v2

--- a/solution.py
+++ b/solution.py
@@ -10,6 +10,8 @@
 F32 = jnp.float32
 BF16 = jnp.bfloat16
 LANES = 128
+EARLY = 3
+LEAD = 4
 NT = (((1,), (1,)), ((), ()))
 TN = (((0,), (0,)), ((), ()))
 
@@ -22,10 +24,22 @@
     return lax.broadcasted_iota(jnp.int32, shape, axis).astype(F32)
 
 
-def slot_tables(routing, top, first_expert, capacity, groups, slots):
+def row_tokens(rows, devices, tensor):
+    device = lax.axis_index("expert") * tensor + lax.axis_index("tensor")
+    pair = lax.div(device, 2)
+    parity = device - pair * 2
+    mine = rows // devices
+    row = lax.broadcasted_iota(jnp.int32, (rows, 1), 0)
+    second = jnp.where(row >= rows // 2, 1, 0)
+    within = row - second * (rows // 2)
+    block = lax.div(within, jnp.full_like(within, mine))
+    token = (block ^ pair) * (2 * mine) + (second ^ parity) * mine + within - block * mine
+    return token.astype(F32)
+
+
+def slot_tables(routing, token, top, first_expert, capacity, groups, slots):
     rows = routing.shape[0]
     lane = fiota((rows, slots), 1)
-    token = fiota((rows, slots), 0)
     expert = whole_part(lane, groups * capacity)
     inner = lane - expert * (groups * capacity)
     group = whole_part(inner, capacity)
@@ -46,9 +60,34 @@
     return [(at, min(LANES, width - at)) for at in range(0, width, LANES)]
 
 
-def pack_kernel(tokens_ref, cotangent_ref, routes_ref, positions_ref, weights_ref, out_ref):
-    mine, width = tokens_ref.shape
+def fetch_experts(weights, held, sems, first, last):
+    return [
+        pltpu.make_async_copy(source.at[e], target.at[e], sems.at[e, i])
+        for e in range(first, last)
+        for i, (source, target) in enumerate(zip(weights, held))
+    ]
+
+
+def pack_kernel(*refs):
+    sources, out_ref = refs[:5], refs[5]
+    routes_ref, positions_ref, weights_ref, sems = refs[6:]
+    mine, width = sources[0].shape
     top, group_size = routes_ref.shape
+    targets = (
+        out_ref.at[:, :width],
+        out_ref.at[:, width : 2 * width],
+        routes_ref,
+        positions_ref,
+        weights_ref,
+    )
+    copies = [
+        pltpu.make_async_copy(source, target, sems.at[i])
+        for i, (source, target) in enumerate(zip(sources, targets))
+    ]
+    for copy in copies:
+        copy.start()
+    for copy in copies:
+        copy.wait()
     weights = weights_ref[...]
     high = weights.astype(BF16)
     low = (weights - high.astype(F32)).astype(BF16)
@@ -61,103 +100,91 @@
     row = lax.broadcasted_iota(jnp.int32, (mine, group_size), 0)
     pick = jnp.where(column == row + first, 1.0, 0.0).astype(BF16)
     routing = lax.dot_general(pick, table, NT, preferred_element_type=F32)
-    out_ref[:, :width] = tokens_ref[...]
-    out_ref[:, width : 2 * width] = cotangent_ref[...]
     out_ref[:, 2 * width :] = jnp.concatenate(
         [routing, jnp.zeros((mine, LANES - 4 * top), F32)], axis=1
     ).astype(BF16)
 
 
+def join_kernel(*refs):
+    out_ref = refs[-3]
+    mine = refs[0].shape[0]
+    for k, block in enumerate(refs[:-5]):
+        out_ref[k * mine : (k + 1) * mine, :] = block[...]
+
+
+def fetch_kernel(last, *refs):
+    weights, held, sems = refs[:2], refs[2:4], refs[4]
+    copies = fetch_experts(weights, held, sems, 0, last)
+    for copy in copies:
+        copy.start()
+    for copy in copies:
+        copy.wait()
+
+
 def activations_kernel(
-    sizes, x_ref, gate_hbm, up_hbm, down_hbm, gate_w, up_w, down_w, backs, picker_ref, gain_ref, *rest
+    sizes, ready, lead, x_ref, far_ref, gate_hbm, up_hbm, down_hbm, *rest
 ):
     top, capacity, groups, tensor, replicas = sizes
-    packs = rest[:replicas]
-    filled, sems = rest[replicas:]
+    gate_w, up_w, down_w, activations, slope_ref, swish_ref, grads_ref, picker_ref, gain_ref = rest[2:11]
+    packs = rest[11 : 11 + replicas]
+    filled, sems, down_sems = rest[11 + replicas :]
     experts, hidden, width = gate_hbm.shape
-    rows = x_ref.shape[0]
+    half = x_ref.shape[0]
+    rows = 2 * half
     slots = filled.shape[0]
     per_expert = slots // experts
-    ahead = min(3, experts)
-
-    def fetch(e):
-        return [
-            pltpu.make_async_copy(source.at[e], target.at[e], sems.at[e, i])
-            for i, (source, target) in enumerate(
-                ((gate_hbm, gate_w), (up_hbm, up_w), (down_hbm, down_w))
-            )
-        ]
-
-    for e in range(ahead):
-        for copy in fetch(e):
-            copy.start()
+    batches = [
+        fetch_experts((gate_hbm, up_hbm), (gate_w, up_w), sems, first, min(first + 2, experts))
+        for first in range(ready, experts, 2)
+    ]
+    downs = fetch_experts((down_hbm,), (down_w,), down_sems, 0, lead)
+    for copy in sum(batches[:2], []):
+        copy.start()
 
     first_expert = (lax.axis_index("expert") * experts).astype(F32)
-    routing = x_ref[:, 2 * width :].astype(F32)
-    chosen, gains = slot_tables(routing, top, first_expert, capacity, groups, slots)
+    routing = jnp.concatenate([x_ref[:, 2 * width :], far_ref[:, 2 * width :]], axis=0).astype(F32)
+    token = row_tokens(rows, groups * tensor, tensor)
+    chosen, gains = slot_tables(routing, token, top, first_expert, capacity, groups, slots)
     scatter = chosen.T.astype(BF16)
     gain = jnp.sum(gains.T, axis=1, keepdims=True)
     gain_ref[...] = gain
+    picker_ref[...] = chosen.astype(BF16)
     step = min(512, width)
-    for at in range(0, width, step):
-        filled[:, at : at + step] = jnp.dot(
-            scatter, x_ref[:, at : at + step], preferred_element_type=F32
-        ).astype(BF16)
-    for at in range(width, 2 * width, step):
-        filled[:, at : at + step] = (
-            gain * jnp.dot(scatter, x_ref[:, at : at + step], preferred_element_type=F32)
-        ).astype(BF16)
-
-    device = lax.axis_index("expert") * tensor + lax.axis_index("tensor")
-    pair = lax.div(device, 2)
-    parity = device - pair * 2
-    per_device = rows // (groups * tensor)
-    half = rows // 2
-    row = lax.broadcasted_iota(jnp.int32, (rows, 1), 0)
-    second = jnp.where(row >= half, 1, 0)
-    within = row - second * half
-    block = lax.div(within, jnp.full_like(within, per_device))
-    token = (
-        (block ^ pair) * (2 * per_device)
-        + (second ^ parity) * per_device
-        + within
-        - block * per_device
-    )
-    order = jnp.where(lax.broadcasted_iota(jnp.int32, (rows, rows), 1) == token, 1.0, 0.0)
-    picker_ref[...] = jnp.dot(
-        order.astype(BF16), chosen.astype(BF16), preferred_element_type=F32
-    ).astype(BF16)
-
-    def one_expert(e, _):
-        for copy in fetch(e):
-            copy.wait()
-
-        @pl.when(e + ahead < experts)
-        def _():
-            for copy in fetch(e + ahead):
+    for at in range(0, 2 * width, step):
+        given = jnp.concatenate([x_ref[:, at : at + step], far_ref[:, at : at + step]], axis=0)
+        slot_rows = jnp.dot(scatter, given, preferred_element_type=F32)
+        if at < width:
+            filled[:, at : at + step] = slot_rows.astype(BF16)
+        else:
+            grads_ref[:, at - width : at - width + step] = (gain * slot_rows).astype(BF16)
+
+    for e in range(experts):
+        if e >= ready and (e - ready) % 2 == 0:
+            at = (e - ready) // 2
+            for copy in batches[at]:
+                copy.wait()
+            for copy in batches[at + 2] if at + 2 < len(batches) else []:
                 copy.start()
-
-        here = pl.ds(pl.multiple_of(e * per_expert, per_expert), per_expert)
-        slot_rows = filled[here, :width]
-        slot_grads = filled[here, width:]
+            if at + 3 == len(batches):
+                for copy in downs:
+                    copy.start()
+        here = slice(e * per_expert, (e + 1) * per_expert)
+        slot_rows = filled[here, :]
         gate_pre = lax.dot_general(slot_rows, gate_w[e], NT, preferred_element_type=F32)
         up_pre = lax.dot_general(slot_rows, up_w[e], NT, preferred_element_type=F32)
-        act_grad = lax.dot_general(slot_grads, down_w[e], NT, preferred_element_type=F32)
         squash = 1.0 / (1.0 + jnp.exp(-gate_pre))
         swish = gate_pre * squash
-        backs[0, here, :] = (swish * up_pre).astype(BF16)
-        backs[1, here, :] = (
-            act_grad * up_pre * squash * (1.0 + gate_pre * (1.0 - squash))
-        ).astype(BF16)
-        backs[2, here, :] = (act_grad * swish).astype(BF16)
-        return 0
-
-    lax.fori_loop(0, experts, one_expert, 0)
+        activations[here, :] = (swish * up_pre).astype(BF16)
+        slope_ref[here, :] = up_pre * squash * (1.0 + gate_pre * (1.0 - squash))
+        swish_ref[here, :] = swish
+    if len(batches) < 3:
+        for copy in downs:
+            copy.start()
 
     replica = lax.axis_index("dp")
     share = width // replicas
     turned = {
-        (block, lane): backs[0, block : block + LANES, lane : lane + size].T
+        (block, lane): activations[block : block + LANES, lane : lane + size].T
         for block in range(0, slots, LANES)
         for lane, size in column_blocks(hidden)
     }
@@ -170,30 +197,43 @@
                 at += size
         for lane in range(0, share, LANES):
             column = pl.multiple_of(width + peer * share + lane, LANES)
-            packs[k][at : at + rows, :] = x_ref[:, pl.ds(column, LANES)]
+            packs[k][at : at + half, :] = x_ref[:, pl.ds(column, LANES)]
+            packs[k][at + half : at + rows, :] = far_ref[:, pl.ds(column, LANES)]
             at += rows
-        packs[k][at : at + rows, :] = x_ref[:, 2 * width :]
+        packs[k][at : at + half, :] = x_ref[:, 2 * width :]
+        packs[k][at + half : at + rows, :] = far_ref[:, 2 * width :]
+    for copy in downs:
+        copy.wait()
 
 
 def outputs_kernel(
-    backs, picker_ref, gain_ref, gate_w, up_w, down_w, keep_ref, send_one, send_two, results
+    lead, activations, slope_ref, swish_ref, grads_ref, picker_ref, gain_ref, gate_w, up_w, unused, down_hbm,
+    keep_ref, send_one, send_two, down_w, results, backs, sems
 ):
     experts, _, width = gate_w.shape
     half = keep_ref.shape[0]
-    slots = backs.shape[1]
+    slots = activations.shape[0]
     per_expert = slots // experts
-
-    def one_expert(e, _):
-        here = pl.ds(pl.multiple_of(e * per_expert, per_expert), per_expert)
-        forward = jnp.dot(backs[0, here, :], down_w[e], preferred_element_type=F32)
+    copies = fetch_experts((down_hbm,), (down_w,), sems, lead, experts)
+    for copy in copies:
+        copy.start()
+    for e in range(experts):
+        if e >= lead and (e - lead) % 2 == 0:
+            for copy in copies[e - lead : e - lead + 2]:
+                copy.wait()
+        here = slice(e * per_expert, (e + 1) * per_expert)
+        act_grad = lax.dot_general(grads_ref[here, :], down_w[e], NT, preferred_element_type=F32)
+        backs[0, here, :] = (act_grad * slope_ref[here, :]).astype(BF16)
+        backs[1, here, :] = (act_grad * swish_ref[here, :]).astype(BF16)
+        forward = jnp.dot(activations[here, :], down_w[e], preferred_element_type=F32)
         results[here, :width] = (forward.astype(BF16).astype(F32) * gain_ref[here, :]).astype(BF16)
+    for e in range(experts):
+        here = slice(e * per_expert, (e + 1) * per_expert)
         results[here, width:] = (
-            jnp.dot(backs[1, here, :], gate_w[e], preferred_element_type=F32)
-            + jnp.dot(backs[2, here, :], up_w[e], preferred_element_type=F32)
+            jnp.dot(backs[0, here, :], gate_w[e], preferred_element_type=F32)
+            + jnp.dot(backs[1, here, :], up_w[e], preferred_element_type=F32)
         ).astype(BF16)
-        return 0
-
-    lax.fori_loop(0, experts, one_expert, 0)
+
     step = min(512, width)
     for at in range(0, 2 * width, step):
         total = jnp.dot(picker_ref[...], results[:, at : at + step], preferred_element_type=F32)
@@ -204,7 +244,7 @@
 
 
 def grad_kernel(sizes, *refs):
-    top, capacity, groups, replicas = sizes
+    top, capacity, groups, tensor, replicas = sizes
     packs = refs[:replicas]
     own_ref, out_hbm, own_out, grads, acts, result, sems = refs[replicas:]
     experts, hidden, share = out_hbm.shape
@@ -215,10 +255,13 @@
     rows = (packs[0].shape[0] - act_rows) // (share // LANES + 1)
 
     first_expert = (lax.axis_index("expert") * experts).astype(F32)
+    token = row_tokens(rows, groups * tensor, tensor)
     for k in range(replicas):
         at = act_rows
         routing = packs[k][at + (share // LANES) * rows :, :].astype(F32)
-        chosen, gains = slot_tables(routing, top, first_expert, capacity, groups, slots)
+        chosen, gains = slot_tables(
+            routing, token, top, first_expert, capacity, groups, slots
+        )
         scatter = chosen.T.astype(BF16)
         gain = jnp.sum(gains.T, axis=1, keepdims=True)
         for lane in range(0, share, LANES):
@@ -281,6 +324,10 @@
             ).astype(part.dtype)
 
 
+def hbm_specs(count):
+    return [pl.BlockSpec(memory_space=pltpu.HBM)] * count
+
+
 def vmem_specs(count):
     return [pl.BlockSpec(memory_space=pltpu.VMEM)] * count
 
@@ -300,66 +347,115 @@
     rows = mine * devices
     both = ("expert", "tensor")
 
-    sent = pl.pallas_call(
-        pack_kernel,
-        out_shape=jax.ShapeDtypeStruct((mine, 2 * width + LANES), BF16),
-        in_specs=vmem_specs(5),
-        out_specs=vmem_specs(1)[0],
-        name="pack",
-    )(tokens, cotangent, routes.T, positions.T, combine_weights.T)
-    gathered = lax.all_gather(sent, both, axis=0, tiled=True)
-
-    pack_rows = slots // LANES * hidden + (width // replicas // LANES + 1) * rows
+    def swap(values, distance):
+        return lax.ppermute(values, both, [(i, i ^ distance) for i in range(devices)])
+
     weights = [
         pltpu.with_memory_space_constraint(jnp.swapaxes(w, 1, 2), pltpu.HBM)
         for w in (gate_weight, up_weight, down_weight)
     ]
+    held = pltpu.VMEM((experts, hidden, width), BF16)
+    ready = min(EARLY, experts)
+    inputs = [
+        pltpu.with_memory_space_constraint(x, pltpu.HBM)
+        for x in (tokens, cotangent, routes.T, positions.T, combine_weights.T)
+    ]
+    row = jax.ShapeDtypeStruct((mine, 2 * width + LANES), BF16)
+    sent = pl.pallas_call(
+        pack_kernel,
+        out_shape=row,
+        in_specs=hbm_specs(5),
+        out_specs=vmem_specs(1)[0],
+        scratch_shapes=[
+            pltpu.VMEM((top, group_size), jnp.int32),
+            pltpu.VMEM((top, group_size), jnp.int32),
+            pltpu.VMEM((top, group_size), F32),
+            pltpu.SemaphoreType.DMA((5,)),
+        ],
+        compiler_params=pltpu.CompilerParams(vmem_limit_bytes=2 * 2**20),
+        name="pack",
+    )(*inputs)
+    held_weights = pl.pallas_call(
+        functools.partial(fetch_kernel, ready),
+        out_shape=[held] * 2,
+        in_specs=hbm_specs(2),
+        out_specs=vmem_specs(2),
+        scratch_shapes=[pltpu.SemaphoreType.DMA((experts, 2))],
+        compiler_params=pltpu.CompilerParams(vmem_limit_bytes=2**20),
+        name="fetch",
+    )(*weights[:2])
+    blocks = devices // 2
+    kept = [pltpu.with_memory_space_constraint(w, pltpu.VMEM) for w in held_weights]
+    near_rows, *held_weights = pl.pallas_call(
+        join_kernel,
+        out_shape=[jax.ShapeDtypeStruct((rows // 2, 2 * width + LANES), BF16)] + [held] * 2,
+        in_specs=vmem_specs(blocks + 2),
+        out_specs=vmem_specs(3),
+        input_output_aliases={blocks: 1, blocks + 1: 2},
+        compiler_params=pltpu.CompilerParams(vmem_limit_bytes=2 * 2**20),
+        name="join",
+    )(sent, *[swap(sent, 2 * k) for k in range(1, blocks)], *kept)
+    far_rows = swap(near_rows, 1)
+
+    pack_rows = slots // LANES * hidden + (width // replicas // LANES + 1) * rows
     half = jax.ShapeDtypeStruct((rows // 2, 2 * width), BF16)
     pack = jax.ShapeDtypeStruct((pack_rows, LANES), BF16)
-    held = pltpu.VMEM((experts, hidden, width), BF16)
+    kept = [pltpu.with_memory_space_constraint(w, pltpu.VMEM) for w in held_weights]
+    lead = min(LEAD, experts)
+    slot_wide = jax.ShapeDtypeStruct((slots, width), BF16)
+    slot_narrow = jax.ShapeDtypeStruct((slots, hidden), F32)
     outs = pl.pallas_call(
-        functools.partial(activations_kernel, (top, capacity, groups, tensor, replicas)),
+        functools.partial(
+            activations_kernel, (top, capacity, groups, tensor, replicas), ready, lead
+        ),
         out_shape=[held] * 3
         + [
-            jax.ShapeDtypeStruct((3, slots, hidden), BF16),
+            jax.ShapeDtypeStruct((slots, hidden), BF16),
+            slot_narrow,
+            slot_narrow,
+            slot_wide,
             jax.ShapeDtypeStruct((rows, slots), BF16),
             jax.ShapeDtypeStruct((slots, 1), F32),
         ]
         + [pack] * replicas,
-        in_specs=vmem_specs(1) + [pl.BlockSpec(memory_space=pltpu.HBM)] * 3,
-        out_specs=vmem_specs(6 + replicas),
+        in_specs=vmem_specs(2) + hbm_specs(3) + vmem_specs(2),
+        out_specs=vmem_specs(9 + replicas),
         scratch_shapes=[
-            pltpu.VMEM((slots, 2 * width), BF16),
-            pltpu.SemaphoreType.DMA((experts, 3)),
+            pltpu.VMEM((slots, width), BF16),
+            pltpu.SemaphoreType.DMA((experts, 2)),
+            pltpu.SemaphoreType.DMA((experts, 1)),
         ],
+        input_output_aliases={5: 0, 6: 1},
         compiler_params=pltpu.CompilerParams(vmem_limit_bytes=6 * 2**20),
         cost_estimate=pl.CostEstimate(
-            flops=6 * slots * hidden * width,
-            bytes_accessed=6 * experts * hidden * width,
+            flops=4 * slots * hidden * width,
+            bytes_accessed=4 * experts * hidden * width,
             transcendentals=slots * hidden,
         ),
         name="activations",
-    )(gathered, *weights)
-    held_weights = [pltpu.with_memory_space_constraint(w, pltpu.VMEM) for w in outs[:3]]
-    packs = outs[6:]
+    )(near_rows, far_rows, *weights, *kept)
+    kept = [pltpu.with_memory_space_constraint(w, pltpu.VMEM) for w in outs[:3]]
+    packs = outs[9:]
     side = jax.ShapeDtypeStruct((rows // 2, width), BF16)
-    keep, send_one, send_two = pl.pallas_call(
-        outputs_kernel,
-        out_shape=[half, side, side],
-        in_specs=vmem_specs(6),
-        out_specs=vmem_specs(3),
-        scratch_shapes=[pltpu.VMEM((slots, 2 * width), BF16)],
+    keep, send_one, send_two, _ = pl.pallas_call(
+        functools.partial(outputs_kernel, lead),
+        out_shape=[half, side, side, held],
+        in_specs=vmem_specs(9) + hbm_specs(1),
+        out_specs=vmem_specs(4),
+        scratch_shapes=[
+            pltpu.VMEM((slots, 2 * width), BF16),
+            pltpu.VMEM((2, slots, hidden), BF16),
+            pltpu.SemaphoreType.DMA((experts, 1)),
+        ],
+        input_output_aliases={8: 3},
         compiler_params=pltpu.CompilerParams(vmem_limit_bytes=6 * 2**20),
         cost_estimate=pl.CostEstimate(
-            flops=6 * slots * hidden * width,
+            flops=8 * slots * hidden * width,
             bytes_accessed=6 * experts * hidden * width,
             transcendentals=0,
         ),
         name="outputs",
-    )(*outs[3:6], *held_weights)
-
-    def swap(values, distance):
-        return lax.ppermute(values, both, [(i, i ^ distance) for i in range(devices)])
+    )(*outs[3:9], *kept, weights[2])
 
     own, *others_near = pl.pallas_call(
         functools.partial(near_kernel, mine),
@@ -377,7 +473,7 @@
         arrived.append(lax.ppermute(packs[k], "dp", [(i, i ^ k) for i in range(replicas)]))
     share = width // replicas
     grad, total = pl.pallas_call(
-        functools.partial(grad_kernel, (top, capacity, groups, replicas)),
+        functools.partial(grad_kernel, (top, capacity, groups, tensor, replicas)),
         out_shape=[
             jax.ShapeDtypeStruct((experts, hidden, share), BF16),
             jax.ShapeDtypeStruct((mine, 2 * width), F32),

time: 45.9 us -> 42.3 us (0.922)
  blocking collectives: 11 us -> 0 us
  starting transfers between devices: 8.57 us -> 13.3 us
  waiting for transfers between devices: 1.44 us -> 4.13 us
    all_gather x1 -> x0, blocking collectives: 11 us -> none  [shards(): gathered = lax.all_gather(sent, both, axis=0, tiled=True)]
    pallas_call x1, Pallas kernels: 12.8 us -> 7.41 us  [shards(): pl.pallas_call(functools.partial(activations_kernel, (top, capacity, grou...]
    pallas_call x3 -> x5, Pallas kernels: 10.3 us -> 15.7 us  [the longest x1 8.31 us: shards(): pl.pallas_call(functools.partial(outputs_kernel, lead), out_shape=[half,...]
    ppermute x5 -> x9, starting transfers between devices: 4.12 us -> 8.79 us  [swap(): lax.ppermute(values, both, [(i, i ^ distance) for i in range(devices)])]
    ppermute x5 -> x9, waiting for transfers between devices: 1.44 us -> 4.12 us  [swap(): lax.ppermute(values, both, [(i, i ^ distance) for i in range(devices)])]
  transfers between devices with their start and end apart: 8 -> 12, of which waited for: 3 -> 5; matrix products, arithmetic and copies ran while one was open for 0% -> 0% of each run, Pallas kernels for 19% -> 35%
where the time goes in v3:
time: 42.3 us; the launch traced here: 42 us
  Pallas kernels  23.2 us (55%)
  starting transfers between devices  13.3 us (31%)
  waiting for transfers between devices  4.13 us (10%)
  between operations  0.74 us (2%)
  local copies, waits for them, and re-layouts  0.62 us (1%)
    ppermute x9, starting transfers between devices, swap(): lax.ppermute(values, both, [(i, i ^ distance) for i in range(devices)])  8.79 us
    pallas_call x1, Pallas kernels, shards(): pl.pallas_call(functools.partial(outputs_kernel, lead), out_shape=[half,...  8.31 us
    pallas_call x1, Pallas kernels, shards(): pl.pallas_call(functools.partial(activations_kernel, (top, capacity, grou...  7.41 us
    ppermute x3, starting transfers between devices, shards(): lax.ppermute(packs[k], 'dp', [(i, i ^ k) for i in range(replicas)])  4.53 us
    ppermute x9, waiting for transfers between devices, swap(): lax.ppermute(values, both, [(i, i ^ distance) for i in range(devices)])  4.12 us
    pallas_call x1, Pallas kernels, shards(): pl.pallas_call(functools.partial(fetch_kernel, ready), out_shape=[held] *...  3.64 us
    pallas_call x1, Pallas kernels, shards(): pl.pallas_call(functools.partial(grad_kernel, (top, capacity, groups, ten...  2.77 us
    pallas_call x1, Pallas kernels, shards(): pl.pallas_call(pack_kernel, out_shape=row, in_specs=hbm_specs(5), out_spe...  0.92 us
  transfers between devices with their start and end apart: 12, of which 5 were waited for; matrix products, arithmetic and copies ran while one was open for 0% of the time, Pallas kernels for 35%

profile of v3, /device:TPU:0, one launch (start us, length us, event | category | flops | bytes accessed | tf_op | source)
XLA Modules:
  0.0 42.0 jit_solution(13595065882458217765)
XLA Ops:
  0.6 0.9 %pack.1.refs_0_ = bf16[4,4224]{1,0:T(4,128)(2,1)S(1)} custom-call(bf16[4,2048]{1,0:T(4,128)(2,1)} %refs_0_.1, bf16[4,2048]{1,0:T(4,128)(2,1)} %refs_1_.1, s32[6,16]{1,0:T(8,128)} %bitcast.13, s32[6,16]{1,0:T(8,128)} %bitcast.14, f32[6,16]{1,0:T(8,128)} %bitcast.15), custom_call_target="tpu_custom_call" | custom-call | tf_op jit(solution)/shard_map/pack/pallas_call | solution.py:364
  1.6 4.0 %collective-permute-start.2 = (bf16[4,4224]{1,0:T(4,128)(2,1)S(1)}, bf16[4,4224]{1,0:T(4,128)(2,1)S(1)}, u32[]{:S(2)}, u32[]{:S(2)}) collective-permute-start(bf16[4,4224]{1,0:T(4,128)(2,1)S(1)} %pack.1.refs_0_), channel_id=1, source_target_pairs={{0,6},{1,7},{2,4},{3,5},{4,2},{5,3},{6,0},{7,1},{8,14},{9,15},{10,... | collective-permute-start | bytes 101384 | tf_op jit(solution)/shard_map/ppermute | solution.py:351
  5.5 0.5 %collective-permute-start.1 = (bf16[4,4224]{1,0:T(4,128)(2,1)S(1)}, bf16[4,4224]{1,0:T(4,128)(2,1)S(1)}, u32[]{:S(2)}, u32[]{:S(2)}) collective-permute-start(bf16[4,4224]{1,0:T(4,128)(2,1)S(1)} %pack.1.refs_0_), channel_id=1, source_target_pairs={{0,4},{1,5},{2,6},{3,7},{4,0},{5,1},{6,2},{7,3},{8,12},{9,13},{10,... | collective-permute-start | bytes 101384 | tf_op jit(solution)/shard_map/ppermute | solution.py:351
  6.0 0.1 collective-permute-start
  6.2 3.6 %fetch.1 = (bf16[8,352,2048]{2,1,0:T(8,128)(2,1)S(1)}, bf16[8,352,2048]{2,1,0:T(8,128)(2,1)S(1)}) custom-call(bf16[8,352,2048]{2,1,0:T(8,128)(2,1)} %bitcast.7, bf16[8,352,2048]{2,1,0:T(8,128)(2,1)} %bitcast.9), custom_call_target="tpu_custom_call" | custom-call | tf_op jit(solution)/shard_map/fetch/pallas_call | solution.py:378
  9.8 0.0 collective-permute-done.1.refs_2_
  9.8 0.1 collective-permute-done.refs_1_
  10.0 0.1 collective-permute-start.3
  10.1 1.3 %collective-permute-done.3.far_ref = bf16[16,4224]{1,0:T(8,128)(2,1)S(1)} collective-permute-done((bf16[16,4224]{1,0:T(8,128)(2,1)S(1)}, bf16[16,4224]{1,0:T(8,128)(2,1)S(1)}, u32[]{:S(2)}, u32[]{:S(2)}) %collective-permute-start.3) | collective-permute-done | bytes 135200 | tf_op jit(solution)/shard_map/ppermute | solution.py:351
  11.4 7.4 %activations.1 = (bf16[8,352,2048]{2,1,0:T(8,128)(2,1)S(1)}, bf16[8,352,2048]{2,1,0:T(8,128)(2,1)S(1)}, bf16[8,352,2048]{2,1,0:T(8,128)(2,1)S(1)}, bf16[128,352]...) custom-call(bf16[16,4224]{1,0:T(8,128)(2,1)S(1)} %get-tuple-element., ...), custom_call_target="tpu_custom_call", output_to_operand_aliasing={{0}: (5, {}), {1}: (6, {})} | custom-call | flops 369098752 | bytes 23068672 | tf_op jit(solution)/shard_map/activations/pallas_call | solution.py:407
  18.8 1.9 %collective-permute-start.4 = (bf16[512,128]{1,0:T(8,128)(2,1)S(1)}, bf16[512,128]{1,0:T(8,128)(2,1)S(1)}, u32[]{:S(2)}, u32[]{:S(2)}) collective-permute-start(bf16[512,128]{1,0:T(8,128)(2,1)S(1)} %get-tuple-element.36), channel_id=1, source_target_pairs={{0,8},{8,0},{16,24},{24,16},{1,9},{9,1},{17,25},{25,17},{2,10},{10... | collective-permute-start | bytes 393224 | tf_op jit(solution)/shard_map/ppermute | solution.py:473
  20.8 2.6 %collective-permute-start.5 = (bf16[512,128]{1,0:T(8,128)(2,1)S(1)}, bf16[512,128]{1,0:T(8,128)(2,1)S(1)}, u32[]{:S(2)}, u32[]{:S(2)}) collective-permute-start(bf16[512,128]{1,0:T(8,128)(2,1)S(1)} %get-tuple-element.37), channel_id=1, source_target_pairs={{0,16},{8,24},{16,0},{24,8},{1,17},{9,25},{17,1},{25,9},{2,18},{10... | collective-permute-start | bytes 393224 | tf_op jit(solution)/shard_map/ppermute | solution.py:473
  23.4 8.3 %outputs.1 = (bf16[16,4096]{1,0:T(8,128)(2,1)S(1)}, bf16[16,2048]{1,0:T(8,128)(2,1)S(1)}, bf16[16,2048]{1,0:T(8,128)(2,1)S(1)}, bf16[8,352,2048]{2,1,0:T(8,128)(2,1)S(1)}) custom-call(bf16[128,352]{1,0:T(8,128)(2,1)S(1)} %get-tuple-element.39.activations, f32[128,352]{1,0:T(8,128)S(1)} %get-tuple-element.40.slope_ref, ...), custom_call_target="tpu_custom_call", output_to_operand_aliasing={{3}: (8, {})} | custom-call | flops 738197504 | bytes 34603008 | tf_op jit(solution)/shard_map/outputs/pallas_call | solution.py:440
  31.7 0.1 collective-permute-start.7
  31.8 0.5 %collective-permute-start.8 = (bf16[16,2048]{1,0:T(8,128)(2,1)S(1)}, bf16[16,2048]{1,0:T(8,128)(2,1)S(1)}, u32[]{:S(2)}, u32[]{:S(2)}) collective-permute-start(bf16[16,2048]{1,0:T(8,128)(2,1)S(1)} %get-tuple-element.50), channel_id=1, source_target_pairs={{0,1},{1,0},{2,3},{3,2},{4,5},{5,4},{6,7},{7,6},{8,9},{9,8},{10,11... | collective-permute-start | bytes 196616 | tf_op jit(solution)/shard_map/ppermute | solution.py:351
  32.3 0.7 %collective-permute-done.7.one_ref = bf16[16,2048]{1,0:T(8,128)(2,1)S(1)} collective-permute-done((bf16[16,2048]{1,0:T(8,128)(2,1)S(1)}, bf16[16,2048]{1,0:T(8,128)(2,1)S(1)}, u32[]{:S(2)}, u32[]{:S(2)}) %collective-permute-start.7) | collective-permute-done | bytes 65568 | tf_op jit(solution)/shard_map/ppermute | solution.py:351
  33.0 0.2 collective-permute-done.8.two_ref
  33.2 0.1 near.1
  33.2 1.8 %collective-permute-start.9 = (bf16[4,4096]{1,0:T(4,128)(2,1)S(1)}, bf16[4,4096]{1,0:T(4,128)(2,1)S(1)}, u32[]{:S(2)}, u32[]{:S(2)}) collective-permute-start(bf16[4,4096]{1,0:T(4,128)(2,1)S(1)} %get-tuple-element.53), channel_id=1, source_target_pairs={{0,2},{1,3},{2,0},{3,1},{4,6},{5,7},{6,4},{7,5},{8,10},{9,11},{10,... | collective-permute-start | bytes 98312 | tf_op jit(solution)/shard_map/ppermute | solution.py:351
  35.0 1.5 %collective-permute-start.10 = (bf16[4,4096]{1,0:T(4,128)(2,1)S(1)}, bf16[4,4096]{1,0:T(4,128)(2,1)S(1)}, u32[]{:S(2)}, u32[]{:S(2)}) collective-permute-start(bf16[4,4096]{1,0:T(4,128)(2,1)S(1)} %get-tuple-element.54), channel_id=1, source_target_pairs={{0,4},{1,5},{2,6},{3,7},{4,0},{5,1},{6,2},{7,3},{8,12},{9,13},{10,... | collective-permute-start | bytes 98312 | tf_op jit(solution)/shard_map/ppermute | solution.py:351
  36.5 0.3 collective-permute-start.11
  36.8 2.8 %grad_down.1 = (bf16[8,352,512]{2,1,0:T(8,128)(2,1)}, f32[4,4096]{1,0:T(4,128)S(1)}) custom-call(bf16[512,128]{1,0:T(8,128)(2,1)S(1)} %get-tuple-element.35.refs_0_, bf16[512,128]{1,0:T(8,128)(2,1)S(1)} %collective-permute-done.4.refs_1_, bf16[512,128]{1,0:T(8,128)(2,1)S(1)} %collective-permute-done.5.refs_2_, ...), custom_call_target="tpu_custom_call" | custom-call | flops 184549376 | bytes 2883584 | tf_op jit(solution)/shard_map/grad_down/pallas_call | solution.py:475
  39.6 1.7 %collective-permute-done.11 = bf16[4,4096]{1,0:T(4,128)(2,1)S(1)} collective-permute-done((bf16[4,4096]{1,0:T(4,128)(2,1)S(1)}, bf16[4,4096]{1,0:T(4,128)(2,1)S(1)}, u32[]{:S(2)}, u32[]{:S(2)}) %collective-permute-start.11) | collective-permute-done | bytes 32800 | tf_op jit(solution)/shard_map/ppermute | solution.py:351
  41.4 0.6 %fusion = (bf16[4,2048]{1,0:T(4,128)(2,1)}, bf16[4,2048]{1,0:T(4,128)(2,1)}) fusion(bf16[4,4096]{1,0:T(4,128)(2,1)S(1)} %add_convert_fusion), kind=kLoop, calls=%fused_computation.1 | loop fusion | bytes 65536 | tf_op jit(solution)/shard_map/slice | solution.py:500
  (9 shorter events, 0.1 us)
Async XLA Ops:
  1.6 8.3 %collective-permute-start.2 = (bf16[4,4224]{1,0:T(4,128)(2,1)S(1)}, bf16[4,4224]{1,0:T(4,128)(2,1)S(1)}, u32[]{:S(2)}, u32[]{:S(2)}) collective-permute-start(bf16[4,4224]{1,0:T(4,128)(2,1)S(1)} %pack.1.refs_0_), channel_id=1, source_target_pairs={{0,6},{1,7},{2,4},{3,5},{4,2},{5,3},{6,0},{7,1},{8,14},{9,15},{10,... | collective-permute-start | bytes 101384 | tf_op jit(solution)/shard_map/ppermute | solution.py:351
  5.5 4.3 %collective-permute-start.1 = (bf16[4,4224]{1,0:T(4,128)(2,1)S(1)}, bf16[4,4224]{1,0:T(4,128)(2,1)S(1)}, u32[]{:S(2)}, u32[]{:S(2)}) collective-permute-start(bf16[4,4224]{1,0:T(4,128)(2,1)S(1)} %pack.1.refs_0_), channel_id=1, source_target_pairs={{0,4},{1,5},{2,6},{3,7},{4,0},{5,1},{6,2},{7,3},{8,12},{9,13},{10,... | collective-permute-start | bytes 101384 | tf_op jit(solution)/shard_map/ppermute | solution.py:351
  6.0 3.9 %collective-permute-start = (bf16[4,4224]{1,0:T(4,128)(2,1)S(1)}, bf16[4,4224]{1,0:T(4,128)(2,1)S(1)}, u32[]{:S(2)}, u32[]{:S(2)}) collective-permute-start(bf16[4,4224]{1,0:T(4,128)(2,1)S(1)} %pack.1.refs_0_), channel_id=1, source_target_pairs={{0,2},{1,3},{2,0},{3,1},{4,6},{5,7},{6,4},{7,5},{8,10},{9,11},{10,... | collective-permute-start | bytes 101384 | tf_op jit(solution)/shard_map/ppermute | solution.py:351
  10.0 1.4 %collective-permute-start.3 = (bf16[16,4224]{1,0:T(8,128)(2,1)S(1)}, bf16[16,4224]{1,0:T(8,128)(2,1)S(1)}, u32[]{:S(2)}, u32[]{:S(2)}) collective-permute-start(bf16[16,4224]{1,0:T(8,128)(2,1)S(1)} %get-tuple-element.32.x_ref), channel_id=1, source_target_pairs={{0,1},{1,0},{2,3},{3,2},{4,5},{5,4},{6,7},{7,6},{8,9},{9,8},{10,11... | collective-permute-start | bytes 405512 | tf_op jit(solution)/shard_map/ppermute | solution.py:351
  18.8 17.7 %collective-permute-start.4 = (bf16[512,128]{1,0:T(8,128)(2,1)S(1)}, bf16[512,128]{1,0:T(8,128)(2,1)S(1)}, u32[]{:S(2)}, u32[]{:S(2)}) collective-permute-start(bf16[512,128]{1,0:T(8,128)(2,1)S(1)} %get-tuple-element.36), channel_id=1, source_target_pairs={{0,8},{8,0},{16,24},{24,16},{1,9},{9,1},{17,25},{25,17},{2,10},{10... | collective-permute-start | bytes 393224 | tf_op jit(solution)/shard_map/ppermute | solution.py:473
  20.8 16.0 %collective-permute-start.5 = (bf16[512,128]{1,0:T(8,128)(2,1)S(1)}, bf16[512,128]{1,0:T(8,128)(2,1)S(1)}, u32[]{:S(2)}, u32[]{:S(2)}) collective-permute-start(bf16[512,128]{1,0:T(8,128)(2,1)S(1)} %get-tuple-element.37), channel_id=1, source_target_pairs={{0,16},{8,24},{16,0},{24,8},{1,17},{9,25},{17,1},{25,9},{2,18},{10... | collective-permute-start | bytes 393224 | tf_op jit(solution)/shard_map/ppermute | solution.py:473
  23.4 13.4 %collective-permute-start.6 = (bf16[512,128]{1,0:T(8,128)(2,1)S(1)}, bf16[512,128]{1,0:T(8,128)(2,1)S(1)}, u32[]{:S(2)}, u32[]{:S(2)}) collective-permute-start(bf16[512,128]{1,0:T(8,128)(2,1)S(1)} %get-tuple-element.38), channel_id=1, source_target_pairs={{0,24},{8,16},{16,8},{24,0},{1,25},{9,17},{17,9},{25,1},{2,26},{10... | collective-permute-start | bytes 393224 | tf_op jit(solution)/shard_map/ppermute | solution.py:473
  31.7 1.3 %collective-permute-start.7 = (bf16[16,2048]{1,0:T(8,128)(2,1)S(1)}, bf16[16,2048]{1,0:T(8,128)(2,1)S(1)}, u32[]{:S(2)}, u32[]{:S(2)}) collective-permute-start(bf16[16,2048]{1,0:T(8,128)(2,1)S(1)} %get-tuple-element.49), channel_id=1, source_target_pairs={{0,1},{1,0},{2,3},{3,2},{4,5},{5,4},{6,7},{7,6},{8,9},{9,8},{10,11... | collective-permute-start | bytes 196616 | tf_op jit(solution)/shard_map/ppermute | solution.py:351
  31.8 1.4 %collective-permute-start.8 = (bf16[16,2048]{1,0:T(8,128)(2,1)S(1)}, bf16[16,2048]{1,0:T(8,128)(2,1)S(1)}, u32[]{:S(2)}, u32[]{:S(2)}) collective-permute-start(bf16[16,2048]{1,0:T(8,128)(2,1)S(1)} %get-tuple-element.50), channel_id=1, source_target_pairs={{0,1},{1,0},{2,3},{3,2},{4,5},{5,4},{6,7},{7,6},{8,9},{9,8},{10,11... | collective-permute-start | bytes 196616 | tf_op jit(solution)/shard_map/ppermute | solution.py:351
  33.2 6.3 %collective-permute-start.9 = (bf16[4,4096]{1,0:T(4,128)(2,1)S(1)}, bf16[4,4096]{1,0:T(4,128)(2,1)S(1)}, u32[]{:S(2)}, u32[]{:S(2)}) collective-permute-start(bf16[4,4096]{1,0:T(4,128)(2,1)S(1)} %get-tuple-element.53), channel_id=1, source_target_pairs={{0,2},{1,3},{2,0},{3,1},{4,6},{5,7},{6,4},{7,5},{8,10},{9,11},{10,... | collective-permute-start | bytes 98312 | tf_op jit(solution)/shard_map/ppermute | solution.py:351
  35.0 4.6 %collective-permute-start.10 = (bf16[4,4096]{1,0:T(4,128)(2,1)S(1)}, bf16[4,4096]{1,0:T(4,128)(2,1)S(1)}, u32[]{:S(2)}, u32[]{:S(2)}) collective-permute-start(bf16[4,4096]{1,0:T(4,128)(2,1)S(1)} %get-tuple-element.54), channel_id=1, source_target_pairs={{0,4},{1,5},{2,6},{3,7},{4,0},{5,1},{6,2},{7,3},{8,12},{9,13},{10,... | collective-permute-start | bytes 98312 | tf_op jit(solution)/shard_map/ppermute | solution.py:351
  36.5 4.8 %collective-permute-start.11 = (bf16[4,4096]{1,0:T(4,128)(2,1)S(1)}, bf16[4,4096]{1,0:T(4,128)(2,1)S(1)}, u32[]{:S(2)}, u32[]{:S(2)}) collective-permute-start(bf16[4,4096]{1,0:T(4,128)(2,1)S(1)} %get-tuple-element.55), channel_id=1, source_target_pairs={{0,6},{1,7},{2,4},{3,5},{4,2},{5,3},{6,0},{7,1},{8,14},{9,15},{10,... | collective-permute-start | bytes 98312 | tf_op jit(solution)/shard_map/ppermute | solution.py:351

commit v4 on v3

--- a/solution.py
+++ b/solution.py
@@ -217,6 +217,13 @@
     copies = fetch_experts((down_hbm,), (down_w,), sems, lead, experts)
     for copy in copies:
         copy.start()
+    def last_products(e):
+        here = slice(e * per_expert, (e + 1) * per_expert)
+        results[here, width:] = (
+            jnp.dot(backs[0, here, :], gate_w[e], preferred_element_type=F32)
+            + jnp.dot(backs[1, here, :], up_w[e], preferred_element_type=F32)
+        ).astype(BF16)
+
     for e in range(experts):
         if e >= lead and (e - lead) % 2 == 0:
             for copy in copies[e - lead : e - lead + 2]:
@@ -227,12 +234,9 @@
         backs[1, here, :] = (act_grad * swish_ref[here, :]).astype(BF16)
         forward = jnp.dot(activations[here, :], down_w[e], preferred_element_type=F32)
         results[here, :width] = (forward.astype(BF16).astype(F32) * gain_ref[here, :]).astype(BF16)
-    for e in range(experts):
-        here = slice(e * per_expert, (e + 1) * per_expert)
-        results[here, width:] = (
-            jnp.dot(backs[0, here, :], gate_w[e], preferred_element_type=F32)
-            + jnp.dot(backs[1, here, :], up_w[e], preferred_element_type=F32)
-        ).astype(BF16)
+        if e > 0:
+            last_products(e - 1)
+    last_products(experts - 1)
 
     step = min(512, width)
     for at in range(0, 2 * width, step):
@@ -494,9 +498,7 @@
         ),
         name="grad_down",
     )(*arrived, own)
-    for part in received:
-        total = total + part.astype(F32)
-    total = total.astype(BF16)
+    total = (total + sum(part.astype(F32) for part in received[::-1])).astype(BF16)
     return (total[:, :width], total[:, width:], jnp.swapaxes(grad, 1, 2))
 
 

time: 42.3 us -> 41.2 us (0.974)
  waiting for transfers between devices: 4.13 us -> 3.18 us
    ppermute x9, waiting for transfers between devices: 4.12 us -> 3.17 us  [swap(): lax.ppermute(values, both, [(i, i ^ distance) for i in range(devices)])]
  transfers between devices with their start and end apart: 12 -> 12, of which waited for: 5 -> 6; matrix products, arithmetic and copies ran while one was open for 0% -> 0% of each run, Pallas kernels for 35% -> 36%
where the time goes in v4:
time: 41.2 us; the launch traced here: 40.9 us
  Pallas kernels  23 us (56%)
  starting transfers between devices  13.3 us (32%)
  waiting for transfers between devices  3.18 us (8%)
  between operations  0.73 us (2%)
  local copies, waits for them, and re-layouts  0.62 us (2%)
    ppermute x9, starting transfers between devices, swap(): lax.ppermute(values, both, [(i, i ^ distance) for i in range(devices)])  8.79 us
    pallas_call x1, Pallas kernels, shards(): pl.pallas_call(functools.partial(outputs_kernel, lead), out_shape=[half,...  8.16 us
    pallas_call x1, Pallas kernels, shards(): pl.pallas_call(functools.partial(activations_kernel, (top, capacity, grou...  7.41 us
    ppermute x3, starting transfers between devices, shards(): lax.ppermute(packs[k], 'dp', [(i, i ^ k) for i in range(replicas)])  4.53 us
    pallas_call x1, Pallas kernels, shards(): pl.pallas_call(functools.partial(fetch_kernel, ready), out_shape=[held] *...  3.64 us
    ppermute x9, waiting for transfers between devices, swap(): lax.ppermute(values, both, [(i, i ^ distance) for i in range(devices)])  3.17 us
    pallas_call x1, Pallas kernels, shards(): pl.pallas_call(functools.partial(grad_kernel, (top, capacity, groups, ten...  2.77 us
    pallas_call x1, Pallas kernels, shards(): pl.pallas_call(pack_kernel, out_shape=row, in_specs=hbm_specs(5), out_spe...  0.92 us
  transfers between devices with their start and end apart: 12, of which 6 were waited for; matrix products, arithmetic and copies ran while one was open for 0% of the time, Pallas kernels for 36%

profile of v4, /device:TPU:0, one launch (start us, length us, event | category | flops | bytes accessed | tf_op | source)
XLA Modules:
  0.0 40.9 jit_solution(4508284103470774989)
XLA Ops:
  0.6 0.9 %pack.1.refs_0_ = bf16[4,4224]{1,0:T(4,128)(2,1)S(1)} custom-call(bf16[4,2048]{1,0:T(4,128)(2,1)} %refs_0_.1, bf16[4,2048]{1,0:T(4,128)(2,1)} %refs_1_.1, s32[6,16]{1,0:T(8,128)} %bitcast.13, s32[6,16]{1,0:T(8,128)} %bitcast.14, f32[6,16]{1,0:T(8,128)} %bitcast.15), custom_call_target="tpu_custom_call" | custom-call | tf_op jit(solution)/shard_map/pack/pallas_call | solution.py:368
  1.6 4.0 %collective-permute-start.2 = (bf16[4,4224]{1,0:T(4,128)(2,1)S(1)}, bf16[4,4224]{1,0:T(4,128)(2,1)S(1)}, u32[]{:S(2)}, u32[]{:S(2)}) collective-permute-start(bf16[4,4224]{1,0:T(4,128)(2,1)S(1)} %pack.1.refs_0_), channel_id=1, source_target_pairs={{0,6},{1,7},{2,4},{3,5},{4,2},{5,3},{6,0},{7,1},{8,14},{9,15},{10,... | collective-permute-start | bytes 101384 | tf_op jit(solution)/shard_map/ppermute | solution.py:355
  5.5 0.5 %collective-permute-start.1 = (bf16[4,4224]{1,0:T(4,128)(2,1)S(1)}, bf16[4,4224]{1,0:T(4,128)(2,1)S(1)}, u32[]{:S(2)}, u32[]{:S(2)}) collective-permute-start(bf16[4,4224]{1,0:T(4,128)(2,1)S(1)} %pack.1.refs_0_), channel_id=1, source_target_pairs={{0,4},{1,5},{2,6},{3,7},{4,0},{5,1},{6,2},{7,3},{8,12},{9,13},{10,... | collective-permute-start | bytes 101384 | tf_op jit(solution)/shard_map/ppermute | solution.py:355
  6.0 0.1 collective-permute-start
  6.2 3.6 %fetch.1 = (bf16[8,352,2048]{2,1,0:T(8,128)(2,1)S(1)}, bf16[8,352,2048]{2,1,0:T(8,128)(2,1)S(1)}) custom-call(bf16[8,352,2048]{2,1,0:T(8,128)(2,1)} %bitcast.7, bf16[8,352,2048]{2,1,0:T(8,128)(2,1)} %bitcast.9), custom_call_target="tpu_custom_call" | custom-call | tf_op jit(solution)/shard_map/fetch/pallas_call | solution.py:382
  9.8 0.1 collective-permute-done.refs_1_
  10.0 0.1 collective-permute-start.3
  10.1 1.3 %collective-permute-done.3.far_ref = bf16[16,4224]{1,0:T(8,128)(2,1)S(1)} collective-permute-done((bf16[16,4224]{1,0:T(8,128)(2,1)S(1)}, bf16[16,4224]{1,0:T(8,128)(2,1)S(1)}, u32[]{:S(2)}, u32[]{:S(2)}) %collective-permute-start.3) | collective-permute-done | bytes 135200 | tf_op jit(solution)/shard_map/ppermute | solution.py:355
  11.4 7.4 %activations.1 = (bf16[8,352,2048]{2,1,0:T(8,128)(2,1)S(1)}, bf16[8,352,2048]{2,1,0:T(8,128)(2,1)S(1)}, bf16[8,352,2048]{2,1,0:T(8,128)(2,1)S(1)}, bf16[128,352]...) custom-call(bf16[16,4224]{1,0:T(8,128)(2,1)S(1)} %get-tuple-element., ...), custom_call_target="tpu_custom_call", output_to_operand_aliasing={{0}: (5, {}), {1}: (6, {})} | custom-call | flops 369098752 | bytes 23068672 | tf_op jit(solution)/shard_map/activations/pallas_call | solution.py:411
  18.8 1.9 %collective-permute-start.4 = (bf16[512,128]{1,0:T(8,128)(2,1)S(1)}, bf16[512,128]{1,0:T(8,128)(2,1)S(1)}, u32[]{:S(2)}, u32[]{:S(2)}) collective-permute-start(bf16[512,128]{1,0:T(8,128)(2,1)S(1)} %get-tuple-element.36), channel_id=1, source_target_pairs={{0,8},{8,0},{16,24},{24,16},{1,9},{9,1},{17,25},{25,17},{2,10},{10... | collective-permute-start | bytes 393224 | tf_op jit(solution)/shard_map/ppermute | solution.py:477
  20.8 2.6 %collective-permute-start.5 = (bf16[512,128]{1,0:T(8,128)(2,1)S(1)}, bf16[512,128]{1,0:T(8,128)(2,1)S(1)}, u32[]{:S(2)}, u32[]{:S(2)}) collective-permute-start(bf16[512,128]{1,0:T(8,128)(2,1)S(1)} %get-tuple-element.37), channel_id=1, source_target_pairs={{0,16},{8,24},{16,0},{24,8},{1,17},{9,25},{17,1},{25,9},{2,18},{10... | collective-permute-start | bytes 393224 | tf_op jit(solution)/shard_map/ppermute | solution.py:477
  23.4 8.2 %outputs.1 = (bf16[16,4096]{1,0:T(8,128)(2,1)S(1)}, bf16[16,2048]{1,0:T(8,128)(2,1)S(1)}, bf16[16,2048]{1,0:T(8,128)(2,1)S(1)}, bf16[8,352,2048]{2,1,0:T(8,128)(2,1)S(1)}) custom-call(bf16[128,352]{1,0:T(8,128)(2,1)S(1)} %get-tuple-element.39.activations, f32[128,352]{1,0:T(8,128)S(1)} %get-tuple-element.40.slope_ref, ...), custom_call_target="tpu_custom_call", output_to_operand_aliasing={{3}: (8, {})} | custom-call | flops 738197504 | bytes 34603008 | tf_op jit(solution)/shard_map/outputs/pallas_call | solution.py:444
  31.5 0.1 collective-permute-start.7
  31.6 0.5 %collective-permute-start.8 = (bf16[16,2048]{1,0:T(8,128)(2,1)S(1)}, bf16[16,2048]{1,0:T(8,128)(2,1)S(1)}, u32[]{:S(2)}, u32[]{:S(2)}) collective-permute-start(bf16[16,2048]{1,0:T(8,128)(2,1)S(1)} %get-tuple-element.50), channel_id=1, source_target_pairs={{0,1},{1,0},{2,3},{3,2},{4,5},{5,4},{6,7},{7,6},{8,9},{9,8},{10,11... | collective-permute-start | bytes 196616 | tf_op jit(solution)/shard_map/ppermute | solution.py:355
  32.1 0.7 %collective-permute-done.7.one_ref = bf16[16,2048]{1,0:T(8,128)(2,1)S(1)} collective-permute-done((bf16[16,2048]{1,0:T(8,128)(2,1)S(1)}, bf16[16,2048]{1,0:T(8,128)(2,1)S(1)}, u32[]{:S(2)}, u32[]{:S(2)}) %collective-permute-start.7) | collective-permute-done | bytes 65568 | tf_op jit(solution)/shard_map/ppermute | solution.py:355
  32.9 0.2 collective-permute-done.8.two_ref
  33.0 0.1 near.1
  33.1 2.7 %collective-permute-start.9 = (bf16[4,4096]{1,0:T(4,128)(2,1)S(1)}, bf16[4,4096]{1,0:T(4,128)(2,1)S(1)}, u32[]{:S(2)}, u32[]{:S(2)}) collective-permute-start(bf16[4,4096]{1,0:T(4,128)(2,1)S(1)} %get-tuple-element.53), channel_id=1, source_target_pairs={{0,6},{1,7},{2,4},{3,5},{4,2},{5,3},{6,0},{7,1},{8,14},{9,15},{10,... | collective-permute-start | bytes 98312 | tf_op jit(solution)/shard_map/ppermute | solution.py:355
  35.8 0.5 %collective-permute-start.10 = (bf16[4,4096]{1,0:T(4,128)(2,1)S(1)}, bf16[4,4096]{1,0:T(4,128)(2,1)S(1)}, u32[]{:S(2)}, u32[]{:S(2)}) collective-permute-start(bf16[4,4096]{1,0:T(4,128)(2,1)S(1)} %get-tuple-element.54), channel_id=1, source_target_pairs={{0,4},{1,5},{2,6},{3,7},{4,0},{5,1},{6,2},{7,3},{8,12},{9,13},{10,... | collective-permute-start | bytes 98312 | tf_op jit(solution)/shard_map/ppermute | solution.py:355
  36.3 0.3 collective-permute-start.11
  36.7 2.8 %grad_down.1 = (bf16[8,352,512]{2,1,0:T(8,128)(2,1)}, f32[4,4096]{1,0:T(4,128)S(1)}) custom-call(bf16[512,128]{1,0:T(8,128)(2,1)S(1)} %get-tuple-element.35.refs_0_, bf16[512,128]{1,0:T(8,128)(2,1)S(1)} %collective-permute-done.4.refs_1_, bf16[512,128]{1,0:T(8,128)(2,1)S(1)} %collective-permute-done.5.refs_2_, ...), custom_call_target="tpu_custom_call" | custom-call | flops 184549376 | bytes 2883584 | tf_op jit(solution)/shard_map/grad_down/pallas_call | solution.py:479
  39.4 0.3 collective-permute-done.10
  39.7 0.5 %collective-permute-done.11 = bf16[4,4096]{1,0:T(4,128)(2,1)S(1)} collective-permute-done((bf16[4,4096]{1,0:T(4,128)(2,1)S(1)}, bf16[4,4096]{1,0:T(4,128)(2,1)S(1)}, u32[]{:S(2)}, u32[]{:S(2)}) %collective-permute-start.11) | collective-permute-done | bytes 32800 | tf_op jit(solution)/shard_map/ppermute | solution.py:355
  40.3 0.6 %fusion = (bf16[4,2048]{1,0:T(4,128)(2,1)}, bf16[4,2048]{1,0:T(4,128)(2,1)}) fusion(bf16[4,4096]{1,0:T(4,128)(2,1)S(1)} %add_convert_fusion), kind=kLoop, calls=%fused_computation.1 | loop fusion | bytes 65536 | tf_op jit(solution)/shard_map/slice | solution.py:502
  (9 shorter events, 0.1 us)
Async XLA Ops:
  1.6 8.3 %collective-permute-start.2 = (bf16[4,4224]{1,0:T(4,128)(2,1)S(1)}, bf16[4,4224]{1,0:T(4,128)(2,1)S(1)}, u32[]{:S(2)}, u32[]{:S(2)}) collective-permute-start(bf16[4,4224]{1,0:T(4,128)(2,1)S(1)} %pack.1.refs_0_), channel_id=1, source_target_pairs={{0,6},{1,7},{2,4},{3,5},{4,2},{5,3},{6,0},{7,1},{8,14},{9,15},{10,... | collective-permute-start | bytes 101384 | tf_op jit(solution)/shard_map/ppermute | solution.py:355
  5.5 4.3 %collective-permute-start.1 = (bf16[4,4224]{1,0:T(4,128)(2,1)S(1)}, bf16[4,4224]{1,0:T(4,128)(2,1)S(1)}, u32[]{:S(2)}, u32[]{:S(2)}) collective-permute-start(bf16[4,4224]{1,0:T(4,128)(2,1)S(1)} %pack.1.refs_0_), channel_id=1, source_target_pairs={{0,4},{1,5},{2,6},{3,7},{4,0},{5,1},{6,2},{7,3},{8,12},{9,13},{10,... | collective-permute-start | bytes 101384 | tf_op jit(solution)/shard_map/ppermute | solution.py:355
  6.0 3.9 %collective-permute-start = (bf16[4,4224]{1,0:T(4,128)(2,1)S(1)}, bf16[4,4224]{1,0:T(4,128)(2,1)S(1)}, u32[]{:S(2)}, u32[]{:S(2)}) collective-permute-start(bf16[4,4224]{1,0:T(4,128)(2,1)S(1)} %pack.1.refs_0_), channel_id=1, source_target_pairs={{0,2},{1,3},{2,0},{3,1},{4,6},{5,7},{6,4},{7,5},{8,10},{9,11},{10,... | collective-permute-start | bytes 101384 | tf_op jit(solution)/shard_map/ppermute | solution.py:355
  10.0 1.4 %collective-permute-start.3 = (bf16[16,4224]{1,0:T(8,128)(2,1)S(1)}, bf16[16,4224]{1,0:T(8,128)(2,1)S(1)}, u32[]{:S(2)}, u32[]{:S(2)}) collective-permute-start(bf16[16,4224]{1,0:T(8,128)(2,1)S(1)} %get-tuple-element.32.x_ref), channel_id=1, source_target_pairs={{0,1},{1,0},{2,3},{3,2},{4,5},{5,4},{6,7},{7,6},{8,9},{9,8},{10,11... | collective-permute-start | bytes 405512 | tf_op jit(solution)/shard_map/ppermute | solution.py:355
  18.8 17.5 %collective-permute-start.4 = (bf16[512,128]{1,0:T(8,128)(2,1)S(1)}, bf16[512,128]{1,0:T(8,128)(2,1)S(1)}, u32[]{:S(2)}, u32[]{:S(2)}) collective-permute-start(bf16[512,128]{1,0:T(8,128)(2,1)S(1)} %get-tuple-element.36), channel_id=1, source_target_pairs={{0,8},{8,0},{16,24},{24,16},{1,9},{9,1},{17,25},{25,17},{2,10},{10... | collective-permute-start | bytes 393224 | tf_op jit(solution)/shard_map/ppermute | solution.py:477
  20.8 15.9 %collective-permute-start.5 = (bf16[512,128]{1,0:T(8,128)(2,1)S(1)}, bf16[512,128]{1,0:T(8,128)(2,1)S(1)}, u32[]{:S(2)}, u32[]{:S(2)}) collective-permute-start(bf16[512,128]{1,0:T(8,128)(2,1)S(1)} %get-tuple-element.37), channel_id=1, source_target_pairs={{0,16},{8,24},{16,0},{24,8},{1,17},{9,25},{17,1},{25,9},{2,18},{10... | collective-permute-start | bytes 393224 | tf_op jit(solution)/shard_map/ppermute | solution.py:477
  23.4 13.3 %collective-permute-start.6 = (bf16[512,128]{1,0:T(8,128)(2,1)S(1)}, bf16[512,128]{1,0:T(8,128)(2,1)S(1)}, u32[]{:S(2)}, u32[]{:S(2)}) collective-permute-start(bf16[512,128]{1,0:T(8,128)(2,1)S(1)} %get-tuple-element.38), channel_id=1, source_target_pairs={{0,24},{8,16},{16,8},{24,0},{1,25},{9,17},{17,9},{25,1},{2,26},{10... | collective-permute-start | bytes 393224 | tf_op jit(solution)/shard_map/ppermute | solution.py:477
  31.5 1.3 %collective-permute-start.7 = (bf16[16,2048]{1,0:T(8,128)(2,1)S(1)}, bf16[16,2048]{1,0:T(8,128)(2,1)S(1)}, u32[]{:S(2)}, u32[]{:S(2)}) collective-permute-start(bf16[16,2048]{1,0:T(8,128)(2,1)S(1)} %get-tuple-element.49), channel_id=1, source_target_pairs={{0,1},{1,0},{2,3},{3,2},{4,5},{5,4},{6,7},{7,6},{8,9},{9,8},{10,11... | collective-permute-start | bytes 196616 | tf_op jit(solution)/shard_map/ppermute | solution.py:355
  31.6 1.4 %collective-permute-start.8 = (bf16[16,2048]{1,0:T(8,128)(2,1)S(1)}, bf16[16,2048]{1,0:T(8,128)(2,1)S(1)}, u32[]{:S(2)}, u32[]{:S(2)}) collective-permute-start(bf16[16,2048]{1,0:T(8,128)(2,1)S(1)} %get-tuple-element.50), channel_id=1, source_target_pairs={{0,1},{1,0},{2,3},{3,2},{4,5},{5,4},{6,7},{7,6},{8,9},{9,8},{10,11... | collective-permute-start | bytes 196616 | tf_op jit(solution)/shard_map/ppermute | solution.py:355
  33.1 6.3 %collective-permute-start.9 = (bf16[4,4096]{1,0:T(4,128)(2,1)S(1)}, bf16[4,4096]{1,0:T(4,128)(2,1)S(1)}, u32[]{:S(2)}, u32[]{:S(2)}) collective-permute-start(bf16[4,4096]{1,0:T(4,128)(2,1)S(1)} %get-tuple-element.53), channel_id=1, source_target_pairs={{0,6},{1,7},{2,4},{3,5},{4,2},{5,3},{6,0},{7,1},{8,14},{9,15},{10,... | collective-permute-start | bytes 98312 | tf_op jit(solution)/shard_map/ppermute | solution.py:355
  35.8 3.9 %collective-permute-start.10 = (bf16[4,4096]{1,0:T(4,128)(2,1)S(1)}, bf16[4,4096]{1,0:T(4,128)(2,1)S(1)}, u32[]{:S(2)}, u32[]{:S(2)}) collective-permute-start(bf16[4,4096]{1,0:T(4,128)(2,1)S(1)} %get-tuple-element.54), channel_id=1, source_target_pairs={{0,4},{1,5},{2,6},{3,7},{4,0},{5,1},{6,2},{7,3},{8,12},{9,13},{10,... | collective-permute-start | bytes 98312 | tf_op jit(solution)/shard_map/ppermute | solution.py:355
  36.3 3.9 %collective-permute-start.11 = (bf16[4,4096]{1,0:T(4,128)(2,1)S(1)}, bf16[4,4096]{1,0:T(4,128)(2,1)S(1)}, u32[]{:S(2)}, u32[]{:S(2)}) collective-permute-start(bf16[4,4096]{1,0:T(4,128)(2,1)S(1)} %get-tuple-element.55), channel_id=1, source_target_pairs={{0,2},{1,3},{2,0},{3,1},{4,6},{5,7},{6,4},{7,5},{8,10},{9,11},{10,... | collective-permute-start | bytes 98312 | tf_op jit(solution)/shard_map/ppermute | solution.py:355

commit v5 on v4

--- a/solution.py
+++ b/solution.py
@@ -11,6 +11,7 @@
 BF16 = jnp.bfloat16
 LANES = 128
 EARLY = 3
+TURNED = 2
 LEAD = 4
 NT = (((1,), (1,)), ((), ()))
 TN = (((0,), (0,)), ((), ()))
@@ -66,6 +67,12 @@
         for e in range(first, last)
         for i, (source, target) in enumerate(zip(weights, held))
     ]
+
+
+def turn_block(source, target, part, parts):
+    size = source.shape[1] // parts
+    for at in range(part * size, (part + 1) * size, LANES):
+        target[at : at + LANES, :] = source[:, at : at + LANES].T
 
 
 def pack_kernel(*refs):
@@ -138,7 +145,7 @@
         for first in range(ready, experts, 2)
     ]
     downs = fetch_experts((down_hbm,), (down_w,), down_sems, 0, lead)
-    for copy in sum(batches[:2], []):
+    for copy in sum(batches[:2], []) + (downs if len(batches) < 3 else []):
         copy.start()
 
     first_expert = (lax.axis_index("expert") * experts).astype(F32)
@@ -177,10 +184,6 @@
         activations[here, :] = (swish * up_pre).astype(BF16)
         slope_ref[here, :] = up_pre * squash * (1.0 + gate_pre * (1.0 - squash))
         swish_ref[here, :] = swish
-    if len(batches) < 3:
-        for copy in downs:
-            copy.start()
-
     replica = lax.axis_index("dp")
     share = width // replicas
     turned = {
@@ -208,7 +211,7 @@
 
 def outputs_kernel(
     lead, activations, slope_ref, swish_ref, grads_ref, picker_ref, gain_ref, gate_w, up_w, unused, down_hbm,
-    keep_ref, send_one, send_two, down_w, results, backs, sems
+    keep_ref, send_one, send_two, down_w, results, backs, turned, sems
 ):
     experts, _, width = gate_w.shape
     half = keep_ref.shape[0]
@@ -217,26 +220,46 @@
     copies = fetch_experts((down_hbm,), (down_w,), sems, lead, experts)
     for copy in copies:
         copy.start()
-    def last_products(e):
-        here = slice(e * per_expert, (e + 1) * per_expert)
-        results[here, width:] = (
-            jnp.dot(backs[0, here, :], gate_w[e], preferred_element_type=F32)
-            + jnp.dot(backs[1, here, :], up_w[e], preferred_element_type=F32)
-        ).astype(BF16)
-
-    for e in range(experts):
+    def arrive(e):
         if e >= lead and (e - lead) % 2 == 0:
             for copy in copies[e - lead : e - lead + 2]:
                 copy.wait()
-        here = slice(e * per_expert, (e + 1) * per_expert)
-        act_grad = lax.dot_general(grads_ref[here, :], down_w[e], NT, preferred_element_type=F32)
-        backs[0, here, :] = (act_grad * slope_ref[here, :]).astype(BF16)
-        backs[1, here, :] = (act_grad * swish_ref[here, :]).astype(BF16)
-        forward = jnp.dot(activations[here, :], down_w[e], preferred_element_type=F32)
-        results[here, :width] = (forward.astype(BF16).astype(F32) * gain_ref[here, :]).astype(BF16)
+
+    def turn(e, part):
+        if e < experts:
+            turn_block(down_w.at[e], turned.at[e % TURNED], part, 4)
+
+    def place(e):
+        return slice(e * per_expert, (e + 1) * per_expert)
+
+    arrive(0)
+    for e in range(experts + 1):
+        arrive(e + 1)
+        turn(e + 1, 0)
+        if e < experts:
+            here = place(e)
+            if e > 0:
+                act_grad = jnp.dot(grads_ref[here, :], turned[e % TURNED], preferred_element_type=F32)
+            else:
+                act_grad = lax.dot_general(
+                    grads_ref[here, :], down_w[e], NT, preferred_element_type=F32
+                )
+            backs[0, here, :] = (act_grad * slope_ref[here, :]).astype(BF16)
+            backs[1, here, :] = (act_grad * swish_ref[here, :]).astype(BF16)
+        turn(e + 1, 1)
+        if e < experts:
+            forward = jnp.dot(activations[here, :], down_w[e], preferred_element_type=F32)
+            results[here, :width] = (
+                forward.astype(BF16).astype(F32) * gain_ref[here, :]
+            ).astype(BF16)
+        turn(e + 1, 2)
         if e > 0:
-            last_products(e - 1)
-    last_products(experts - 1)
+            there = place(e - 1)
+            back = jnp.dot(backs[0, there, :], gate_w[e - 1], preferred_element_type=F32)
+        turn(e + 1, 3)
+        if e > 0:
+            back = back + jnp.dot(backs[1, there, :], up_w[e - 1], preferred_element_type=F32)
+            results[there, width:] = back.astype(BF16)
 
     step = min(512, width)
     for at in range(0, 2 * width, step):
@@ -449,6 +472,7 @@
         scratch_shapes=[
             pltpu.VMEM((slots, 2 * width), BF16),
             pltpu.VMEM((2, slots, hidden), BF16),
+            pltpu.VMEM((TURNED, width, hidden), BF16),
             pltpu.SemaphoreType.DMA((experts, 1)),
         ],
         input_output_aliases={8: 3},

time: 41.2 us -> 40.3 us (0.978)
  Pallas kernels: 23 us -> 22.1 us
    pallas_call x1, Pallas kernels: 8.16 us -> 7.25 us  [shards(): pl.pallas_call(functools.partial(outputs_kernel, lead), out_shape=[half,...]
  transfers between devices with their start and end apart: 12 -> 12, of which waited for: 6 -> 6; matrix products, arithmetic and copies ran while one was open for 0% -> 0% of each run, Pallas kernels for 36% -> 34%
where the time goes in v5:
time: 40.3 us; the launch traced here: 40 us
  Pallas kernels  22.1 us (55%)
  starting transfers between devices  13.3 us (33%)
  waiting for transfers between devices  3.17 us (8%)
  between operations  0.73 us (2%)
  local copies, waits for them, and re-layouts  0.62 us (2%)
    ppermute x9, starting transfers between devices, swap(): lax.ppermute(values, both, [(i, i ^ distance) for i in range(devices)])  8.79 us
    pallas_call x1, Pallas kernels, shards(): pl.pallas_call(functools.partial(activations_kernel, (top, capacity, grou...  7.41 us
    pallas_call x1, Pallas kernels, shards(): pl.pallas_call(functools.partial(outputs_kernel, lead), out_shape=[half,...  7.25 us
    ppermute x3, starting transfers between devices, shards(): lax.ppermute(packs[k], 'dp', [(i, i ^ k) for i in range(replicas)])  4.53 us
    pallas_call x1, Pallas kernels, shards(): pl.pallas_call(functools.partial(fetch_kernel, ready), out_shape=[held] *...  3.64 us
    ppermute x9, waiting for transfers between devices, swap(): lax.ppermute(values, both, [(i, i ^ distance) for i in range(devices)])  3.16 us
    pallas_call x1, Pallas kernels, shards(): pl.pallas_call(functools.partial(grad_kernel, (top, capacity, groups, ten...  2.78 us
    pallas_call x1, Pallas kernels, shards(): pl.pallas_call(pack_kernel, out_shape=row, in_specs=hbm_specs(5), out_spe...  0.92 us
  transfers between devices with their start and end apart: 12, of which 6 were waited for; matrix products, arithmetic and copies ran while one was open for 0% of the time, Pallas kernels for 34%

profile of v5, /device:TPU:0, one launch (start us, length us, event | category | flops | bytes accessed | tf_op | source)
XLA Modules:
  0.0 40.0 jit_solution(5150787603152773027)
XLA Ops:
  0.6 0.9 %pack.1.refs_0_ = bf16[4,4224]{1,0:T(4,128)(2,1)S(1)} custom-call(bf16[4,2048]{1,0:T(4,128)(2,1)} %refs_0_.1, bf16[4,2048]{1,0:T(4,128)(2,1)} %refs_1_.1, s32[6,16]{1,0:T(8,128)} %bitcast.13, s32[6,16]{1,0:T(8,128)} %bitcast.14, f32[6,16]{1,0:T(8,128)} %bitcast.15), custom_call_target="tpu_custom_call" | custom-call | tf_op jit(solution)/shard_map/pack/pallas_call | solution.py:391
  1.6 4.0 %collective-permute-start.2 = (bf16[4,4224]{1,0:T(4,128)(2,1)S(1)}, bf16[4,4224]{1,0:T(4,128)(2,1)S(1)}, u32[]{:S(2)}, u32[]{:S(2)}) collective-permute-start(bf16[4,4224]{1,0:T(4,128)(2,1)S(1)} %pack.1.refs_0_), channel_id=1, source_target_pairs={{0,6},{1,7},{2,4},{3,5},{4,2},{5,3},{6,0},{7,1},{8,14},{9,15},{10,... | collective-permute-start | bytes 101384 | tf_op jit(solution)/shard_map/ppermute | solution.py:378
  5.5 0.5 %collective-permute-start.1 = (bf16[4,4224]{1,0:T(4,128)(2,1)S(1)}, bf16[4,4224]{1,0:T(4,128)(2,1)S(1)}, u32[]{:S(2)}, u32[]{:S(2)}) collective-permute-start(bf16[4,4224]{1,0:T(4,128)(2,1)S(1)} %pack.1.refs_0_), channel_id=1, source_target_pairs={{0,4},{1,5},{2,6},{3,7},{4,0},{5,1},{6,2},{7,3},{8,12},{9,13},{10,... | collective-permute-start | bytes 101384 | tf_op jit(solution)/shard_map/ppermute | solution.py:378
  6.0 0.1 collective-permute-start
  6.2 3.6 %fetch.1 = (bf16[8,352,2048]{2,1,0:T(8,128)(2,1)S(1)}, bf16[8,352,2048]{2,1,0:T(8,128)(2,1)S(1)}) custom-call(bf16[8,352,2048]{2,1,0:T(8,128)(2,1)} %bitcast.7, bf16[8,352,2048]{2,1,0:T(8,128)(2,1)} %bitcast.9), custom_call_target="tpu_custom_call" | custom-call | tf_op jit(solution)/shard_map/fetch/pallas_call | solution.py:405
  9.8 0.1 collective-permute-done.refs_1_
  10.0 0.1 collective-permute-start.3
  10.1 1.3 %collective-permute-done.3.far_ref = bf16[16,4224]{1,0:T(8,128)(2,1)S(1)} collective-permute-done((bf16[16,4224]{1,0:T(8,128)(2,1)S(1)}, bf16[16,4224]{1,0:T(8,128)(2,1)S(1)}, u32[]{:S(2)}, u32[]{:S(2)}) %collective-permute-start.3) | collective-permute-done | bytes 135200 | tf_op jit(solution)/shard_map/ppermute | solution.py:378
  11.4 7.4 %activations.1 = (bf16[8,352,2048]{2,1,0:T(8,128)(2,1)S(1)}, bf16[8,352,2048]{2,1,0:T(8,128)(2,1)S(1)}, bf16[8,352,2048]{2,1,0:T(8,128)(2,1)S(1)}, bf16[128,352]...) custom-call(bf16[16,4224]{1,0:T(8,128)(2,1)S(1)} %get-tuple-element., ...), custom_call_target="tpu_custom_call", output_to_operand_aliasing={{0}: (5, {}), {1}: (6, {})} | custom-call | flops 369098752 | bytes 23068672 | tf_op jit(solution)/shard_map/activations/pallas_call | solution.py:434
  18.8 1.9 %collective-permute-start.4 = (bf16[512,128]{1,0:T(8,128)(2,1)S(1)}, bf16[512,128]{1,0:T(8,128)(2,1)S(1)}, u32[]{:S(2)}, u32[]{:S(2)}) collective-permute-start(bf16[512,128]{1,0:T(8,128)(2,1)S(1)} %get-tuple-element.36), channel_id=1, source_target_pairs={{0,8},{8,0},{16,24},{24,16},{1,9},{9,1},{17,25},{25,17},{2,10},{10... | collective-permute-start | bytes 393224 | tf_op jit(solution)/shard_map/ppermute | solution.py:501
  20.8 2.6 %collective-permute-start.5 = (bf16[512,128]{1,0:T(8,128)(2,1)S(1)}, bf16[512,128]{1,0:T(8,128)(2,1)S(1)}, u32[]{:S(2)}, u32[]{:S(2)}) collective-permute-start(bf16[512,128]{1,0:T(8,128)(2,1)S(1)} %get-tuple-element.37), channel_id=1, source_target_pairs={{0,16},{8,24},{16,0},{24,8},{1,17},{9,25},{17,1},{25,9},{2,18},{10... | collective-permute-start | bytes 393224 | tf_op jit(solution)/shard_map/ppermute | solution.py:501
  23.4 7.3 %outputs.1 = (bf16[16,4096]{1,0:T(8,128)(2,1)S(1)}, bf16[16,2048]{1,0:T(8,128)(2,1)S(1)}, bf16[16,2048]{1,0:T(8,128)(2,1)S(1)}, bf16[8,352,2048]{2,1,0:T(8,128)(2,1)S(1)}) custom-call(bf16[128,352]{1,0:T(8,128)(2,1)S(1)} %get-tuple-element.39.activations, f32[128,352]{1,0:T(8,128)S(1)} %get-tuple-element.40.slope_ref, ...), custom_call_target="tpu_custom_call", output_to_operand_aliasing={{3}: (8, {})} | custom-call | flops 738197504 | bytes 34603008 | tf_op jit(solution)/shard_map/outputs/pallas_call | solution.py:467
  30.6 0.1 collective-permute-start.7
  30.7 0.5 %collective-permute-start.8 = (bf16[16,2048]{1,0:T(8,128)(2,1)S(1)}, bf16[16,2048]{1,0:T(8,128)(2,1)S(1)}, u32[]{:S(2)}, u32[]{:S(2)}) collective-permute-start(bf16[16,2048]{1,0:T(8,128)(2,1)S(1)} %get-tuple-element.50), channel_id=1, source_target_pairs={{0,1},{1,0},{2,3},{3,2},{4,5},{5,4},{6,7},{7,6},{8,9},{9,8},{10,11... | collective-permute-start | bytes 196616 | tf_op jit(solution)/shard_map/ppermute | solution.py:378
  31.2 0.7 %collective-permute-done.7.one_ref = bf16[16,2048]{1,0:T(8,128)(2,1)S(1)} collective-permute-done((bf16[16,2048]{1,0:T(8,128)(2,1)S(1)}, bf16[16,2048]{1,0:T(8,128)(2,1)S(1)}, u32[]{:S(2)}, u32[]{:S(2)}) %collective-permute-start.7) | collective-permute-done | bytes 65568 | tf_op jit(solution)/shard_map/ppermute | solution.py:378
  31.9 0.2 collective-permute-done.8.two_ref
  32.1 0.1 near.1
  32.2 2.7 %collective-permute-start.9 = (bf16[4,4096]{1,0:T(4,128)(2,1)S(1)}, bf16[4,4096]{1,0:T(4,128)(2,1)S(1)}, u32[]{:S(2)}, u32[]{:S(2)}) collective-permute-start(bf16[4,4096]{1,0:T(4,128)(2,1)S(1)} %get-tuple-element.53), channel_id=1, source_target_pairs={{0,6},{1,7},{2,4},{3,5},{4,2},{5,3},{6,0},{7,1},{8,14},{9,15},{10,... | collective-permute-start | bytes 98312 | tf_op jit(solution)/shard_map/ppermute | solution.py:378
  34.9 0.5 %collective-permute-start.10 = (bf16[4,4096]{1,0:T(4,128)(2,1)S(1)}, bf16[4,4096]{1,0:T(4,128)(2,1)S(1)}, u32[]{:S(2)}, u32[]{:S(2)}) collective-permute-start(bf16[4,4096]{1,0:T(4,128)(2,1)S(1)} %get-tuple-element.54), channel_id=1, source_target_pairs={{0,4},{1,5},{2,6},{3,7},{4,0},{5,1},{6,2},{7,3},{8,12},{9,13},{10,... | collective-permute-start | bytes 98312 | tf_op jit(solution)/shard_map/ppermute | solution.py:378
  35.4 0.3 collective-permute-start.11
  35.7 2.8 %grad_down.1 = (bf16[8,352,512]{2,1,0:T(8,128)(2,1)}, f32[4,4096]{1,0:T(4,128)S(1)}) custom-call(bf16[512,128]{1,0:T(8,128)(2,1)S(1)} %get-tuple-element.35.refs_0_, bf16[512,128]{1,0:T(8,128)(2,1)S(1)} %collective-permute-done.4.refs_1_, bf16[512,128]{1,0:T(8,128)(2,1)S(1)} %collective-permute-done.5.refs_2_, ...), custom_call_target="tpu_custom_call" | custom-call | flops 184549376 | bytes 2883584 | tf_op jit(solution)/shard_map/grad_down/pallas_call | solution.py:503
  38.5 0.3 collective-permute-done.10
  38.8 0.5 %collective-permute-done.11 = bf16[4,4096]{1,0:T(4,128)(2,1)S(1)} collective-permute-done((bf16[4,4096]{1,0:T(4,128)(2,1)S(1)}, bf16[4,4096]{1,0:T(4,128)(2,1)S(1)}, u32[]{:S(2)}, u32[]{:S(2)}) %collective-permute-start.11) | collective-permute-done | bytes 32800 | tf_op jit(solution)/shard_map/ppermute | solution.py:378
  39.4 0.6 %fusion = (bf16[4,2048]{1,0:T(4,128)(2,1)}, bf16[4,2048]{1,0:T(4,128)(2,1)}) fusion(bf16[4,4096]{1,0:T(4,128)(2,1)S(1)} %add_convert_fusion), kind=kLoop, calls=%fused_computation.1 | loop fusion | bytes 65536 | tf_op jit(solution)/shard_map/slice | solution.py:526
  (9 shorter events, 0.1 us)
Async XLA Ops:
  1.6 8.3 %collective-permute-start.2 = (bf16[4,4224]{1,0:T(4,128)(2,1)S(1)}, bf16[4,4224]{1,0:T(4,128)(2,1)S(1)}, u32[]{:S(2)}, u32[]{:S(2)}) collective-permute-start(bf16[4,4224]{1,0:T(4,128)(2,1)S(1)} %pack.1.refs_0_), channel_id=1, source_target_pairs={{0,6},{1,7},{2,4},{3,5},{4,2},{5,3},{6,0},{7,1},{8,14},{9,15},{10,... | collective-permute-start | bytes 101384 | tf_op jit(solution)/shard_map/ppermute | solution.py:378
  5.5 4.3 %collective-permute-start.1 = (bf16[4,4224]{1,0:T(4,128)(2,1)S(1)}, bf16[4,4224]{1,0:T(4,128)(2,1)S(1)}, u32[]{:S(2)}, u32[]{:S(2)}) collective-permute-start(bf16[4,4224]{1,0:T(4,128)(2,1)S(1)} %pack.1.refs_0_), channel_id=1, source_target_pairs={{0,4},{1,5},{2,6},{3,7},{4,0},{5,1},{6,2},{7,3},{8,12},{9,13},{10,... | collective-permute-start | bytes 101384 | tf_op jit(solution)/shard_map/ppermute | solution.py:378
  6.0 3.9 %collective-permute-start = (bf16[4,4224]{1,0:T(4,128)(2,1)S(1)}, bf16[4,4224]{1,0:T(4,128)(2,1)S(1)}, u32[]{:S(2)}, u32[]{:S(2)}) collective-permute-start(bf16[4,4224]{1,0:T(4,128)(2,1)S(1)} %pack.1.refs_0_), channel_id=1, source_target_pairs={{0,2},{1,3},{2,0},{3,1},{4,6},{5,7},{6,4},{7,5},{8,10},{9,11},{10,... | collective-permute-start | bytes 101384 | tf_op jit(solution)/shard_map/ppermute | solution.py:378
  10.0 1.4 %collective-permute-start.3 = (bf16[16,4224]{1,0:T(8,128)(2,1)S(1)}, bf16[16,4224]{1,0:T(8,128)(2,1)S(1)}, u32[]{:S(2)}, u32[]{:S(2)}) collective-permute-start(bf16[16,4224]{1,0:T(8,128)(2,1)S(1)} %get-tuple-element.32.x_ref), channel_id=1, source_target_pairs={{0,1},{1,0},{2,3},{3,2},{4,5},{5,4},{6,7},{7,6},{8,9},{9,8},{10,11... | collective-permute-start | bytes 405512 | tf_op jit(solution)/shard_map/ppermute | solution.py:378
  18.8 16.6 %collective-permute-start.4 = (bf16[512,128]{1,0:T(8,128)(2,1)S(1)}, bf16[512,128]{1,0:T(8,128)(2,1)S(1)}, u32[]{:S(2)}, u32[]{:S(2)}) collective-permute-start(bf16[512,128]{1,0:T(8,128)(2,1)S(1)} %get-tuple-element.36), channel_id=1, source_target_pairs={{0,8},{8,0},{16,24},{24,16},{1,9},{9,1},{17,25},{25,17},{2,10},{10... | collective-permute-start | bytes 393224 | tf_op jit(solution)/shard_map/ppermute | solution.py:501
  20.8 15.0 %collective-permute-start.5 = (bf16[512,128]{1,0:T(8,128)(2,1)S(1)}, bf16[512,128]{1,0:T(8,128)(2,1)S(1)}, u32[]{:S(2)}, u32[]{:S(2)}) collective-permute-start(bf16[512,128]{1,0:T(8,128)(2,1)S(1)} %get-tuple-element.37), channel_id=1, source_target_pairs={{0,16},{8,24},{16,0},{24,8},{1,17},{9,25},{17,1},{25,9},{2,18},{10... | collective-permute-start | bytes 393224 | tf_op jit(solution)/shard_map/ppermute | solution.py:501
  23.4 12.4 %collective-permute-start.6 = (bf16[512,128]{1,0:T(8,128)(2,1)S(1)}, bf16[512,128]{1,0:T(8,128)(2,1)S(1)}, u32[]{:S(2)}, u32[]{:S(2)}) collective-permute-start(bf16[512,128]{1,0:T(8,128)(2,1)S(1)} %get-tuple-element.38), channel_id=1, source_target_pairs={{0,24},{8,16},{16,8},{24,0},{1,25},{9,17},{17,9},{25,1},{2,26},{10... | collective-permute-start | bytes 393224 | tf_op jit(solution)/shard_map/ppermute | solution.py:501
  30.6 1.3 %collective-permute-start.7 = (bf16[16,2048]{1,0:T(8,128)(2,1)S(1)}, bf16[16,2048]{1,0:T(8,128)(2,1)S(1)}, u32[]{:S(2)}, u32[]{:S(2)}) collective-permute-start(bf16[16,2048]{1,0:T(8,128)(2,1)S(1)} %get-tuple-element.49), channel_id=1, source_target_pairs={{0,1},{1,0},{2,3},{3,2},{4,5},{5,4},{6,7},{7,6},{8,9},{9,8},{10,11... | collective-permute-start | bytes 196616 | tf_op jit(solution)/shard_map/ppermute | solution.py:378
  30.7 1.4 %collective-permute-start.8 = (bf16[16,2048]{1,0:T(8,128)(2,1)S(1)}, bf16[16,2048]{1,0:T(8,128)(2,1)S(1)}, u32[]{:S(2)}, u32[]{:S(2)}) collective-permute-start(bf16[16,2048]{1,0:T(8,128)(2,1)S(1)} %get-tuple-element.50), channel_id=1, source_target_pairs={{0,1},{1,0},{2,3},{3,2},{4,5},{5,4},{6,7},{7,6},{8,9},{9,8},{10,11... | collective-permute-start | bytes 196616 | tf_op jit(solution)/shard_map/ppermute | solution.py:378
  32.2 6.4 %collective-permute-start.9 = (bf16[4,4096]{1,0:T(4,128)(2,1)S(1)}, bf16[4,4096]{1,0:T(4,128)(2,1)S(1)}, u32[]{:S(2)}, u32[]{:S(2)}) collective-permute-start(bf16[4,4096]{1,0:T(4,128)(2,1)S(1)} %get-tuple-element.53), channel_id=1, source_target_pairs={{0,6},{1,7},{2,4},{3,5},{4,2},{5,3},{6,0},{7,1},{8,14},{9,15},{10,... | collective-permute-start | bytes 98312 | tf_op jit(solution)/shard_map/ppermute | solution.py:378
  34.9 3.9 %collective-permute-start.10 = (bf16[4,4096]{1,0:T(4,128)(2,1)S(1)}, bf16[4,4096]{1,0:T(4,128)(2,1)S(1)}, u32[]{:S(2)}, u32[]{:S(2)}) collective-permute-start(bf16[4,4096]{1,0:T(4,128)(2,1)S(1)} %get-tuple-element.54), channel_id=1, source_target_pairs={{0,4},{1,5},{2,6},{3,7},{4,0},{5,1},{6,2},{7,3},{8,12},{9,13},{10,... | collective-permute-start | bytes 98312 | tf_op jit(solution)/shard_map/ppermute | solution.py:378
  35.4 3.9 %collective-permute-start.11 = (bf16[4,4096]{1,0:T(4,128)(2,1)S(1)}, bf16[4,4096]{1,0:T(4,128)(2,1)S(1)}, u32[]{:S(2)}, u32[]{:S(2)}) collective-permute-start(bf16[4,4096]{1,0:T(4,128)(2,1)S(1)} %get-tuple-element.55), channel_id=1, source_target_pairs={{0,2},{1,3},{2,0},{3,1},{4,6},{5,7},{6,4},{7,5},{8,10},{9,11},{10,... | collective-permute-start | bytes 98312 | tf_op jit(solution)/shard_map/ppermute | solution.py:378

commit v6 on v5

--- a/solution.py
+++ b/solution.py
@@ -76,17 +76,10 @@
 
 
 def pack_kernel(*refs):
-    sources, out_ref = refs[:5], refs[5]
-    routes_ref, positions_ref, weights_ref, sems = refs[6:]
-    mine, width = sources[0].shape
+    sources, out_ref, targets, sems = refs[:5], refs[5], refs[6:11], refs[11]
+    tokens_ref, cotangent_ref, routes_ref, positions_ref, weights_ref = targets
+    mine, width = tokens_ref.shape
     top, group_size = routes_ref.shape
-    targets = (
-        out_ref.at[:, :width],
-        out_ref.at[:, width : 2 * width],
-        routes_ref,
-        positions_ref,
-        weights_ref,
-    )
     copies = [
         pltpu.make_async_copy(source, target, sems.at[i])
         for i, (source, target) in enumerate(zip(sources, targets))
@@ -107,6 +100,8 @@
     row = lax.broadcasted_iota(jnp.int32, (mine, group_size), 0)
     pick = jnp.where(column == row + first, 1.0, 0.0).astype(BF16)
     routing = lax.dot_general(pick, table, NT, preferred_element_type=F32)
+    out_ref[:, :width] = tokens_ref[...]
+    out_ref[:, width : 2 * width] = cotangent_ref[...]
     out_ref[:, 2 * width :] = jnp.concatenate(
         [routing, jnp.zeros((mine, LANES - 4 * top), F32)], axis=1
     ).astype(BF16)
@@ -157,17 +152,23 @@
     gain_ref[...] = gain
     picker_ref[...] = chosen.astype(BF16)
     step = min(512, width)
-    for at in range(0, 2 * width, step):
+    def fill(at):
         given = jnp.concatenate([x_ref[:, at : at + step], far_ref[:, at : at + step]], axis=0)
-        slot_rows = jnp.dot(scatter, given, preferred_element_type=F32)
-        if at < width:
-            filled[:, at : at + step] = slot_rows.astype(BF16)
-        else:
-            grads_ref[:, at - width : at - width + step] = (gain * slot_rows).astype(BF16)
+        return jnp.dot(scatter, given, preferred_element_type=F32)
+
+    def fill_grads(at):
+        grads_ref[:, at : at + step] = (gain * fill(width + at)).astype(BF16)
+
+    for at in range(0, width, step):
+        filled[:, at : at + step] = fill(at).astype(BF16)
+    unfilled = list(range(0, width, step))
 
     for e in range(experts):
         if e >= ready and (e - ready) % 2 == 0:
             at = (e - ready) // 2
+            for column in unfilled[:2]:
+                fill_grads(column)
+            unfilled = unfilled[2:]
             for copy in batches[at]:
                 copy.wait()
             for copy in batches[at + 2] if at + 2 < len(batches) else []:
@@ -394,6 +395,8 @@
         in_specs=hbm_specs(5),
         out_specs=vmem_specs(1)[0],
         scratch_shapes=[
+            pltpu.VMEM((mine, width), BF16),
+            pltpu.VMEM((mine, width), BF16),
             pltpu.VMEM((top, group_size), jnp.int32),
             pltpu.VMEM((top, group_size), jnp.int32),
             pltpu.VMEM((top, group_size), F32),

time: 40.3 us -> 40.2 us (level)
  no operation moved by 1% of the time
where the time goes in v6:
time: 40.2 us; the launch traced here: 39.9 us
  Pallas kernels  22 us (55%)
  starting transfers between devices  13.3 us (33%)
  waiting for transfers between devices  3.18 us (8%)
  between operations  0.73 us (2%)
  local copies, waits for them, and re-layouts  0.62 us (2%)
    ppermute x9, starting transfers between devices, swap(): lax.ppermute(values, both, [(i, i ^ distance) for i in range(devices)])  8.79 us
    pallas_call x1, Pallas kernels, shards(): pl.pallas_call(functools.partial(activations_kernel, (top, capacity, grou...  7.32 us
    pallas_call x1, Pallas kernels, shards(): pl.pallas_call(functools.partial(outputs_kernel, lead), out_shape=[half,...  7.25 us
    ppermute x3, starting transfers between devices, shards(): lax.ppermute(packs[k], 'dp', [(i, i ^ k) for i in range(replicas)])  4.53 us
    pallas_call x1, Pallas kernels, shards(): pl.pallas_call(functools.partial(fetch_kernel, ready), out_shape=[held] *...  3.64 us
    ppermute x9, waiting for transfers between devices, swap(): lax.ppermute(values, both, [(i, i ^ distance) for i in range(devices)])  3.17 us
    pallas_call x1, Pallas kernels, shards(): pl.pallas_call(functools.partial(grad_kernel, (top, capacity, groups, ten...  2.78 us
    pallas_call x1, Pallas kernels, shards(): pl.pallas_call(pack_kernel, out_shape=row, in_specs=hbm_specs(5), out_spe...  0.92 us
  transfers between devices with their start and end apart: 12, of which 6 were waited for; matrix products, arithmetic and copies ran while one was open for 0% of the time, Pallas kernels for 34%

profile of v6, /device:TPU:0, one launch (start us, length us, event | category | flops | bytes accessed | tf_op | source)
XLA Modules:
  0.0 39.9 jit_solution(7000924460706445022)
XLA Ops:
  0.6 0.9 %pack.1.refs_0_ = bf16[4,4224]{1,0:T(4,128)(2,1)S(1)} custom-call(bf16[4,2048]{1,0:T(4,128)(2,1)} %refs_0_.1, bf16[4,2048]{1,0:T(4,128)(2,1)} %refs_1_.1, s32[6,16]{1,0:T(8,128)} %bitcast.13, s32[6,16]{1,0:T(8,128)} %bitcast.14, f32[6,16]{1,0:T(8,128)} %bitcast.15), custom_call_target="tpu_custom_call" | custom-call | tf_op jit(solution)/shard_map/pack/pallas_call | solution.py:392
  1.6 4.0 %collective-permute-start.2 = (bf16[4,4224]{1,0:T(4,128)(2,1)S(1)}, bf16[4,4224]{1,0:T(4,128)(2,1)S(1)}, u32[]{:S(2)}, u32[]{:S(2)}) collective-permute-start(bf16[4,4224]{1,0:T(4,128)(2,1)S(1)} %pack.1.refs_0_), channel_id=1, source_target_pairs={{0,6},{1,7},{2,4},{3,5},{4,2},{5,3},{6,0},{7,1},{8,14},{9,15},{10,... | collective-permute-start | bytes 101384 | tf_op jit(solution)/shard_map/ppermute | solution.py:379
  5.5 0.5 %collective-permute-start.1 = (bf16[4,4224]{1,0:T(4,128)(2,1)S(1)}, bf16[4,4224]{1,0:T(4,128)(2,1)S(1)}, u32[]{:S(2)}, u32[]{:S(2)}) collective-permute-start(bf16[4,4224]{1,0:T(4,128)(2,1)S(1)} %pack.1.refs_0_), channel_id=1, source_target_pairs={{0,4},{1,5},{2,6},{3,7},{4,0},{5,1},{6,2},{7,3},{8,12},{9,13},{10,... | collective-permute-start | bytes 101384 | tf_op jit(solution)/shard_map/ppermute | solution.py:379
  6.0 0.1 collective-permute-start
  6.2 3.6 %fetch.1 = (bf16[8,352,2048]{2,1,0:T(8,128)(2,1)S(1)}, bf16[8,352,2048]{2,1,0:T(8,128)(2,1)S(1)}) custom-call(bf16[8,352,2048]{2,1,0:T(8,128)(2,1)} %bitcast.7, bf16[8,352,2048]{2,1,0:T(8,128)(2,1)} %bitcast.9), custom_call_target="tpu_custom_call" | custom-call | tf_op jit(solution)/shard_map/fetch/pallas_call | solution.py:408
  9.8 0.1 collective-permute-done.refs_1_
  10.0 0.1 collective-permute-start.3
  10.1 1.3 %collective-permute-done.3.far_ref = bf16[16,4224]{1,0:T(8,128)(2,1)S(1)} collective-permute-done((bf16[16,4224]{1,0:T(8,128)(2,1)S(1)}, bf16[16,4224]{1,0:T(8,128)(2,1)S(1)}, u32[]{:S(2)}, u32[]{:S(2)}) %collective-permute-start.3) | collective-permute-done | bytes 135200 | tf_op jit(solution)/shard_map/ppermute | solution.py:379
  11.4 7.3 %activations.1 = (bf16[8,352,2048]{2,1,0:T(8,128)(2,1)S(1)}, bf16[8,352,2048]{2,1,0:T(8,128)(2,1)S(1)}, bf16[8,352,2048]{2,1,0:T(8,128)(2,1)S(1)}, bf16[128,352]...) custom-call(bf16[16,4224]{1,0:T(8,128)(2,1)S(1)} %get-tuple-element., ...), custom_call_target="tpu_custom_call", output_to_operand_aliasing={{0}: (5, {}), {1}: (6, {})} | custom-call | flops 369098752 | bytes 23068672 | tf_op jit(solution)/shard_map/activations/pallas_call | solution.py:437
  18.8 1.9 %collective-permute-start.4 = (bf16[512,128]{1,0:T(8,128)(2,1)S(1)}, bf16[512,128]{1,0:T(8,128)(2,1)S(1)}, u32[]{:S(2)}, u32[]{:S(2)}) collective-permute-start(bf16[512,128]{1,0:T(8,128)(2,1)S(1)} %get-tuple-element.36), channel_id=1, source_target_pairs={{0,8},{8,0},{16,24},{24,16},{1,9},{9,1},{17,25},{25,17},{2,10},{10... | collective-permute-start | bytes 393224 | tf_op jit(solution)/shard_map/ppermute | solution.py:504
  20.7 2.6 %collective-permute-start.5 = (bf16[512,128]{1,0:T(8,128)(2,1)S(1)}, bf16[512,128]{1,0:T(8,128)(2,1)S(1)}, u32[]{:S(2)}, u32[]{:S(2)}) collective-permute-start(bf16[512,128]{1,0:T(8,128)(2,1)S(1)} %get-tuple-element.37), channel_id=1, source_target_pairs={{0,16},{8,24},{16,0},{24,8},{1,17},{9,25},{17,1},{25,9},{2,18},{10... | collective-permute-start | bytes 393224 | tf_op jit(solution)/shard_map/ppermute | solution.py:504
  23.3 7.3 %outputs.1 = (bf16[16,4096]{1,0:T(8,128)(2,1)S(1)}, bf16[16,2048]{1,0:T(8,128)(2,1)S(1)}, bf16[16,2048]{1,0:T(8,128)(2,1)S(1)}, bf16[8,352,2048]{2,1,0:T(8,128)(2,1)S(1)}) custom-call(bf16[128,352]{1,0:T(8,128)(2,1)S(1)} %get-tuple-element.39.activations, f32[128,352]{1,0:T(8,128)S(1)} %get-tuple-element.40.slope_ref, ...), custom_call_target="tpu_custom_call", output_to_operand_aliasing={{3}: (8, {})} | custom-call | flops 738197504 | bytes 34603008 | tf_op jit(solution)/shard_map/outputs/pallas_call | solution.py:470
  30.5 0.1 collective-permute-start.7
  30.6 0.5 %collective-permute-start.8 = (bf16[16,2048]{1,0:T(8,128)(2,1)S(1)}, bf16[16,2048]{1,0:T(8,128)(2,1)S(1)}, u32[]{:S(2)}, u32[]{:S(2)}) collective-permute-start(bf16[16,2048]{1,0:T(8,128)(2,1)S(1)} %get-tuple-element.50), channel_id=1, source_target_pairs={{0,1},{1,0},{2,3},{3,2},{4,5},{5,4},{6,7},{7,6},{8,9},{9,8},{10,11... | collective-permute-start | bytes 196616 | tf_op jit(solution)/shard_map/ppermute | solution.py:379
  31.1 0.7 %collective-permute-done.7.one_ref = bf16[16,2048]{1,0:T(8,128)(2,1)S(1)} collective-permute-done((bf16[16,2048]{1,0:T(8,128)(2,1)S(1)}, bf16[16,2048]{1,0:T(8,128)(2,1)S(1)}, u32[]{:S(2)}, u32[]{:S(2)}) %collective-permute-start.7) | collective-permute-done | bytes 65568 | tf_op jit(solution)/shard_map/ppermute | solution.py:379
  31.9 0.2 collective-permute-done.8.two_ref
  32.0 0.1 near.1
  32.1 2.7 %collective-permute-start.9 = (bf16[4,4096]{1,0:T(4,128)(2,1)S(1)}, bf16[4,4096]{1,0:T(4,128)(2,1)S(1)}, u32[]{:S(2)}, u32[]{:S(2)}) collective-permute-start(bf16[4,4096]{1,0:T(4,128)(2,1)S(1)} %get-tuple-element.53), channel_id=1, source_target_pairs={{0,6},{1,7},{2,4},{3,5},{4,2},{5,3},{6,0},{7,1},{8,14},{9,15},{10,... | collective-permute-start | bytes 98312 | tf_op jit(solution)/shard_map/ppermute | solution.py:379
  34.8 0.5 %collective-permute-start.10 = (bf16[4,4096]{1,0:T(4,128)(2,1)S(1)}, bf16[4,4096]{1,0:T(4,128)(2,1)S(1)}, u32[]{:S(2)}, u32[]{:S(2)}) collective-permute-start(bf16[4,4096]{1,0:T(4,128)(2,1)S(1)} %get-tuple-element.54), channel_id=1, source_target_pairs={{0,4},{1,5},{2,6},{3,7},{4,0},{5,1},{6,2},{7,3},{8,12},{9,13},{10,... | collective-permute-start | bytes 98312 | tf_op jit(solution)/shard_map/ppermute | solution.py:379
  35.4 0.3 collective-permute-start.11
  35.7 2.8 %grad_down.1 = (bf16[8,352,512]{2,1,0:T(8,128)(2,1)}, f32[4,4096]{1,0:T(4,128)S(1)}) custom-call(bf16[512,128]{1,0:T(8,128)(2,1)S(1)} %get-tuple-element.35.refs_0_, bf16[512,128]{1,0:T(8,128)(2,1)S(1)} %collective-permute-done.4.refs_1_, bf16[512,128]{1,0:T(8,128)(2,1)S(1)} %collective-permute-done.5.refs_2_, ...), custom_call_target="tpu_custom_call" | custom-call | flops 184549376 | bytes 2883584 | tf_op jit(solution)/shard_map/grad_down/pallas_call | solution.py:506
  38.5 0.3 collective-permute-done.10
  38.8 0.5 %collective-permute-done.11 = bf16[4,4096]{1,0:T(4,128)(2,1)S(1)} collective-permute-done((bf16[4,4096]{1,0:T(4,128)(2,1)S(1)}, bf16[4,4096]{1,0:T(4,128)(2,1)S(1)}, u32[]{:S(2)}, u32[]{:S(2)}) %collective-permute-start.11) | collective-permute-done | bytes 32800 | tf_op jit(solution)/shard_map/ppermute | solution.py:379
  39.3 0.6 %fusion = (bf16[4,2048]{1,0:T(4,128)(2,1)}, bf16[4,2048]{1,0:T(4,128)(2,1)}) fusion(bf16[4,4096]{1,0:T(4,128)(2,1)S(1)} %add_convert_fusion), kind=kLoop, calls=%fused_computation.1 | loop fusion | bytes 65536 | tf_op jit(solution)/shard_map/slice | solution.py:529
  (9 shorter events, 0.1 us)
Async XLA Ops:
  1.6 8.3 %collective-permute-start.2 = (bf16[4,4224]{1,0:T(4,128)(2,1)S(1)}, bf16[4,4224]{1,0:T(4,128)(2,1)S(1)}, u32[]{:S(2)}, u32[]{:S(2)}) collective-permute-start(bf16[4,4224]{1,0:T(4,128)(2,1)S(1)} %pack.1.refs_0_), channel_id=1, source_target_pairs={{0,6},{1,7},{2,4},{3,5},{4,2},{5,3},{6,0},{7,1},{8,14},{9,15},{10,... | collective-permute-start | bytes 101384 | tf_op jit(solution)/shard_map/ppermute | solution.py:379
  5.5 4.3 %collective-permute-start.1 = (bf16[4,4224]{1,0:T(4,128)(2,1)S(1)}, bf16[4,4224]{1,0:T(4,128)(2,1)S(1)}, u32[]{:S(2)}, u32[]{:S(2)}) collective-permute-start(bf16[4,4224]{1,0:T(4,128)(2,1)S(1)} %pack.1.refs_0_), channel_id=1, source_target_pairs={{0,4},{1,5},{2,6},{3,7},{4,0},{5,1},{6,2},{7,3},{8,12},{9,13},{10,... | collective-permute-start | bytes 101384 | tf_op jit(solution)/shard_map/ppermute | solution.py:379
  6.0 3.9 %collective-permute-start = (bf16[4,4224]{1,0:T(4,128)(2,1)S(1)}, bf16[4,4224]{1,0:T(4,128)(2,1)S(1)}, u32[]{:S(2)}, u32[]{:S(2)}) collective-permute-start(bf16[4,4224]{1,0:T(4,128)(2,1)S(1)} %pack.1.refs_0_), channel_id=1, source_target_pairs={{0,2},{1,3},{2,0},{3,1},{4,6},{5,7},{6,4},{7,5},{8,10},{9,11},{10,... | collective-permute-start | bytes 101384 | tf_op jit(solution)/shard_map/ppermute | solution.py:379
  10.0 1.4 %collective-permute-start.3 = (bf16[16,4224]{1,0:T(8,128)(2,1)S(1)}, bf16[16,4224]{1,0:T(8,128)(2,1)S(1)}, u32[]{:S(2)}, u32[]{:S(2)}) collective-permute-start(bf16[16,4224]{1,0:T(8,128)(2,1)S(1)} %get-tuple-element.32.x_ref), channel_id=1, source_target_pairs={{0,1},{1,0},{2,3},{3,2},{4,5},{5,4},{6,7},{7,6},{8,9},{9,8},{10,11... | collective-permute-start | bytes 405512 | tf_op jit(solution)/shard_map/ppermute | solution.py:379
  18.8 16.6 %collective-permute-start.4 = (bf16[512,128]{1,0:T(8,128)(2,1)S(1)}, bf16[512,128]{1,0:T(8,128)(2,1)S(1)}, u32[]{:S(2)}, u32[]{:S(2)}) collective-permute-start(bf16[512,128]{1,0:T(8,128)(2,1)S(1)} %get-tuple-element.36), channel_id=1, source_target_pairs={{0,8},{8,0},{16,24},{24,16},{1,9},{9,1},{17,25},{25,17},{2,10},{10... | collective-permute-start | bytes 393224 | tf_op jit(solution)/shard_map/ppermute | solution.py:504
  20.7 15.0 %collective-permute-start.5 = (bf16[512,128]{1,0:T(8,128)(2,1)S(1)}, bf16[512,128]{1,0:T(8,128)(2,1)S(1)}, u32[]{:S(2)}, u32[]{:S(2)}) collective-permute-start(bf16[512,128]{1,0:T(8,128)(2,1)S(1)} %get-tuple-element.37), channel_id=1, source_target_pairs={{0,16},{8,24},{16,0},{24,8},{1,17},{9,25},{17,1},{25,9},{2,18},{10... | collective-permute-start | bytes 393224 | tf_op jit(solution)/shard_map/ppermute | solution.py:504
  23.3 12.4 %collective-permute-start.6 = (bf16[512,128]{1,0:T(8,128)(2,1)S(1)}, bf16[512,128]{1,0:T(8,128)(2,1)S(1)}, u32[]{:S(2)}, u32[]{:S(2)}) collective-permute-start(bf16[512,128]{1,0:T(8,128)(2,1)S(1)} %get-tuple-element.38), channel_id=1, source_target_pairs={{0,24},{8,16},{16,8},{24,0},{1,25},{9,17},{17,9},{25,1},{2,26},{10... | collective-permute-start | bytes 393224 | tf_op jit(solution)/shard_map/ppermute | solution.py:504
  30.5 1.3 %collective-permute-start.7 = (bf16[16,2048]{1,0:T(8,128)(2,1)S(1)}, bf16[16,2048]{1,0:T(8,128)(2,1)S(1)}, u32[]{:S(2)}, u32[]{:S(2)}) collective-permute-start(bf16[16,2048]{1,0:T(8,128)(2,1)S(1)} %get-tuple-element.49), channel_id=1, source_target_pairs={{0,1},{1,0},{2,3},{3,2},{4,5},{5,4},{6,7},{7,6},{8,9},{9,8},{10,11... | collective-permute-start | bytes 196616 | tf_op jit(solution)/shard_map/ppermute | solution.py:379
  30.6 1.4 %collective-permute-start.8 = (bf16[16,2048]{1,0:T(8,128)(2,1)S(1)}, bf16[16,2048]{1,0:T(8,128)(2,1)S(1)}, u32[]{:S(2)}, u32[]{:S(2)}) collective-permute-start(bf16[16,2048]{1,0:T(8,128)(2,1)S(1)} %get-tuple-element.50), channel_id=1, source_target_pairs={{0,1},{1,0},{2,3},{3,2},{4,5},{5,4},{6,7},{7,6},{8,9},{9,8},{10,11... | collective-permute-start | bytes 196616 | tf_op jit(solution)/shard_map/ppermute | solution.py:379
  32.1 6.4 %collective-permute-start.9 = (bf16[4,4096]{1,0:T(4,128)(2,1)S(1)}, bf16[4,4096]{1,0:T(4,128)(2,1)S(1)}, u32[]{:S(2)}, u32[]{:S(2)}) collective-permute-start(bf16[4,4096]{1,0:T(4,128)(2,1)S(1)} %get-tuple-element.53), channel_id=1, source_target_pairs={{0,6},{1,7},{2,4},{3,5},{4,2},{5,3},{6,0},{7,1},{8,14},{9,15},{10,... | collective-permute-start | bytes 98312 | tf_op jit(solution)/shard_map/ppermute | solution.py:379
  34.8 3.9 %collective-permute-start.10 = (bf16[4,4096]{1,0:T(4,128)(2,1)S(1)}, bf16[4,4096]{1,0:T(4,128)(2,1)S(1)}, u32[]{:S(2)}, u32[]{:S(2)}) collective-permute-start(bf16[4,4096]{1,0:T(4,128)(2,1)S(1)} %get-tuple-element.54), channel_id=1, source_target_pairs={{0,4},{1,5},{2,6},{3,7},{4,0},{5,1},{6,2},{7,3},{8,12},{9,13},{10,... | collective-permute-start | bytes 98312 | tf_op jit(solution)/shard_map/ppermute | solution.py:379
  35.4 3.9 %collective-permute-start.11 = (bf16[4,4096]{1,0:T(4,128)(2,1)S(1)}, bf16[4,4096]{1,0:T(4,128)(2,1)S(1)}, u32[]{:S(2)}, u32[]{:S(2)}) collective-permute-start(bf16[4,4096]{1,0:T(4,128)(2,1)S(1)} %get-tuple-element.55), channel_id=1, source_target_pairs={{0,2},{1,3},{2,0},{3,1},{4,6},{5,7},{6,4},{7,5},{8,10},{9,11},{10,... | collective-permute-start | bytes 98312 | tf_op jit(solution)/shard_map/ppermute | solution.py:379

commit v7 on v6

--- a/solution.py
+++ b/solution.py
@@ -84,9 +84,9 @@
         pltpu.make_async_copy(source, target, sems.at[i])
         for i, (source, target) in enumerate(zip(sources, targets))
     ]
-    for copy in copies:
+    for copy in copies[2:] + copies[:2]:
         copy.start()
-    for copy in copies:
+    for copy in copies[2:]:
         copy.wait()
     weights = weights_ref[...]
     high = weights.astype(BF16)
@@ -100,11 +100,13 @@
     row = lax.broadcasted_iota(jnp.int32, (mine, group_size), 0)
     pick = jnp.where(column == row + first, 1.0, 0.0).astype(BF16)
     routing = lax.dot_general(pick, table, NT, preferred_element_type=F32)
-    out_ref[:, :width] = tokens_ref[...]
-    out_ref[:, width : 2 * width] = cotangent_ref[...]
     out_ref[:, 2 * width :] = jnp.concatenate(
         [routing, jnp.zeros((mine, LANES - 4 * top), F32)], axis=1
     ).astype(BF16)
+    for copy in copies[:2]:
+        copy.wait()
+    out_ref[:, :width] = tokens_ref[...]
+    out_ref[:, width : 2 * width] = cotangent_ref[...]
 
 
 def join_kernel(*refs):
@@ -500,7 +502,7 @@
     received = [swap(part, 2 * k) for k, part in enumerate(others_near, 1)]
 
     arrived = [packs[0]]
-    for k in range(1, replicas):
+    for k in [*range(2, replicas), 1]:
         arrived.append(lax.ppermute(packs[k], "dp", [(i, i ^ k) for i in range(replicas)]))
     share = width // replicas
     grad, total = pl.pallas_call(

time: 40.2 us -> 39.9 us (level)
  transfers between devices with their start and end apart: 12 -> 12, of which waited for: 6 -> 6; matrix products, arithmetic and copies ran while one was open for 0% -> 0% of each run, Pallas kernels for 34% -> 35%
where the time goes in v7:
time: 39.9 us; the launch traced here: 39.7 us
  Pallas kernels  22 us (55%)
  starting transfers between devices  13.3 us (33%)
  waiting for transfers between devices  2.96 us (7%)
  between operations  0.73 us (2%)
  local copies, waits for them, and re-layouts  0.62 us (2%)
    ppermute x9, starting transfers between devices, swap(): lax.ppermute(values, both, [(i, i ^ distance) for i in range(devices)])  8.79 us
    pallas_call x1, Pallas kernels, shards(): pl.pallas_call(functools.partial(activations_kernel, (top, capacity, grou...  7.33 us
    pallas_call x1, Pallas kernels, shards(): pl.pallas_call(functools.partial(outputs_kernel, lead), out_shape=[half,...  7.25 us
    ppermute x3, starting transfers between devices, shards(): lax.ppermute(packs[k], 'dp', [(i, i ^ k) for i in range(replicas)])  4.53 us
    pallas_call x1, Pallas kernels, shards(): pl.pallas_call(functools.partial(fetch_kernel, ready), out_shape=[held] *...  3.64 us
    ppermute x9, waiting for transfers between devices, swap(): lax.ppermute(values, both, [(i, i ^ distance) for i in range(devices)])  2.95 us
    pallas_call x1, Pallas kernels, shards(): pl.pallas_call(functools.partial(grad_kernel, (top, capacity, groups, ten...  2.78 us
    pallas_call x1, Pallas kernels, shards(): pl.pallas_call(pack_kernel, out_shape=row, in_specs=hbm_specs(5), out_spe...  0.9 us
  transfers between devices with their start and end apart: 12, of which 6 were waited for; matrix products, arithmetic and copies ran while one was open for 0% of the time, Pallas kernels for 35%

profile of v7, /device:TPU:0, one launch (start us, length us, event | category | flops | bytes accessed | tf_op | source)
XLA Modules:
  0.0 39.7 jit_solution(9968239811388482324)
XLA Ops:
  0.6 0.9 %pack.1.refs_0_ = bf16[4,4224]{1,0:T(4,128)(2,1)S(1)} custom-call(bf16[4,2048]{1,0:T(4,128)(2,1)} %refs_0_.1, bf16[4,2048]{1,0:T(4,128)(2,1)} %refs_1_.1, s32[6,16]{1,0:T(8,128)} %bitcast.13, s32[6,16]{1,0:T(8,128)} %bitcast.14, f32[6,16]{1,0:T(8,128)} %bitcast.15), custom_call_target="tpu_custom_call" | custom-call | tf_op jit(solution)/shard_map/pack/pallas_call | solution.py:394
  1.5 4.0 %collective-permute-start.2 = (bf16[4,4224]{1,0:T(4,128)(2,1)S(1)}, bf16[4,4224]{1,0:T(4,128)(2,1)S(1)}, u32[]{:S(2)}, u32[]{:S(2)}) collective-permute-start(bf16[4,4224]{1,0:T(4,128)(2,1)S(1)} %pack.1.refs_0_), channel_id=1, source_target_pairs={{0,6},{1,7},{2,4},{3,5},{4,2},{5,3},{6,0},{7,1},{8,14},{9,15},{10,... | collective-permute-start | bytes 101384 | tf_op jit(solution)/shard_map/ppermute | solution.py:381
  5.5 0.5 %collective-permute-start.1 = (bf16[4,4224]{1,0:T(4,128)(2,1)S(1)}, bf16[4,4224]{1,0:T(4,128)(2,1)S(1)}, u32[]{:S(2)}, u32[]{:S(2)}) collective-permute-start(bf16[4,4224]{1,0:T(4,128)(2,1)S(1)} %pack.1.refs_0_), channel_id=1, source_target_pairs={{0,4},{1,5},{2,6},{3,7},{4,0},{5,1},{6,2},{7,3},{8,12},{9,13},{10,... | collective-permute-start | bytes 101384 | tf_op jit(solution)/shard_map/ppermute | solution.py:381
  6.0 0.1 collective-permute-start
  6.1 3.6 %fetch.1 = (bf16[8,352,2048]{2,1,0:T(8,128)(2,1)S(1)}, bf16[8,352,2048]{2,1,0:T(8,128)(2,1)S(1)}) custom-call(bf16[8,352,2048]{2,1,0:T(8,128)(2,1)} %bitcast.7, bf16[8,352,2048]{2,1,0:T(8,128)(2,1)} %bitcast.9), custom_call_target="tpu_custom_call" | custom-call | tf_op jit(solution)/shard_map/fetch/pallas_call | solution.py:410
  9.8 0.1 collective-permute-done.refs_1_
  10.0 0.1 collective-permute-start.3
  10.0 1.3 %collective-permute-done.3.far_ref = bf16[16,4224]{1,0:T(8,128)(2,1)S(1)} collective-permute-done((bf16[16,4224]{1,0:T(8,128)(2,1)S(1)}, bf16[16,4224]{1,0:T(8,128)(2,1)S(1)}, u32[]{:S(2)}, u32[]{:S(2)}) %collective-permute-start.3) | collective-permute-done | bytes 135200 | tf_op jit(solution)/shard_map/ppermute | solution.py:381
  11.4 7.3 %activations.1 = (bf16[8,352,2048]{2,1,0:T(8,128)(2,1)S(1)}, bf16[8,352,2048]{2,1,0:T(8,128)(2,1)S(1)}, bf16[8,352,2048]{2,1,0:T(8,128)(2,1)S(1)}, bf16[128,352]...) custom-call(bf16[16,4224]{1,0:T(8,128)(2,1)S(1)} %get-tuple-element., ...), custom_call_target="tpu_custom_call", output_to_operand_aliasing={{0}: (5, {}), {1}: (6, {})} | custom-call | flops 369098752 | bytes 23068672 | tf_op jit(solution)/shard_map/activations/pallas_call | solution.py:439
  18.7 3.0 %collective-permute-start.4 = (bf16[512,128]{1,0:T(8,128)(2,1)S(1)}, bf16[512,128]{1,0:T(8,128)(2,1)S(1)}, u32[]{:S(2)}, u32[]{:S(2)}) collective-permute-start(bf16[512,128]{1,0:T(8,128)(2,1)S(1)} %get-tuple-element.36), channel_id=1, source_target_pairs={{0,16},{8,24},{16,0},{24,8},{1,17},{9,25},{17,1},{25,9},{2,18},{10... | collective-permute-start | bytes 393224 | tf_op jit(solution)/shard_map/ppermute | solution.py:506
  21.7 1.3 %collective-permute-start.5 = (bf16[512,128]{1,0:T(8,128)(2,1)S(1)}, bf16[512,128]{1,0:T(8,128)(2,1)S(1)}, u32[]{:S(2)}, u32[]{:S(2)}) collective-permute-start(bf16[512,128]{1,0:T(8,128)(2,1)S(1)} %get-tuple-element.37), channel_id=1, source_target_pairs={{0,24},{8,16},{16,8},{24,0},{1,25},{9,17},{17,9},{25,1},{2,26},{10... | collective-permute-start | bytes 393224 | tf_op jit(solution)/shard_map/ppermute | solution.py:506
  23.0 0.2 collective-permute-start.6
  23.3 7.3 %outputs.1 = (bf16[16,4096]{1,0:T(8,128)(2,1)S(1)}, bf16[16,2048]{1,0:T(8,128)(2,1)S(1)}, bf16[16,2048]{1,0:T(8,128)(2,1)S(1)}, bf16[8,352,2048]{2,1,0:T(8,128)(2,1)S(1)}) custom-call(bf16[128,352]{1,0:T(8,128)(2,1)S(1)} %get-tuple-element.39.activations, f32[128,352]{1,0:T(8,128)S(1)} %get-tuple-element.40.slope_ref, ...), custom_call_target="tpu_custom_call", output_to_operand_aliasing={{3}: (8, {})} | custom-call | flops 738197504 | bytes 34603008 | tf_op jit(solution)/shard_map/outputs/pallas_call | solution.py:472
  30.5 0.1 collective-permute-start.7
  30.6 0.5 %collective-permute-start.8 = (bf16[16,2048]{1,0:T(8,128)(2,1)S(1)}, bf16[16,2048]{1,0:T(8,128)(2,1)S(1)}, u32[]{:S(2)}, u32[]{:S(2)}) collective-permute-start(bf16[16,2048]{1,0:T(8,128)(2,1)S(1)} %get-tuple-element.50), channel_id=1, source_target_pairs={{0,1},{1,0},{2,3},{3,2},{4,5},{5,4},{6,7},{7,6},{8,9},{9,8},{10,11... | collective-permute-start | bytes 196616 | tf_op jit(solution)/shard_map/ppermute | solution.py:381
  31.1 0.7 %collective-permute-done.7.one_ref = bf16[16,2048]{1,0:T(8,128)(2,1)S(1)} collective-permute-done((bf16[16,2048]{1,0:T(8,128)(2,1)S(1)}, bf16[16,2048]{1,0:T(8,128)(2,1)S(1)}, u32[]{:S(2)}, u32[]{:S(2)}) %collective-permute-start.7) | collective-permute-done | bytes 65568 | tf_op jit(solution)/shard_map/ppermute | solution.py:381
  31.8 0.2 collective-permute-done.8.two_ref
  32.0 0.1 near.1
  32.1 2.5 %collective-permute-start.9 = (bf16[4,4096]{1,0:T(4,128)(2,1)S(1)}, bf16[4,4096]{1,0:T(4,128)(2,1)S(1)}, u32[]{:S(2)}, u32[]{:S(2)}) collective-permute-start(bf16[4,4096]{1,0:T(4,128)(2,1)S(1)} %get-tuple-element.53), channel_id=1, source_target_pairs={{0,6},{1,7},{2,4},{3,5},{4,2},{5,3},{6,0},{7,1},{8,14},{9,15},{10,... | collective-permute-start | bytes 98312 | tf_op jit(solution)/shard_map/ppermute | solution.py:381
  34.6 0.5 %collective-permute-start.10 = (bf16[4,4096]{1,0:T(4,128)(2,1)S(1)}, bf16[4,4096]{1,0:T(4,128)(2,1)S(1)}, u32[]{:S(2)}, u32[]{:S(2)}) collective-permute-start(bf16[4,4096]{1,0:T(4,128)(2,1)S(1)} %get-tuple-element.54), channel_id=1, source_target_pairs={{0,4},{1,5},{2,6},{3,7},{4,0},{5,1},{6,2},{7,3},{8,12},{9,13},{10,... | collective-permute-start | bytes 98312 | tf_op jit(solution)/shard_map/ppermute | solution.py:381
  35.1 0.5 %collective-permute-start.11 = (bf16[4,4096]{1,0:T(4,128)(2,1)S(1)}, bf16[4,4096]{1,0:T(4,128)(2,1)S(1)}, u32[]{:S(2)}, u32[]{:S(2)}) collective-permute-start(bf16[4,4096]{1,0:T(4,128)(2,1)S(1)} %get-tuple-element.55), channel_id=1, source_target_pairs={{0,2},{1,3},{2,0},{3,1},{4,6},{5,7},{6,4},{7,5},{8,10},{9,11},{10,... | collective-permute-start | bytes 98312 | tf_op jit(solution)/shard_map/ppermute | solution.py:381
  35.6 2.8 %grad_down.1 = (bf16[8,352,512]{2,1,0:T(8,128)(2,1)}, f32[4,4096]{1,0:T(4,128)S(1)}) custom-call(bf16[512,128]{1,0:T(8,128)(2,1)S(1)} %get-tuple-element.35.refs_0_, bf16[512,128]{1,0:T(8,128)(2,1)S(1)} %collective-permute-done.4.refs_1_, bf16[512,128]{1,0:T(8,128)(2,1)S(1)} %collective-permute-done.5.refs_2_, ...), custom_call_target="tpu_custom_call" | custom-call | flops 184549376 | bytes 2883584 | tf_op jit(solution)/shard_map/grad_down/pallas_call | solution.py:508
  38.5 0.5 %collective-permute-done.11 = bf16[4,4096]{1,0:T(4,128)(2,1)S(1)} collective-permute-done((bf16[4,4096]{1,0:T(4,128)(2,1)S(1)}, bf16[4,4096]{1,0:T(4,128)(2,1)S(1)}, u32[]{:S(2)}, u32[]{:S(2)}) %collective-permute-start.11) | collective-permute-done | bytes 32800 | tf_op jit(solution)/shard_map/ppermute | solution.py:381
  39.1 0.6 %fusion = (bf16[4,2048]{1,0:T(4,128)(2,1)}, bf16[4,2048]{1,0:T(4,128)(2,1)}) fusion(bf16[4,4096]{1,0:T(4,128)(2,1)S(1)} %add_convert_fusion), kind=kLoop, calls=%fused_computation.1 | loop fusion | bytes 65536 | tf_op jit(solution)/shard_map/slice | solution.py:531
  (9 shorter events, 0.2 us)
Async XLA Ops:
  1.5 8.3 %collective-permute-start.2 = (bf16[4,4224]{1,0:T(4,128)(2,1)S(1)}, bf16[4,4224]{1,0:T(4,128)(2,1)S(1)}, u32[]{:S(2)}, u32[]{:S(2)}) collective-permute-start(bf16[4,4224]{1,0:T(4,128)(2,1)S(1)} %pack.1.refs_0_), channel_id=1, source_target_pairs={{0,6},{1,7},{2,4},{3,5},{4,2},{5,3},{6,0},{7,1},{8,14},{9,15},{10,... | collective-permute-start | bytes 101384 | tf_op jit(solution)/shard_map/ppermute | solution.py:381
  5.5 4.3 %collective-permute-start.1 = (bf16[4,4224]{1,0:T(4,128)(2,1)S(1)}, bf16[4,4224]{1,0:T(4,128)(2,1)S(1)}, u32[]{:S(2)}, u32[]{:S(2)}) collective-permute-start(bf16[4,4224]{1,0:T(4,128)(2,1)S(1)} %pack.1.refs_0_), channel_id=1, source_target_pairs={{0,4},{1,5},{2,6},{3,7},{4,0},{5,1},{6,2},{7,3},{8,12},{9,13},{10,... | collective-permute-start | bytes 101384 | tf_op jit(solution)/shard_map/ppermute | solution.py:381
  6.0 3.9 %collective-permute-start = (bf16[4,4224]{1,0:T(4,128)(2,1)S(1)}, bf16[4,4224]{1,0:T(4,128)(2,1)S(1)}, u32[]{:S(2)}, u32[]{:S(2)}) collective-permute-start(bf16[4,4224]{1,0:T(4,128)(2,1)S(1)} %pack.1.refs_0_), channel_id=1, source_target_pairs={{0,2},{1,3},{2,0},{3,1},{4,6},{5,7},{6,4},{7,5},{8,10},{9,11},{10,... | collective-permute-start | bytes 101384 | tf_op jit(solution)/shard_map/ppermute | solution.py:381
  10.0 1.4 %collective-permute-start.3 = (bf16[16,4224]{1,0:T(8,128)(2,1)S(1)}, bf16[16,4224]{1,0:T(8,128)(2,1)S(1)}, u32[]{:S(2)}, u32[]{:S(2)}) collective-permute-start(bf16[16,4224]{1,0:T(8,128)(2,1)S(1)} %get-tuple-element.32.x_ref), channel_id=1, source_target_pairs={{0,1},{1,0},{2,3},{3,2},{4,5},{5,4},{6,7},{7,6},{8,9},{9,8},{10,11... | collective-permute-start | bytes 405512 | tf_op jit(solution)/shard_map/ppermute | solution.py:381
  18.7 16.4 %collective-permute-start.4 = (bf16[512,128]{1,0:T(8,128)(2,1)S(1)}, bf16[512,128]{1,0:T(8,128)(2,1)S(1)}, u32[]{:S(2)}, u32[]{:S(2)}) collective-permute-start(bf16[512,128]{1,0:T(8,128)(2,1)S(1)} %get-tuple-element.36), channel_id=1, source_target_pairs={{0,16},{8,24},{16,0},{24,8},{1,17},{9,25},{17,1},{25,9},{2,18},{10... | collective-permute-start | bytes 393224 | tf_op jit(solution)/shard_map/ppermute | solution.py:506
  21.7 14.0 %collective-permute-start.5 = (bf16[512,128]{1,0:T(8,128)(2,1)S(1)}, bf16[512,128]{1,0:T(8,128)(2,1)S(1)}, u32[]{:S(2)}, u32[]{:S(2)}) collective-permute-start(bf16[512,128]{1,0:T(8,128)(2,1)S(1)} %get-tuple-element.37), channel_id=1, source_target_pairs={{0,24},{8,16},{16,8},{24,0},{1,25},{9,17},{17,9},{25,1},{2,26},{10... | collective-permute-start | bytes 393224 | tf_op jit(solution)/shard_map/ppermute | solution.py:506
  23.0 12.6 %collective-permute-start.6 = (bf16[512,128]{1,0:T(8,128)(2,1)S(1)}, bf16[512,128]{1,0:T(8,128)(2,1)S(1)}, u32[]{:S(2)}, u32[]{:S(2)}) collective-permute-start(bf16[512,128]{1,0:T(8,128)(2,1)S(1)} %get-tuple-element.38), channel_id=1, source_target_pairs={{0,8},{8,0},{16,24},{24,16},{1,9},{9,1},{17,25},{25,17},{2,10},{10... | collective-permute-start | bytes 393224 | tf_op jit(solution)/shard_map/ppermute | solution.py:506
  30.5 1.3 %collective-permute-start.7 = (bf16[16,2048]{1,0:T(8,128)(2,1)S(1)}, bf16[16,2048]{1,0:T(8,128)(2,1)S(1)}, u32[]{:S(2)}, u32[]{:S(2)}) collective-permute-start(bf16[16,2048]{1,0:T(8,128)(2,1)S(1)} %get-tuple-element.49), channel_id=1, source_target_pairs={{0,1},{1,0},{2,3},{3,2},{4,5},{5,4},{6,7},{7,6},{8,9},{9,8},{10,11... | collective-permute-start | bytes 196616 | tf_op jit(solution)/shard_map/ppermute | solution.py:381
  30.6 1.4 %collective-permute-start.8 = (bf16[16,2048]{1,0:T(8,128)(2,1)S(1)}, bf16[16,2048]{1,0:T(8,128)(2,1)S(1)}, u32[]{:S(2)}, u32[]{:S(2)}) collective-permute-start(bf16[16,2048]{1,0:T(8,128)(2,1)S(1)} %get-tuple-element.50), channel_id=1, source_target_pairs={{0,1},{1,0},{2,3},{3,2},{4,5},{5,4},{6,7},{7,6},{8,9},{9,8},{10,11... | collective-permute-start | bytes 196616 | tf_op jit(solution)/shard_map/ppermute | solution.py:381
  32.1 6.4 %collective-permute-start.9 = (bf16[4,4096]{1,0:T(4,128)(2,1)S(1)}, bf16[4,4096]{1,0:T(4,128)(2,1)S(1)}, u32[]{:S(2)}, u32[]{:S(2)}) collective-permute-start(bf16[4,4096]{1,0:T(4,128)(2,1)S(1)} %get-tuple-element.53), channel_id=1, source_target_pairs={{0,6},{1,7},{2,4},{3,5},{4,2},{5,3},{6,0},{7,1},{8,14},{9,15},{10,... | collective-permute-start | bytes 98312 | tf_op jit(solution)/shard_map/ppermute | solution.py:381
  34.6 3.9 %collective-permute-start.10 = (bf16[4,4096]{1,0:T(4,128)(2,1)S(1)}, bf16[4,4096]{1,0:T(4,128)(2,1)S(1)}, u32[]{:S(2)}, u32[]{:S(2)}) collective-permute-start(bf16[4,4096]{1,0:T(4,128)(2,1)S(1)} %get-tuple-element.54), channel_id=1, source_target_pairs={{0,4},{1,5},{2,6},{3,7},{4,0},{5,1},{6,2},{7,3},{8,12},{9,13},{10,... | collective-permute-start | bytes 98312 | tf_op jit(solution)/shard_map/ppermute | solution.py:381
  35.1 3.9 %collective-permute-start.11 = (bf16[4,4096]{1,0:T(4,128)(2,1)S(1)}, bf16[4,4096]{1,0:T(4,128)(2,1)S(1)}, u32[]{:S(2)}, u32[]{:S(2)}) collective-permute-start(bf16[4,4096]{1,0:T(4,128)(2,1)S(1)} %get-tuple-element.55), channel_id=1, source_target_pairs={{0,2},{1,3},{2,0},{3,1},{4,6},{5,7},{6,4},{7,5},{8,10},{9,11},{10,... | collective-permute-start | bytes 98312 | tf_op jit(solution)/shard_map/ppermute | solution.py:381

commit v8 on v7

--- a/solution.py
+++ b/solution.py
@@ -527,7 +527,7 @@
         ),
         name="grad_down",
     )(*arrived, own)
-    total = (total + sum(part.astype(F32) for part in received[::-1])).astype(BF16)
+    total = (total + sum(part.astype(F32) for part in received[-1:] + received[:-1])).astype(BF16)
     return (total[:, :width], total[:, width:], jnp.swapaxes(grad, 1, 2))
 
 

time: 39.9 us -> 39.9 us (level)
  no operation moved by 1% of the time
where the time goes in v8:
time: 39.9 us; the launch traced here: 39.7 us
  Pallas kernels  22 us (55%)
  starting transfers between devices  13.3 us (33%)
  waiting for transfers between devices  2.99 us (7%)
  between operations  0.73 us (2%)
  local copies, waits for them, and re-layouts  0.62 us (2%)
    ppermute x9, starting transfers between devices, swap(): lax.ppermute(values, both, [(i, i ^ distance) for i in range(devices)])  8.79 us
    pallas_call x1, Pallas kernels, shards(): pl.pallas_call(functools.partial(activations_kernel, (top, capacity, grou...  7.33 us
    pallas_call x1, Pallas kernels, shards(): pl.pallas_call(functools.partial(outputs_kernel, lead), out_shape=[half,...  7.25 us
    ppermute x3, starting transfers between devices, shards(): lax.ppermute(packs[k], 'dp', [(i, i ^ k) for i in range(replicas)])  4.53 us
    pallas_call x1, Pallas kernels, shards(): pl.pallas_call(functools.partial(fetch_kernel, ready), out_shape=[held] *...  3.64 us
    ppermute x9, waiting for transfers between devices, swap(): lax.ppermute(values, both, [(i, i ^ distance) for i in range(devices)])  2.98 us
    pallas_call x1, Pallas kernels, shards(): pl.pallas_call(functools.partial(grad_kernel, (top, capacity, groups, ten...  2.78 us
    pallas_call x1, Pallas kernels, shards(): pl.pallas_call(pack_kernel, out_shape=row, in_specs=hbm_specs(5), out_spe...  0.9 us
  transfers between devices with their start and end apart: 12, of which 6 were waited for; matrix products, arithmetic and copies ran while one was open for 0% of the time, Pallas kernels for 35%

profile of v8, /device:TPU:0, one launch (start us, length us, event | category | flops | bytes accessed | tf_op | source)
XLA Modules:
  0.0 39.7 jit_solution(17243140884119048333)
XLA Ops:
  0.6 0.9 %pack.1.refs_0_ = bf16[4,4224]{1,0:T(4,128)(2,1)S(1)} custom-call(bf16[4,2048]{1,0:T(4,128)(2,1)} %refs_0_.1, bf16[4,2048]{1,0:T(4,128)(2,1)} %refs_1_.1, s32[6,16]{1,0:T(8,128)} %bitcast.13, s32[6,16]{1,0:T(8,128)} %bitcast.14, f32[6,16]{1,0:T(8,128)} %bitcast.15), custom_call_target="tpu_custom_call" | custom-call | tf_op jit(solution)/shard_map/pack/pallas_call | solution.py:394
  1.5 4.0 %collective-permute-start.2 = (bf16[4,4224]{1,0:T(4,128)(2,1)S(1)}, bf16[4,4224]{1,0:T(4,128)(2,1)S(1)}, u32[]{:S(2)}, u32[]{:S(2)}) collective-permute-start(bf16[4,4224]{1,0:T(4,128)(2,1)S(1)} %pack.1.refs_0_), channel_id=1, source_target_pairs={{0,6},{1,7},{2,4},{3,5},{4,2},{5,3},{6,0},{7,1},{8,14},{9,15},{10,... | collective-permute-start | bytes 101384 | tf_op jit(solution)/shard_map/ppermute | solution.py:381
  5.5 0.5 %collective-permute-start.1 = (bf16[4,4224]{1,0:T(4,128)(2,1)S(1)}, bf16[4,4224]{1,0:T(4,128)(2,1)S(1)}, u32[]{:S(2)}, u32[]{:S(2)}) collective-permute-start(bf16[4,4224]{1,0:T(4,128)(2,1)S(1)} %pack.1.refs_0_), channel_id=1, source_target_pairs={{0,4},{1,5},{2,6},{3,7},{4,0},{5,1},{6,2},{7,3},{8,12},{9,13},{10,... | collective-permute-start | bytes 101384 | tf_op jit(solution)/shard_map/ppermute | solution.py:381
  6.0 0.1 collective-permute-start
  6.1 3.6 %fetch.1 = (bf16[8,352,2048]{2,1,0:T(8,128)(2,1)S(1)}, bf16[8,352,2048]{2,1,0:T(8,128)(2,1)S(1)}) custom-call(bf16[8,352,2048]{2,1,0:T(8,128)(2,1)} %bitcast.7, bf16[8,352,2048]{2,1,0:T(8,128)(2,1)} %bitcast.9), custom_call_target="tpu_custom_call" | custom-call | tf_op jit(solution)/shard_map/fetch/pallas_call | solution.py:410
  9.8 0.1 collective-permute-done.refs_1_
  10.0 0.1 collective-permute-start.3
  10.0 1.3 %collective-permute-done.3.far_ref = bf16[16,4224]{1,0:T(8,128)(2,1)S(1)} collective-permute-done((bf16[16,4224]{1,0:T(8,128)(2,1)S(1)}, bf16[16,4224]{1,0:T(8,128)(2,1)S(1)}, u32[]{:S(2)}, u32[]{:S(2)}) %collective-permute-start.3) | collective-permute-done | bytes 135200 | tf_op jit(solution)/shard_map/ppermute | solution.py:381
  11.4 7.3 %activations.1 = (bf16[8,352,2048]{2,1,0:T(8,128)(2,1)S(1)}, bf16[8,352,2048]{2,1,0:T(8,128)(2,1)S(1)}, bf16[8,352,2048]{2,1,0:T(8,128)(2,1)S(1)}, bf16[128,352]...) custom-call(bf16[16,4224]{1,0:T(8,128)(2,1)S(1)} %get-tuple-element., ...), custom_call_target="tpu_custom_call", output_to_operand_aliasing={{0}: (5, {}), {1}: (6, {})} | custom-call | flops 369098752 | bytes 23068672 | tf_op jit(solution)/shard_map/activations/pallas_call | solution.py:439
  18.7 3.0 %collective-permute-start.4 = (bf16[512,128]{1,0:T(8,128)(2,1)S(1)}, bf16[512,128]{1,0:T(8,128)(2,1)S(1)}, u32[]{:S(2)}, u32[]{:S(2)}) collective-permute-start(bf16[512,128]{1,0:T(8,128)(2,1)S(1)} %get-tuple-element.36), channel_id=1, source_target_pairs={{0,16},{8,24},{16,0},{24,8},{1,17},{9,25},{17,1},{25,9},{2,18},{10... | collective-permute-start | bytes 393224 | tf_op jit(solution)/shard_map/ppermute | solution.py:506
  21.7 1.3 %collective-permute-start.5 = (bf16[512,128]{1,0:T(8,128)(2,1)S(1)}, bf16[512,128]{1,0:T(8,128)(2,1)S(1)}, u32[]{:S(2)}, u32[]{:S(2)}) collective-permute-start(bf16[512,128]{1,0:T(8,128)(2,1)S(1)} %get-tuple-element.37), channel_id=1, source_target_pairs={{0,24},{8,16},{16,8},{24,0},{1,25},{9,17},{17,9},{25,1},{2,26},{10... | collective-permute-start | bytes 393224 | tf_op jit(solution)/shard_map/ppermute | solution.py:506
  23.0 0.2 collective-permute-start.6
  23.3 7.3 %outputs.1 = (bf16[16,4096]{1,0:T(8,128)(2,1)S(1)}, bf16[16,2048]{1,0:T(8,128)(2,1)S(1)}, bf16[16,2048]{1,0:T(8,128)(2,1)S(1)}, bf16[8,352,2048]{2,1,0:T(8,128)(2,1)S(1)}) custom-call(bf16[128,352]{1,0:T(8,128)(2,1)S(1)} %get-tuple-element.39.activations, f32[128,352]{1,0:T(8,128)S(1)} %get-tuple-element.40.slope_ref, ...), custom_call_target="tpu_custom_call", output_to_operand_aliasing={{3}: (8, {})} | custom-call | flops 738197504 | bytes 34603008 | tf_op jit(solution)/shard_map/outputs/pallas_call | solution.py:472
  30.5 0.1 collective-permute-start.7
  30.6 0.5 %collective-permute-start.8 = (bf16[16,2048]{1,0:T(8,128)(2,1)S(1)}, bf16[16,2048]{1,0:T(8,128)(2,1)S(1)}, u32[]{:S(2)}, u32[]{:S(2)}) collective-permute-start(bf16[16,2048]{1,0:T(8,128)(2,1)S(1)} %get-tuple-element.50), channel_id=1, source_target_pairs={{0,1},{1,0},{2,3},{3,2},{4,5},{5,4},{6,7},{7,6},{8,9},{9,8},{10,11... | collective-permute-start | bytes 196616 | tf_op jit(solution)/shard_map/ppermute | solution.py:381
  31.1 0.7 %collective-permute-done.7.one_ref = bf16[16,2048]{1,0:T(8,128)(2,1)S(1)} collective-permute-done((bf16[16,2048]{1,0:T(8,128)(2,1)S(1)}, bf16[16,2048]{1,0:T(8,128)(2,1)S(1)}, u32[]{:S(2)}, u32[]{:S(2)}) %collective-permute-start.7) | collective-permute-done | bytes 65568 | tf_op jit(solution)/shard_map/ppermute | solution.py:381
  31.8 0.2 collective-permute-done.8.two_ref
  32.0 0.1 near.1
  32.1 2.5 %collective-permute-start.9 = (bf16[4,4096]{1,0:T(4,128)(2,1)S(1)}, bf16[4,4096]{1,0:T(4,128)(2,1)S(1)}, u32[]{:S(2)}, u32[]{:S(2)}) collective-permute-start(bf16[4,4096]{1,0:T(4,128)(2,1)S(1)} %get-tuple-element.53), channel_id=1, source_target_pairs={{0,6},{1,7},{2,4},{3,5},{4,2},{5,3},{6,0},{7,1},{8,14},{9,15},{10,... | collective-permute-start | bytes 98312 | tf_op jit(solution)/shard_map/ppermute | solution.py:381
  34.6 0.5 %collective-permute-start.10 = (bf16[4,4096]{1,0:T(4,128)(2,1)S(1)}, bf16[4,4096]{1,0:T(4,128)(2,1)S(1)}, u32[]{:S(2)}, u32[]{:S(2)}) collective-permute-start(bf16[4,4096]{1,0:T(4,128)(2,1)S(1)} %get-tuple-element.54), channel_id=1, source_target_pairs={{0,2},{1,3},{2,0},{3,1},{4,6},{5,7},{6,4},{7,5},{8,10},{9,11},{10,... | collective-permute-start | bytes 98312 | tf_op jit(solution)/shard_map/ppermute | solution.py:381
  35.1 0.5 %collective-permute-start.11 = (bf16[4,4096]{1,0:T(4,128)(2,1)S(1)}, bf16[4,4096]{1,0:T(4,128)(2,1)S(1)}, u32[]{:S(2)}, u32[]{:S(2)}) collective-permute-start(bf16[4,4096]{1,0:T(4,128)(2,1)S(1)} %get-tuple-element.55), channel_id=1, source_target_pairs={{0,4},{1,5},{2,6},{3,7},{4,0},{5,1},{6,2},{7,3},{8,12},{9,13},{10,... | collective-permute-start | bytes 98312 | tf_op jit(solution)/shard_map/ppermute | solution.py:381
  35.6 2.8 %grad_down.1 = (bf16[8,352,512]{2,1,0:T(8,128)(2,1)}, f32[4,4096]{1,0:T(4,128)S(1)}) custom-call(bf16[512,128]{1,0:T(8,128)(2,1)S(1)} %get-tuple-element.35.refs_0_, bf16[512,128]{1,0:T(8,128)(2,1)S(1)} %collective-permute-done.4.refs_1_, bf16[512,128]{1,0:T(8,128)(2,1)S(1)} %collective-permute-done.5.refs_2_, ...), custom_call_target="tpu_custom_call" | custom-call | flops 184549376 | bytes 2883584 | tf_op jit(solution)/shard_map/grad_down/pallas_call | solution.py:508
  38.5 0.5 %collective-permute-done.11 = bf16[4,4096]{1,0:T(4,128)(2,1)S(1)} collective-permute-done((bf16[4,4096]{1,0:T(4,128)(2,1)S(1)}, bf16[4,4096]{1,0:T(4,128)(2,1)S(1)}, u32[]{:S(2)}, u32[]{:S(2)}) %collective-permute-start.11) | collective-permute-done | bytes 32800 | tf_op jit(solution)/shard_map/ppermute | solution.py:381
  39.1 0.6 %fusion = (bf16[4,2048]{1,0:T(4,128)(2,1)}, bf16[4,2048]{1,0:T(4,128)(2,1)}) fusion(bf16[4,4096]{1,0:T(4,128)(2,1)S(1)} %add_convert_fusion), kind=kLoop, calls=%fused_computation.1 | loop fusion | bytes 65536 | tf_op jit(solution)/shard_map/slice | solution.py:531
  (9 shorter events, 0.2 us)
Async XLA Ops:
  1.5 8.3 %collective-permute-start.2 = (bf16[4,4224]{1,0:T(4,128)(2,1)S(1)}, bf16[4,4224]{1,0:T(4,128)(2,1)S(1)}, u32[]{:S(2)}, u32[]{:S(2)}) collective-permute-start(bf16[4,4224]{1,0:T(4,128)(2,1)S(1)} %pack.1.refs_0_), channel_id=1, source_target_pairs={{0,6},{1,7},{2,4},{3,5},{4,2},{5,3},{6,0},{7,1},{8,14},{9,15},{10,... | collective-permute-start | bytes 101384 | tf_op jit(solution)/shard_map/ppermute | solution.py:381
  5.5 4.3 %collective-permute-start.1 = (bf16[4,4224]{1,0:T(4,128)(2,1)S(1)}, bf16[4,4224]{1,0:T(4,128)(2,1)S(1)}, u32[]{:S(2)}, u32[]{:S(2)}) collective-permute-start(bf16[4,4224]{1,0:T(4,128)(2,1)S(1)} %pack.1.refs_0_), channel_id=1, source_target_pairs={{0,4},{1,5},{2,6},{3,7},{4,0},{5,1},{6,2},{7,3},{8,12},{9,13},{10,... | collective-permute-start | bytes 101384 | tf_op jit(solution)/shard_map/ppermute | solution.py:381
  6.0 3.9 %collective-permute-start = (bf16[4,4224]{1,0:T(4,128)(2,1)S(1)}, bf16[4,4224]{1,0:T(4,128)(2,1)S(1)}, u32[]{:S(2)}, u32[]{:S(2)}) collective-permute-start(bf16[4,4224]{1,0:T(4,128)(2,1)S(1)} %pack.1.refs_0_), channel_id=1, source_target_pairs={{0,2},{1,3},{2,0},{3,1},{4,6},{5,7},{6,4},{7,5},{8,10},{9,11},{10,... | collective-permute-start | bytes 101384 | tf_op jit(solution)/shard_map/ppermute | solution.py:381
  10.0 1.4 %collective-permute-start.3 = (bf16[16,4224]{1,0:T(8,128)(2,1)S(1)}, bf16[16,4224]{1,0:T(8,128)(2,1)S(1)}, u32[]{:S(2)}, u32[]{:S(2)}) collective-permute-start(bf16[16,4224]{1,0:T(8,128)(2,1)S(1)} %get-tuple-element.32.x_ref), channel_id=1, source_target_pairs={{0,1},{1,0},{2,3},{3,2},{4,5},{5,4},{6,7},{7,6},{8,9},{9,8},{10,11... | collective-permute-start | bytes 405512 | tf_op jit(solution)/shard_map/ppermute | solution.py:381
  18.7 16.4 %collective-permute-start.4 = (bf16[512,128]{1,0:T(8,128)(2,1)S(1)}, bf16[512,128]{1,0:T(8,128)(2,1)S(1)}, u32[]{:S(2)}, u32[]{:S(2)}) collective-permute-start(bf16[512,128]{1,0:T(8,128)(2,1)S(1)} %get-tuple-element.36), channel_id=1, source_target_pairs={{0,16},{8,24},{16,0},{24,8},{1,17},{9,25},{17,1},{25,9},{2,18},{10... | collective-permute-start | bytes 393224 | tf_op jit(solution)/shard_map/ppermute | solution.py:506
  21.7 14.0 %collective-permute-start.5 = (bf16[512,128]{1,0:T(8,128)(2,1)S(1)}, bf16[512,128]{1,0:T(8,128)(2,1)S(1)}, u32[]{:S(2)}, u32[]{:S(2)}) collective-permute-start(bf16[512,128]{1,0:T(8,128)(2,1)S(1)} %get-tuple-element.37), channel_id=1, source_target_pairs={{0,24},{8,16},{16,8},{24,0},{1,25},{9,17},{17,9},{25,1},{2,26},{10... | collective-permute-start | bytes 393224 | tf_op jit(solution)/shard_map/ppermute | solution.py:506
  23.0 12.6 %collective-permute-start.6 = (bf16[512,128]{1,0:T(8,128)(2,1)S(1)}, bf16[512,128]{1,0:T(8,128)(2,1)S(1)}, u32[]{:S(2)}, u32[]{:S(2)}) collective-permute-start(bf16[512,128]{1,0:T(8,128)(2,1)S(1)} %get-tuple-element.38), channel_id=1, source_target_pairs={{0,8},{8,0},{16,24},{24,16},{1,9},{9,1},{17,25},{25,17},{2,10},{10... | collective-permute-start | bytes 393224 | tf_op jit(solution)/shard_map/ppermute | solution.py:506
  30.5 1.3 %collective-permute-start.7 = (bf16[16,2048]{1,0:T(8,128)(2,1)S(1)}, bf16[16,2048]{1,0:T(8,128)(2,1)S(1)}, u32[]{:S(2)}, u32[]{:S(2)}) collective-permute-start(bf16[16,2048]{1,0:T(8,128)(2,1)S(1)} %get-tuple-element.49), channel_id=1, source_target_pairs={{0,1},{1,0},{2,3},{3,2},{4,5},{5,4},{6,7},{7,6},{8,9},{9,8},{10,11... | collective-permute-start | bytes 196616 | tf_op jit(solution)/shard_map/ppermute | solution.py:381
  30.6 1.4 %collective-permute-start.8 = (bf16[16,2048]{1,0:T(8,128)(2,1)S(1)}, bf16[16,2048]{1,0:T(8,128)(2,1)S(1)}, u32[]{:S(2)}, u32[]{:S(2)}) collective-permute-start(bf16[16,2048]{1,0:T(8,128)(2,1)S(1)} %get-tuple-element.50), channel_id=1, source_target_pairs={{0,1},{1,0},{2,3},{3,2},{4,5},{5,4},{6,7},{7,6},{8,9},{9,8},{10,11... | collective-permute-start | bytes 196616 | tf_op jit(solution)/shard_map/ppermute | solution.py:381
  32.1 6.4 %collective-permute-start.9 = (bf16[4,4096]{1,0:T(4,128)(2,1)S(1)}, bf16[4,4096]{1,0:T(4,128)(2,1)S(1)}, u32[]{:S(2)}, u32[]{:S(2)}) collective-permute-start(bf16[4,4096]{1,0:T(4,128)(2,1)S(1)} %get-tuple-element.53), channel_id=1, source_target_pairs={{0,6},{1,7},{2,4},{3,5},{4,2},{5,3},{6,0},{7,1},{8,14},{9,15},{10,... | collective-permute-start | bytes 98312 | tf_op jit(solution)/shard_map/ppermute | solution.py:381
  34.6 3.9 %collective-permute-start.10 = (bf16[4,4096]{1,0:T(4,128)(2,1)S(1)}, bf16[4,4096]{1,0:T(4,128)(2,1)S(1)}, u32[]{:S(2)}, u32[]{:S(2)}) collective-permute-start(bf16[4,4096]{1,0:T(4,128)(2,1)S(1)} %get-tuple-element.54), channel_id=1, source_target_pairs={{0,2},{1,3},{2,0},{3,1},{4,6},{5,7},{6,4},{7,5},{8,10},{9,11},{10,... | collective-permute-start | bytes 98312 | tf_op jit(solution)/shard_map/ppermute | solution.py:381
  35.1 3.9 %collective-permute-start.11 = (bf16[4,4096]{1,0:T(4,128)(2,1)S(1)}, bf16[4,4096]{1,0:T(4,128)(2,1)S(1)}, u32[]{:S(2)}, u32[]{:S(2)}) collective-permute-start(bf16[4,4096]{1,0:T(4,128)(2,1)S(1)} %get-tuple-element.55), channel_id=1, source_target_pairs={{0,4},{1,5},{2,6},{3,7},{4,0},{5,1},{6,2},{7,3},{8,12},{9,13},{10,... | collective-permute-start | bytes 98312 | tf_op jit(solution)/shard_map/ppermute | solution.py:381
